TPU v7x, 32 devices: a whole 2x2x4 slice. The times are simulated.
32 devices in a mesh: wide: 8 (over z, x), grp: 4 (over y, core).
Axes of the slice: x: 2, y: 2, z: 4, core: 2. Of those that a mesh axis runs over, the one named last changes fastest.
Arguments:
- images: bfloat16 [64, 196, 768], P(('wide', 'grp')), may hold values from -6 to 6
- slot_mask: int32 [64], P(('wide', 'grp')), may hold values from 0 to 1
- labels: int32 [64], P(('wide', 'grp')), may hold values from 0 to 999
- patch_weight: float32 [768, 768], P(('wide', 'grp')), may hold values from -0.21875 to 0.21875
- patch_moment: float32 [768, 768], P(('wide', 'grp')), may hold values from -1.335144e-05 to 1.335144e-05
- patch_square: float32 [768, 768], P(('wide', 'grp')), may hold values from 2.1972157e-11 to 8.788863e-11
- triple_weight: float32 [3, 768, 2304], P(None, ('wide', 'grp')), may hold values from -0.21875 to 0.21875
- triple_moment: float32 [3, 768, 2304], P(None, ('wide', 'grp')), may hold values from -1.335144e-05 to 1.335144e-05
- triple_square: float32 [3, 768, 2304], P(None, ('wide', 'grp')), may hold values from 2.1972157e-11 to 8.788863e-11
- output_weight: float32 [3, 768, 768], P(None, ('wide', 'grp')), may hold values from -1.75 to 1.75
- output_moment: float32 [3, 768, 768], P(None, ('wide', 'grp')), may hold values from -1.335144e-05 to 1.335144e-05
- output_square: float32 [3, 768, 768], P(None, ('wide', 'grp')), may hold values from 2.1972157e-11 to 8.788863e-11
- expand_weight: float32 [3, 768, 3072], P(None, ('wide', 'grp')), may hold values from -0.21875 to 0.21875
- expand_moment: float32 [3, 768, 3072], P(None, ('wide', 'grp')), may hold values from -1.335144e-05 to 1.335144e-05
- expand_square: float32 [3, 768, 3072], P(None, ('wide', 'grp')), may hold values from 2.1972157e-11 to 8.788863e-11
- shrink_weight: float32 [3, 3072, 768], P(None, ('wide', 'grp')), may hold values from -0.109375 to 0.109375
- shrink_moment: float32 [3, 3072, 768], P(None, ('wide', 'grp')), may hold values from -1.335144e-05 to 1.335144e-05
- shrink_square: float32 [3, 3072, 768], P(None, ('wide', 'grp')), may hold values from 2.1972157e-11 to 8.788863e-11
- vector_weight: float32 [213, 768], replicated, may hold values from -0.9 to 2.5
- vector_moment: float32 [213, 768], replicated, may hold values from -6.1035156e-05 to 6.1035156e-05
- vector_square: float32 [213, 768], replicated, may hold values from 5.4930394e-10 to 2.1972157e-09
- head_weight: float32 [769, 1000], replicated, may hold values from -0.21875 to 0.21875
- head_moment: float32 [769, 1000], replicated, may hold values from -6.1035156e-05 to 6.1035156e-05
- head_square: float32 [769, 1000], replicated, may hold values from 5.4930394e-10 to 2.1972157e-09
Outputs:
- loss_sum: float32 [], replicated
- image_total: float32 [], replicated
- grad_norm: float32 [], replicated
- patch_master: float32 [768, 768], P(('wide', 'grp'))
- patch_first: float32 [768, 768], P(('wide', 'grp'))
- patch_second: float32 [768, 768], P(('wide', 'grp'))
- triple_master: float32 [3, 768, 2304], P(None, ('wide', 'grp'))
- triple_first: float32 [3, 768, 2304], P(None, ('wide', 'grp'))
- triple_second: float32 [3, 768, 2304], P(None, ('wide', 'grp'))
- output_master: float32 [3, 768, 768], P(None, ('wide', 'grp'))
- output_first: float32 [3, 768, 768], P(None, ('wide', 'grp'))
- output_second: float32 [3, 768, 768], P(None, ('wide', 'grp'))
- expand_master: float32 [3, 768, 3072], P(None, ('wide', 'grp'))
- expand_first: float32 [3, 768, 3072], P(None, ('wide', 'grp'))
- expand_second: float32 [3, 768, 3072], P(None, ('wide', 'grp'))
- shrink_master: float32 [3, 3072, 768], P(None, ('wide', 'grp'))
- shrink_first: float32 [3, 3072, 768], P(None, ('wide', 'grp'))
- shrink_second: float32 [3, 3072, 768], P(None, ('wide', 'grp'))
- vector_master: float32 [213, 768], replicated
- vector_first: float32 [213, 768], replicated
- vector_second: float32 [213, 768], replicated
- head_master: float32 [769, 1000], replicated
- head_first: float32 [769, 1000], replicated
- head_second: float32 [769, 1000], replicated
- head_bias_grad: float32 [1000], replicated
All inputs are finite; a program needn't handle non-finite values.
Results may differ from a plain program's by a relative error of at most 0.023.
Values may be sent and summed in bfloat16 or wider, within the bound.
A program may use at most 448 MiB of HBM per device.

v0:
```python
import jax
import jax.numpy as jnp
from jax import lax
from jax.sharding import PartitionSpec as P

D = 768
HEADS = 12
HEAD_DIM = 64
CLASSES = 1000
LAYERS = 3
MICRO = 2
STEP_INDEX = 10
S = 197


EPS_NORM = 1e-06
CLIP = 0.1
BETA_ONE = 0.9
BETA_TWO = 0.95
ADAM_EPS = 1e-08
DECAY = 0.05
RATE_MATRIX = 0.03
RATE_OUTPUT = 0.2
RATE_VECTOR = 0.3
SMOOTH = 0.1


def normalize(values, gain_row, shift_row):
    center = values - jnp.mean(values, -1, keepdims=True)
    spread = jnp.mean(center * center, -1, keepdims=True)
    return center * lax.rsqrt(spread + EPS_NORM) * gain_row + shift_row


def gelu_exact(values):
    return jax.nn.gelu(values, approximate=False)


def adam_update(master, moment, square, gradient, step_rate):
    moment_new = BETA_ONE * moment + (1.0 - BETA_ONE) * gradient
    square_new = BETA_TWO * square + (1.0 - BETA_TWO) * gradient * gradient
    moment_hat = moment_new / (1.0 - BETA_ONE**STEP_INDEX)
    square_hat = square_new / (1.0 - BETA_TWO**STEP_INDEX)
    master_new = master - step_rate * (
        moment_hat / (jnp.sqrt(square_hat) + ADAM_EPS) + DECAY * master
    )
    return (master_new, moment_new, square_new)


def layer_forward(hidden, weights, vectors):
    w_triple, w_output, w_expand, w_shrink = weights
    count_img, length, width_all = hidden.shape
    normed = normalize(hidden, vectors[0], vectors[1]).astype(jnp.bfloat16)
    triple = jnp.einsum("bsd,de->bse", normed, w_triple, preferred_element_type=jnp.float32).astype(
        jnp.bfloat16
    )
    split_heads = triple.reshape(count_img, length, 3, HEADS, HEAD_DIM)
    scores = jnp.einsum(
        "bqhd,bkhd->bhqk",
        split_heads[:, :, 0],
        split_heads[:, :, 1],
        preferred_element_type=jnp.float32,
    ) * HEAD_DIM ** (-0.5)
    log_total = jax.nn.logsumexp(scores, axis=-1, keepdims=True)
    probs_low = jnp.exp(scores - log_total).astype(jnp.bfloat16)
    attended = jnp.einsum(
        "bhqk,bkhd->bqhd", probs_low, split_heads[:, :, 2], preferred_element_type=jnp.float32
    )
    attended = attended.reshape(count_img, length, width_all).astype(jnp.bfloat16)
    after_attn = hidden + jnp.einsum(
        "bsd,de->bse", attended, w_output, preferred_element_type=jnp.float32
    )
    normed_two = normalize(after_attn, vectors[2], vectors[3]).astype(jnp.bfloat16)
    expanded = jnp.einsum("bsd,df->bsf", normed_two, w_expand, preferred_element_type=jnp.float32)
    active = gelu_exact(expanded).astype(jnp.bfloat16)
    result = after_attn + jnp.einsum(
        "bsf,fd->bsd", active, w_shrink, preferred_element_type=jnp.float32
    )
    return (
        result,
        (
            hidden,
            normed,
            split_heads,
            log_total,
            attended,
            after_attn,
            normed_two,
            expanded,
            active,
        ),
    )


def layer_backward(upstream, weights, vectors, stored):
    w_triple, w_output, w_expand, w_shrink = weights
    hidden, normed, split_heads, log_total, attended, after_attn, normed_two, expanded, active = (
        stored
    )
    count_img, length, width_all = hidden.shape
    attn_scale = HEAD_DIM ** (-0.5)
    grad_low = upstream.astype(jnp.bfloat16)
    g_shrink = jnp.einsum("bsf,bsd->fd", active, grad_low, preferred_element_type=jnp.float32)
    d_active = jnp.einsum("bsd,fd->bsf", grad_low, w_shrink, preferred_element_type=jnp.float32)
    d_expanded = jax.vjp(gelu_exact, expanded)[1](d_active)[0].astype(jnp.bfloat16)
    g_expand = jnp.einsum("bsd,bsf->df", normed_two, d_expanded, preferred_element_type=jnp.float32)
    d_normed_two = jnp.einsum(
        "bsf,df->bsd", d_expanded, w_expand, preferred_element_type=jnp.float32
    )
    d_after, g_gain_two, g_shift_two = jax.vjp(normalize, after_attn, vectors[2], vectors[3])[1](
        d_normed_two
    )
    upstream_two = upstream + d_after
    grad_two = upstream_two.astype(jnp.bfloat16)
    g_output = jnp.einsum("bsd,bse->de", attended, grad_two, preferred_element_type=jnp.float32)
    d_attended = jnp.einsum(
        "bse,de->bsd", grad_two, w_output, preferred_element_type=jnp.float32
    ).astype(jnp.bfloat16)
    d_attended = d_attended.reshape(count_img, length, HEADS, HEAD_DIM)
    queries = split_heads[:, :, 0]
    keys_all = split_heads[:, :, 1]
    values_all = split_heads[:, :, 2]
    scores = (
        jnp.einsum("bqhd,bkhd->bhqk", queries, keys_all, preferred_element_type=jnp.float32)
        * attn_scale
    )
    probs_full = jnp.exp(scores - log_total)
    d_values = jnp.einsum(
        "bhqk,bqhd->bkhd",
        probs_full.astype(jnp.bfloat16),
        d_attended,
        preferred_element_type=jnp.float32,
    )
    d_probs = jnp.einsum(
        "bqhd,bkhd->bhqk", d_attended, values_all, preferred_element_type=jnp.float32
    )
    centered = d_probs - jnp.sum(probs_full * d_probs, -1, keepdims=True)
    d_scores = (probs_full * centered).astype(jnp.bfloat16)
    d_queries = (
        jnp.einsum("bhqk,bkhd->bqhd", d_scores, keys_all, preferred_element_type=jnp.float32)
        * attn_scale
    )
    d_keys = (
        jnp.einsum("bhqk,bqhd->bkhd", d_scores, queries, preferred_element_type=jnp.float32)
        * attn_scale
    )
    d_triple = (
        jnp.stack([d_queries, d_keys, d_values], axis=2)
        .reshape(count_img, length, 3 * width_all)
        .astype(jnp.bfloat16)
    )
    g_triple = jnp.einsum("bsd,bse->de", normed, d_triple, preferred_element_type=jnp.float32)
    d_normed = jnp.einsum("bse,de->bsd", d_triple, w_triple, preferred_element_type=jnp.float32)
    d_hidden, g_gain_one, g_shift_one = jax.vjp(normalize, hidden, vectors[0], vectors[1])[1](
        d_normed
    )
    vector_part = jnp.stack([g_gain_one, g_shift_one, g_gain_two, g_shift_two])
    return (upstream_two + d_hidden, (g_triple, g_output, g_expand, g_shrink), vector_part)


def head_step(
    hidden, head_table, bias_row, gain_row, shift_row, weight_img, label_ids, image_total
):
    first_row = hidden[:, 0]
    feature_low = normalize(first_row, gain_row, shift_row).astype(jnp.bfloat16)
    logits = jnp.dot(feature_low, head_table, preferred_element_type=jnp.float32) + bias_row
    log_prob = jax.nn.log_softmax(logits, axis=-1)
    class_ids = lax.broadcasted_iota(jnp.int32, logits.shape, 1)
    target = (1.0 - SMOOTH) * (class_ids == label_ids[:, None]).astype(
        jnp.float32
    ) + SMOOTH / CLASSES
    loss_part = jnp.sum(weight_img * -jnp.sum(target * log_prob, axis=-1))
    d_logits = ((weight_img / image_total)[:, None] * (jnp.exp(log_prob) - target)).astype(
        jnp.bfloat16
    )
    g_table = jnp.dot(feature_low.T, d_logits, preferred_element_type=jnp.float32)
    g_bias = jnp.sum(d_logits.astype(jnp.float32), 0)
    d_feature = jnp.dot(d_logits, head_table.T, preferred_element_type=jnp.float32)
    d_first, g_gain, g_shift = jax.vjp(normalize, first_row, gain_row, shift_row)[1](d_feature)
    d_hidden = jnp.zeros_like(hidden).at[:, 0].set(d_first)
    return (
        loss_part,
        d_hidden,
        jnp.concatenate([g_table, g_bias[None]], 0),
        jnp.stack([g_gain, g_shift]),
    )


def per_device(
    images,
    slot_mask,
    labels,
    patch_weight,
    patch_moment,
    patch_square,
    triple_weight,
    triple_moment,
    triple_square,
    output_weight,
    output_moment,
    output_square,
    expand_weight,
    expand_moment,
    expand_square,
    shrink_weight,
    shrink_moment,
    shrink_square,
    vector_weight,
    vector_moment,
    vector_square,
    head_weight,
    head_moment,
    head_square,
):
    image_total = lax.psum(jnp.sum(slot_mask.astype(jnp.float32)), ("wide", "grp"))
    rows_patch, rows_triple, rows_output, rows_expand, rows_shrink = (
        lax.all_gather(patch_weight.astype(jnp.bfloat16), "grp", axis=0, tiled=True),
        lax.all_gather(triple_weight.astype(jnp.bfloat16), "grp", axis=1, tiled=True),
        lax.all_gather(output_weight.astype(jnp.bfloat16), "grp", axis=1, tiled=True),
        lax.all_gather(expand_weight.astype(jnp.bfloat16), "grp", axis=1, tiled=True),
        lax.all_gather(shrink_weight.astype(jnp.bfloat16), "grp", axis=1, tiled=True),
    )
    patch_copy = lax.all_gather(rows_patch, "wide", axis=0, tiled=True)
    head_table = head_weight[:D].astype(jnp.bfloat16)

    def layer_copy(layer_at):
        return (
            lax.all_gather(rows_triple[layer_at], "wide", axis=0, tiled=True),
            lax.all_gather(rows_output[layer_at], "wide", axis=0, tiled=True),
            lax.all_gather(rows_expand[layer_at], "wide", axis=0, tiled=True),
            lax.all_gather(rows_shrink[layer_at], "wide", axis=0, tiled=True),
        )

    layer_sums = [
        jnp.zeros(rows_triple.shape, jnp.float32),
        jnp.zeros(rows_output.shape, jnp.float32),
        jnp.zeros(rows_expand.shape, jnp.float32),
        jnp.zeros(rows_shrink.shape, jnp.float32),
    ]
    patch_sum = jnp.zeros(patch_copy.shape, jnp.float32)
    vector_sum = jnp.zeros_like(vector_weight)
    head_sum = jnp.zeros_like(head_weight)
    loss_running = jnp.zeros((), jnp.float32)
    per_micro = images.shape[0] // MICRO
    final_at = S + 2 + 4 * LAYERS
    for micro_at in range(MICRO):
        offset = micro_at * per_micro
        pieces = images[offset : offset + per_micro]
        weight_img = slot_mask[offset : offset + per_micro].astype(jnp.float32)
        label_ids = labels[offset : offset + per_micro]
        embedded = (
            jnp.einsum("bnp,pd->bnd", pieces, patch_copy, preferred_element_type=jnp.float32)
            + vector_weight[S + 1]
        )
        opening = jnp.broadcast_to(vector_weight[S], (per_micro, 1, D))
        hidden = jnp.concatenate([opening, embedded], axis=1) + vector_weight[:S]
        stored = []
        for layer_at in range(LAYERS):
            base_at = S + 2 + 4 * layer_at
            hidden, layer_saved = layer_forward(
                hidden, layer_copy(layer_at), vector_weight[base_at : base_at + 4]
            )
            stored.append(layer_saved)
        loss_part, upstream, head_part, final_part = head_step(
            hidden,
            head_table,
            head_weight[D],
            vector_weight[final_at],
            vector_weight[final_at + 1],
            weight_img,
            label_ids,
            image_total,
        )
        vector_rows = [final_part]
        for layer_at in reversed(range(LAYERS)):
            base_at = S + 2 + 4 * layer_at
            upstream, matrices, vector_part = layer_backward(
                upstream,
                layer_copy(layer_at),
                vector_weight[base_at : base_at + 4],
                stored[layer_at],
            )
            reduced = (
                lax.psum_scatter(
                    matrices[0].astype(jnp.bfloat16), "wide", scatter_dimension=0, tiled=True
                ).astype(jnp.float32),
                lax.psum_scatter(
                    matrices[1].astype(jnp.bfloat16), "wide", scatter_dimension=0, tiled=True
                ).astype(jnp.float32),
                lax.psum_scatter(
                    matrices[2].astype(jnp.bfloat16), "wide", scatter_dimension=0, tiled=True
                ).astype(jnp.float32),
                lax.psum_scatter(
                    matrices[3].astype(jnp.bfloat16), "wide", scatter_dimension=0, tiled=True
                ).astype(jnp.float32),
            )
            layer_sums = [
                layer_sums[member].at[layer_at].add(reduced[member]) for member in range(4)
            ]
            vector_rows.insert(0, vector_part)
        patch_sum = patch_sum + jnp.einsum(
            "bnp,bnd->pd",
            pieces,
            upstream[:, 1:].astype(jnp.bfloat16),
            preferred_element_type=jnp.float32,
        )
        lead_rows = jnp.concatenate(
            [
                jnp.sum(upstream, 0),
                jnp.sum(upstream[:, 0], 0)[None],
                jnp.sum(upstream[:, 1:], (0, 1))[None],
            ],
            0,
        )
        vector_sum = vector_sum + jnp.concatenate([lead_rows] + vector_rows, 0)
        head_sum = head_sum + head_part
        loss_running = loss_running + loss_part
    owned_triple, owned_output, owned_expand, owned_shrink = (
        lax.psum_scatter(
            layer_sums[0].astype(jnp.bfloat16), "grp", scatter_dimension=1, tiled=True
        ).astype(jnp.float32),
        lax.psum_scatter(
            layer_sums[1].astype(jnp.bfloat16), "grp", scatter_dimension=1, tiled=True
        ).astype(jnp.float32),
        lax.psum_scatter(
            layer_sums[2].astype(jnp.bfloat16), "grp", scatter_dimension=1, tiled=True
        ).astype(jnp.float32),
        lax.psum_scatter(
            layer_sums[3].astype(jnp.bfloat16), "grp", scatter_dimension=1, tiled=True
        ).astype(jnp.float32),
    )
    owned_patch = lax.psum_scatter(patch_sum, ("wide", "grp"), scatter_dimension=0, tiled=True)
    owned = (owned_patch, owned_triple, owned_output, owned_expand, owned_shrink)
    local_square = jnp.sum(jnp.stack([jnp.sum(member * member) for member in owned]))
    head_grad, vector_grad, loss_total = lax.psum(
        (head_sum, vector_sum, loss_running), ("wide", "grp")
    )
    shard_square = lax.psum(local_square, ("wide", "grp"))
    grad_norm = jnp.sqrt(
        shard_square + jnp.sum(head_grad * head_grad) + jnp.sum(vector_grad * vector_grad)
    )
    clip_scale = CLIP / jnp.maximum(grad_norm, CLIP)
    patch_new = adam_update(
        patch_weight, patch_moment, patch_square, owned_patch * clip_scale, RATE_MATRIX
    )
    triple_new = adam_update(
        triple_weight, triple_moment, triple_square, owned_triple * clip_scale, RATE_MATRIX
    )
    output_new = adam_update(
        output_weight, output_moment, output_square, owned_output * clip_scale, RATE_OUTPUT
    )
    expand_new = adam_update(
        expand_weight, expand_moment, expand_square, owned_expand * clip_scale, RATE_MATRIX
    )
    shrink_new = adam_update(
        shrink_weight, shrink_moment, shrink_square, owned_shrink * clip_scale, RATE_MATRIX
    )
    vector_new = adam_update(
        vector_weight, vector_moment, vector_square, vector_grad * clip_scale, RATE_VECTOR
    )
    head_clipped = head_grad * clip_scale
    head_new = adam_update(head_weight, head_moment, head_square, head_clipped, RATE_MATRIX)
    return (
        loss_total,
        image_total,
        grad_norm,
        patch_new[0],
        patch_new[1],
        patch_new[2],
        triple_new[0],
        triple_new[1],
        triple_new[2],
        output_new[0],
        output_new[1],
        output_new[2],
        expand_new[0],
        expand_new[1],
        expand_new[2],
        shrink_new[0],
        shrink_new[1],
        shrink_new[2],
        vector_new[0],
        vector_new[1],
        vector_new[2],
        head_new[0],
        head_new[1],
        head_new[2],
        head_clipped[D],
    )


def solution(mesh):
    in_specs = (
        P(("wide", "grp"), None, None),
        P(("wide", "grp")),
        P(("wide", "grp")),
        P(("wide", "grp"), None),
        P(("wide", "grp"), None),
        P(("wide", "grp"), None),
        P(None, ("wide", "grp"), None),
        P(None, ("wide", "grp"), None),
        P(None, ("wide", "grp"), None),
        P(None, ("wide", "grp"), None),
        P(None, ("wide", "grp"), None),
        P(None, ("wide", "grp"), None),
        P(None, ("wide", "grp"), None),
        P(None, ("wide", "grp"), None),
        P(None, ("wide", "grp"), None),
        P(None, ("wide", "grp"), None),
        P(None, ("wide", "grp"), None),
        P(None, ("wide", "grp"), None),
        P(),
        P(),
        P(),
        P(),
        P(),
        P(),
    )
    out_specs = (
        P(),
        P(),
        P(),
        P(("wide", "grp"), None),
        P(("wide", "grp"), None),
        P(("wide", "grp"), None),
        P(None, ("wide", "grp"), None),
        P(None, ("wide", "grp"), None),
        P(None, ("wide", "grp"), None),
        P(None, ("wide", "grp"), None),
        P(None, ("wide", "grp"), None),
        P(None, ("wide", "grp"), None),
        P(None, ("wide", "grp"), None),
        P(None, ("wide", "grp"), None),
        P(None, ("wide", "grp"), None),
        P(None, ("wide", "grp"), None),
        P(None, ("wide", "grp"), None),
        P(None, ("wide", "grp"), None),
        P(),
        P(),
        P(),
        P(),
        P(),
        P(),
        P(),
    )
    return jax.shard_map(
        per_device, mesh=mesh, in_specs=in_specs, out_specs=out_specs, check_vma=False
    )
```

profile of v0, /device:TPU:0, one launch (start us, length us, event | category | flops | bytes accessed | tf_op | source)
XLA Modules:
  0.0 3616.9 jit_solution(18170455859554928043)
XLA Ops:
  19.4 11.8 all-gather.31.cloned.1.call-done
  41.3 12.9 all-gather.33.cloned.1.call-done
  56.9 20.2 all-gather.35.cloned.1.call-done
  85.0 39.7 %psum.36 = f32[]{:T(128)} all-reduce(f32[]{:T(128)} %convert_reduce_fusion.4), channel_id=1, replica_groups=mesh['wide'=8,'grp'=4] {'wide','grp'}, use_global_device_ids=true, to_apply=%region_48.49 | all-reduce | flops 1 | bytes 8 | tf_op jit(solution)/shard_map/psum | solution.py:214
  137.2 49.7 %all-gather.37.cloned.1.call-done = bf16[1,768,2304]{2,1,0:T(8,128)(2,1)} async-done(((bf16[1,96,2304]{2,1,0:T(8,128)(2,1)}), bf16[1,768,2304]{2,1,0:T(8,128)(2,1)}) %all-gather.37.cloned.1.call-update) | async-done | bytes 3538960 | tf_op jit(solution)/shard_map/all_gather | solution.py:227
  200.6 28.4 all-gather.39.cloned.1.call-done
  235.0 75.5 %all-gather.41.cloned.1.call-done = bf16[1,768,3072]{2,1,0:T(8,128)(2,1)} async-done(((bf16[1,96,3072]{2,1,0:T(8,128)(2,1)}), bf16[1,768,3072]{2,1,0:T(8,128)(2,1)}) %all-gather.41.cloned.1.call-update) | async-done | bytes 4718608 | tf_op jit(solution)/shard_map/all_gather | solution.py:229
  319.7 71.6 %all-gather.43.cloned.1.call-done = bf16[1,3072,768]{2,1,0:T(8,128)(2,1)} async-done(((bf16[1,384,768]{2,1,0:T(8,128)(2,1)}), bf16[1,3072,768]{2,1,0:T(8,128)(2,1)}) %all-gather.43.cloned.1.call-update) | async-done | bytes 4718608 | tf_op jit(solution)/shard_map/all_gather | solution.py:230
  395.2 62.2 %all-gather.45.cloned.1.call-done = bf16[1,768,2304]{2,1,0:T(8,128)(2,1)} async-done(((bf16[1,96,2304]{2,1,0:T(8,128)(2,1)}), bf16[1,768,2304]{2,1,0:T(8,128)(2,1)}) %all-gather.45.cloned.1.call-update) | async-done | bytes 3538960 | tf_op jit(solution)/shard_map/all_gather | solution.py:227
  465.7 33.9 all-gather.47.cloned.1.call-done
  501.7 79.3 %all-gather.49.cloned.1.call-done = bf16[1,768,3072]{2,1,0:T(8,128)(2,1)} async-done(((bf16[1,96,3072]{2,1,0:T(8,128)(2,1)}), bf16[1,768,3072]{2,1,0:T(8,128)(2,1)}) %all-gather.49.cloned.1.call-update) | async-done | bytes 4718608 | tf_op jit(solution)/shard_map/all_gather | solution.py:229
  590.2 71.5 %all-gather.51.cloned.1.call-done = bf16[1,3072,768]{2,1,0:T(8,128)(2,1)} async-done(((bf16[1,384,768]{2,1,0:T(8,128)(2,1)}), bf16[1,3072,768]{2,1,0:T(8,128)(2,1)}) %all-gather.51.cloned.1.call-update) | async-done | bytes 4718608 | tf_op jit(solution)/shard_map/all_gather | solution.py:230
  665.6 62.2 %all-gather.53.cloned.1.call-done = bf16[1,768,2304]{2,1,0:T(8,128)(2,1)} async-done(((bf16[1,96,2304]{2,1,0:T(8,128)(2,1)}), bf16[1,768,2304]{2,1,0:T(8,128)(2,1)}) %all-gather.53.cloned.1.call-update) | async-done | bytes 3538960 | tf_op jit(solution)/shard_map/all_gather | solution.py:227
  735.9 34.1 all-gather.55.cloned.1.call-done
  772.1 79.2 %all-gather.57.cloned.1.call-done = bf16[1,768,3072]{2,1,0:T(8,128)(2,1)} async-done(((bf16[1,96,3072]{2,1,0:T(8,128)(2,1)}), bf16[1,768,3072]{2,1,0:T(8,128)(2,1)}) %all-gather.57.cloned.1.call-update) | async-done | bytes 4718608 | tf_op jit(solution)/shard_map/all_gather | solution.py:229
  851.3 9.4 multiply_convert_fusion.9
  860.7 71.2 %all-gather.59.cloned.1.call-done = bf16[1,3072,768]{2,1,0:T(8,128)(2,1)} async-done(((bf16[1,384,768]{2,1,0:T(8,128)(2,1)}), bf16[1,3072,768]{2,1,0:T(8,128)(2,1)}) %all-gather.59.cloned.1.call-update) | async-done | bytes 4718608 | tf_op jit(solution)/shard_map/all_gather | solution.py:230
  939.8 9.3 multiply_convert_fusion.8
  958.8 10.1 multiply_convert_fusion.7
  981.3 10.1 multiply_convert_fusion.6
  1303.2 64.4 %reduce-scatter.56.cloned.1.call-done = bf16[96,768]{1,0:T(8,128)(2,1)} async-done(((bf16[768,768]{1,0:T(8,128)(2,1)}), bf16[96,768]{1,0:T(8,128)(2,1)}) %reduce-scatter.56.cloned.1.call-update) | async-done | bytes 147472 | tf_op jit(solution)/shard_map/reduce_scatter | solution.py:286
  1368.6 65.5 %reduce-scatter.58.cloned.1.call-done = bf16[96,768]{1,0:T(8,128)(2,1)} async-done(((bf16[768,768]{1,0:T(8,128)(2,1)}), bf16[96,768]{1,0:T(8,128)(2,1)}) %reduce-scatter.58.cloned.1.call-update) | async-done | bytes 147472 | tf_op jit(solution)/shard_map/reduce_scatter | solution.py:286
  1435.1 65.5 %reduce-scatter.60.cloned.1.call-done = bf16[96,768]{1,0:T(8,128)(2,1)} async-done(((bf16[768,768]{1,0:T(8,128)(2,1)}), bf16[96,768]{1,0:T(8,128)(2,1)}) %reduce-scatter.60.cloned.1.call-update) | async-done | bytes 147472 | tf_op jit(solution)/shard_map/reduce_scatter | solution.py:286
  1502.9 79.4 %reduce-scatter.38.cloned.1.call-done = bf16[96,2304]{1,0:T(8,128)(2,1)} async-done(((bf16[768,2304]{1,0:T(8,128)(2,1)}), bf16[96,2304]{1,0:T(8,128)(2,1)}) %reduce-scatter.38.cloned.1.call-update) | async-done | bytes 442384 | tf_op jit(solution)/shard_map/reduce_scatter | solution.py:283
  1583.5 81.0 %reduce-scatter.40.cloned.1.call-done = bf16[96,2304]{1,0:T(8,128)(2,1)} async-done(((bf16[768,2304]{1,0:T(8,128)(2,1)}), bf16[96,2304]{1,0:T(8,128)(2,1)}) %reduce-scatter.40.cloned.1.call-update) | async-done | bytes 442384 | tf_op jit(solution)/shard_map/reduce_scatter | solution.py:283
  1665.5 81.3 %reduce-scatter.42.cloned.1.call-done = bf16[96,2304]{1,0:T(8,128)(2,1)} async-done(((bf16[768,2304]{1,0:T(8,128)(2,1)}), bf16[96,2304]{1,0:T(8,128)(2,1)}) %reduce-scatter.42.cloned.1.call-update) | async-done | bytes 442384 | tf_op jit(solution)/shard_map/reduce_scatter | solution.py:283
  1748.0 81.1 %reduce-scatter.44.cloned.1.call-done = bf16[96,2304]{1,0:T(8,128)(2,1)} async-done(((bf16[768,2304]{1,0:T(8,128)(2,1)}), bf16[96,2304]{1,0:T(8,128)(2,1)}) %reduce-scatter.44.cloned.1.call-update) | async-done | bytes 442384 | tf_op jit(solution)/shard_map/reduce_scatter | solution.py:283
  1830.2 81.1 %reduce-scatter.46.cloned.1.call-done = bf16[96,2304]{1,0:T(8,128)(2,1)} async-done(((bf16[768,2304]{1,0:T(8,128)(2,1)}), bf16[96,2304]{1,0:T(8,128)(2,1)}) %reduce-scatter.46.cloned.1.call-update) | async-done | bytes 442384 | tf_op jit(solution)/shard_map/reduce_scatter | solution.py:283
  1912.4 81.2 %reduce-scatter.48.cloned.1.call-done = bf16[96,2304]{1,0:T(8,128)(2,1)} async-done(((bf16[768,2304]{1,0:T(8,128)(2,1)}), bf16[96,2304]{1,0:T(8,128)(2,1)}) %reduce-scatter.48.cloned.1.call-update) | async-done | bytes 442384 | tf_op jit(solution)/shard_map/reduce_scatter | solution.py:283
  1997.3 94.8 %reduce-scatter.62.cloned.1.call-done = bf16[96,3072]{1,0:T(8,128)(2,1)} async-done(((bf16[768,3072]{1,0:T(8,128)(2,1)}), bf16[96,3072]{1,0:T(8,128)(2,1)}) %reduce-scatter.62.cloned.1.call-update) | async-done | bytes 589840 | tf_op jit(solution)/shard_map/reduce_scatter | solution.py:289
  2093.6 97.1 %reduce-scatter.64.cloned.1.call-done = bf16[96,3072]{1,0:T(8,128)(2,1)} async-done(((bf16[768,3072]{1,0:T(8,128)(2,1)}), bf16[96,3072]{1,0:T(8,128)(2,1)}) %reduce-scatter.64.cloned.1.call-update) | async-done | bytes 589840 | tf_op jit(solution)/shard_map/reduce_scatter | solution.py:289
  2191.9 97.5 %reduce-scatter.66.cloned.1.call-done = bf16[96,3072]{1,0:T(8,128)(2,1)} async-done(((bf16[768,3072]{1,0:T(8,128)(2,1)}), bf16[96,3072]{1,0:T(8,128)(2,1)}) %reduce-scatter.66.cloned.1.call-update) | async-done | bytes 589840 | tf_op jit(solution)/shard_map/reduce_scatter | solution.py:289
  2290.8 97.3 %reduce-scatter.68.cloned.1.call-done = bf16[96,3072]{1,0:T(8,128)(2,1)} async-done(((bf16[768,3072]{1,0:T(8,128)(2,1)}), bf16[96,3072]{1,0:T(8,128)(2,1)}) %reduce-scatter.68.cloned.1.call-update) | async-done | bytes 589840 | tf_op jit(solution)/shard_map/reduce_scatter | solution.py:289
  2389.4 97.2 %reduce-scatter.70.cloned.1.call-done = bf16[96,3072]{1,0:T(8,128)(2,1)} async-done(((bf16[768,3072]{1,0:T(8,128)(2,1)}), bf16[96,3072]{1,0:T(8,128)(2,1)}) %reduce-scatter.70.cloned.1.call-update) | async-done | bytes 589840 | tf_op jit(solution)/shard_map/reduce_scatter | solution.py:289
  2487.9 97.3 %reduce-scatter.72.cloned.1.call-done = bf16[96,3072]{1,0:T(8,128)(2,1)} async-done(((bf16[768,3072]{1,0:T(8,128)(2,1)}), bf16[96,3072]{1,0:T(8,128)(2,1)}) %reduce-scatter.72.cloned.1.call-update) | async-done | bytes 589840 | tf_op jit(solution)/shard_map/reduce_scatter | solution.py:289
  2590.6 93.3 %reduce-scatter.74.cloned.1.call-done = bf16[384,768]{1,0:T(8,128)(2,1)} async-done(((bf16[3072,768]{1,0:T(8,128)(2,1)}), bf16[384,768]{1,0:T(8,128)(2,1)}) %reduce-scatter.74.cloned.1.call-update) | async-done | bytes 589840 | tf_op jit(solution)/shard_map/reduce_scatter | solution.py:292
  2685.3 97.2 %reduce-scatter.76.cloned.1.call-done = bf16[384,768]{1,0:T(8,128)(2,1)} async-done(((bf16[3072,768]{1,0:T(8,128)(2,1)}), bf16[384,768]{1,0:T(8,128)(2,1)}) %reduce-scatter.76.cloned.1.call-update) | async-done | bytes 589840 | tf_op jit(solution)/shard_map/reduce_scatter | solution.py:292
  2783.6 97.4 %reduce-scatter.78.cloned.1.call-done = bf16[384,768]{1,0:T(8,128)(2,1)} async-done(((bf16[3072,768]{1,0:T(8,128)(2,1)}), bf16[384,768]{1,0:T(8,128)(2,1)}) %reduce-scatter.78.cloned.1.call-update) | async-done | bytes 589840 | tf_op jit(solution)/shard_map/reduce_scatter | solution.py:292
  2882.3 97.4 %reduce-scatter.80.cloned.1.call-done = bf16[384,768]{1,0:T(8,128)(2,1)} async-done(((bf16[3072,768]{1,0:T(8,128)(2,1)}), bf16[384,768]{1,0:T(8,128)(2,1)}) %reduce-scatter.80.cloned.1.call-update) | async-done | bytes 589840 | tf_op jit(solution)/shard_map/reduce_scatter | solution.py:292
  2981.0 97.2 %reduce-scatter.82.cloned.1.call-done = bf16[384,768]{1,0:T(8,128)(2,1)} async-done(((bf16[3072,768]{1,0:T(8,128)(2,1)}), bf16[384,768]{1,0:T(8,128)(2,1)}) %reduce-scatter.82.cloned.1.call-update) | async-done | bytes 589840 | tf_op jit(solution)/shard_map/reduce_scatter | solution.py:292
  3079.5 97.4 %reduce-scatter.84.cloned.1.call-done = bf16[384,768]{1,0:T(8,128)(2,1)} async-done(((bf16[3072,768]{1,0:T(8,128)(2,1)}), bf16[384,768]{1,0:T(8,128)(2,1)}) %reduce-scatter.84.cloned.1.call-update) | async-done | bytes 589840 | tf_op jit(solution)/shard_map/reduce_scatter | solution.py:292
  3184.8 138.5 %all-reduce.10.cloned.1.call-done = (f32[769,1000]{1,0:T(8,128)}, f32[213,768]{1,0:T(8,128)}) async-done(((f32[769,1000]{1,0:T(8,128)}, f32[213,768]{1,0:T(8,128)}), (f32[769,1000]{1,0:T(8,128)}, f32[213,768]{1,0:T(8,128)})) %all-reduce.10.cloned.1.call-update) | async-done | bytes 3730352 | tf_op jit(solution)/shard_map/psum | solution.py:334
  3328.5 100.0 %reduce-scatter.88.cloned.1.call-done = f32[24,768]{1,0:T(8,128)} async-done(((f32[768,768]{1,0:T(8,128)}), f32[24,768]{1,0:T(8,128)}) %reduce-scatter.88.cloned.1.call-update) | async-done | bytes 73744 | tf_op jit(solution)/shard_map/reduce_scatter | solution.py:331
  3432.0 19.6 reduce-scatter.92.cloned.1.call-done
  3453.2 27.6 reduce-scatter.90.cloned.1.call-done
  3486.5 27.0 reduce-scatter.94.cloned.1.call-done
  3518.4 26.9 reduce-scatter.86.cloned.1.call-done
  3547.8 40.1 %all-reduce.6 = (f32[]{:T(128)}, f32[]{:T(128)}) all-reduce(f32[]{:T(128)} %bitcast.70, f32[]{:T(128)S(6)} %reduce_sum.1101), channel_id=1, replica_groups=mesh['wide'=8,'grp'=4] {'wide','grp'}, use_global_device_ids=true, to_apply=%region_46.47 | all-reduce | flops 2 | bytes 16 | tf_op jit(solution)/shard_map/psum | solution.py:334
  (1174 shorter events, 516.6 us)
Async XLA Ops:
  7.2 24.0 all-gather.31.cloned.1.call-start
  9.2 44.9 %all-gather.33.cloned.1.call-start = ((), (), s32[]{:S(2)}) async-start(), calls=%async_computation.31 | async-start | bytes 2211840 | tf_op jit(solution)/shard_map/all_gather | solution.py:219
  11.3 65.8 %all-gather.35.cloned.1.call-start = ((), (), s32[]{:S(2)}) async-start(), calls=%async_computation.32 | async-start | bytes 2211840 | tf_op jit(solution)/shard_map/all_gather | solution.py:220
  12.2 118.0 %all-gather.29.cloned.1.call-start = ((), (), s32[]{:S(2)}) async-start(), calls=%async_computation.29 | async-start | bytes 1327104 | tf_op jit(solution)/shard_map/all_gather | solution.py:222
  19.3 167.5 %all-gather.37.cloned.1.call-start = ((), (), s32[]{:S(2)}) async-start(), calls=%async_computation.58 | async-start | bytes 3981312 | tf_op jit(solution)/shard_map/all_gather | solution.py:227
  33.6 195.4 %all-gather.39.cloned.1.call-start = ((), (), s32[]{:S(2)}) async-start(), calls=%async_computation.59 | async-start | bytes 1327104 | tf_op jit(solution)/shard_map/all_gather | solution.py:228
  41.2 269.3 %all-gather.41.cloned.1.call-start = ((), (), s32[]{:S(2)}) async-start(), calls=%async_computation.60 | async-start | bytes 5308416 | tf_op jit(solution)/shard_map/all_gather | solution.py:229
  56.8 334.5 %all-gather.43.cloned.1.call-start = ((), (), s32[]{:S(2)}) async-start(), calls=%async_computation.61 | async-start | bytes 5308416 | tf_op jit(solution)/shard_map/all_gather | solution.py:230
  79.8 377.6 %all-gather.45.cloned.1.call-start = ((), (), s32[]{:S(2)}) async-start(), calls=%async_computation.62 | async-start | bytes 3981312 | tf_op jit(solution)/shard_map/all_gather | solution.py:227
  80.5 419.1 %all-gather.47.cloned.1.call-start = ((), (), s32[]{:S(2)}) async-start(), calls=%async_computation.63 | async-start | bytes 1327104 | tf_op jit(solution)/shard_map/all_gather | solution.py:228
  81.1 499.9 %all-gather.49.cloned.1.call-start = ((), (), s32[]{:S(2)}) async-start(), calls=%async_computation.64 | async-start | bytes 5308416 | tf_op jit(solution)/shard_map/all_gather | solution.py:229
  81.8 579.9 %all-gather.51.cloned.1.call-start = ((), (), s32[]{:S(2)}) async-start(), calls=%async_computation.65 | async-start | bytes 5308416 | tf_op jit(solution)/shard_map/all_gather | solution.py:230
  82.4 645.4 %all-gather.53.cloned.1.call-start = ((), (), s32[]{:S(2)}) async-start(), calls=%async_computation.66 | async-start | bytes 3981312 | tf_op jit(solution)/shard_map/all_gather | solution.py:227
  83.2 686.8 %all-gather.55.cloned.1.call-start = ((), (), s32[]{:S(2)}) async-start(), calls=%async_computation.67 | async-start | bytes 1327104 | tf_op jit(solution)/shard_map/all_gather | solution.py:228
  83.7 767.6 %all-gather.57.cloned.1.call-start = ((), (), s32[]{:S(2)}) async-start(), calls=%async_computation.68 | async-start | bytes 5308416 | tf_op jit(solution)/shard_map/all_gather | solution.py:229
  84.3 847.6 %all-gather.59.cloned.1.call-start = ((), (), s32[]{:S(2)}) async-start(), calls=%async_computation.69 | async-start | bytes 5308416 | tf_op jit(solution)/shard_map/all_gather | solution.py:230
  136.7 1163.6 %reduce-scatter.50.cloned.1.call-start = ((), (), s32[]{:S(2)}) async-start(), calls=%async_computation.39 | async-start | bytes 1327104 | tf_op jit(solution)/shard_map/reduce_scatter | solution.py:286
  230.9 718.2 %copy-start.48 = (f32[197,768]{1,0:T(8,128)}, f32[197,768]{1,0:T(8,128)S(1)}, u32[]{:S(2)}) copy-start(f32[197,768]{1,0:T(8,128)S(1)} %get-tuple-element.601) | copy-start | bytes 1815556
  230.9 708.9 %copy-start.243 = (f32[197]{0:T(256)}, f32[197]{0:T(256)S(1)}, u32[]{:S(2)}) copy-start(f32[197]{0:T(256)S(1)} %broadcast_multiply_fusion.7) | copy-start | bytes 2368
  1106.1 195.2 %reduce-scatter.52.cloned.1.call-start = ((), (), s32[]{:S(2)}) async-start(), calls=%async_computation.40 | async-start | bytes 1327104 | tf_op jit(solution)/shard_map/reduce_scatter | solution.py:286
  1116.3 185.9 %reduce-scatter.54.cloned.1.call-start = ((), (), s32[]{:S(2)}) async-start(), calls=%async_computation.41 | async-start | bytes 1327104 | tf_op jit(solution)/shard_map/reduce_scatter | solution.py:286
  1134.7 233.0 %reduce-scatter.56.cloned.1.call-start = ((), (), s32[]{:S(2)}) async-start(), calls=%async_computation.42 | async-start | bytes 1327104 | tf_op jit(solution)/shard_map/reduce_scatter | solution.py:286
  1136.2 297.9 %reduce-scatter.58.cloned.1.call-start = ((), (), s32[]{:S(2)}) async-start(), calls=%async_computation.43 | async-start | bytes 1327104 | tf_op jit(solution)/shard_map/reduce_scatter | solution.py:286
  1137.8 362.8 %reduce-scatter.60.cloned.1.call-start = ((), (), s32[]{:S(2)}) async-start(), calls=%async_computation.44 | async-start | bytes 1327104 | tf_op jit(solution)/shard_map/reduce_scatter | solution.py:286
  1141.0 441.3 %reduce-scatter.38.cloned.1.call-start = ((), (), s32[]{:S(2)}) async-start(), calls=%async_computation.33 | async-start | bytes 3981312 | tf_op jit(solution)/shard_map/reduce_scatter | solution.py:283
  1144.3 520.1 %reduce-scatter.40.cloned.1.call-start = ((), (), s32[]{:S(2)}) async-start(), calls=%async_computation.34 | async-start | bytes 3981312 | tf_op jit(solution)/shard_map/reduce_scatter | solution.py:283
  1148.9 597.9 %reduce-scatter.42.cloned.1.call-start = ((), (), s32[]{:S(2)}) async-start(), calls=%async_computation.35 | async-start | bytes 3981312 | tf_op jit(solution)/shard_map/reduce_scatter | solution.py:283
  1162.3 666.8 %reduce-scatter.44.cloned.1.call-start = ((), (), s32[]{:S(2)}) async-start(), calls=%async_computation.36 | async-start | bytes 3981312 | tf_op jit(solution)/shard_map/reduce_scatter | solution.py:283
  1166.8 744.5 %reduce-scatter.46.cloned.1.call-start = ((), (), s32[]{:S(2)}) async-start(), calls=%async_computation.37 | async-start | bytes 3981312 | tf_op jit(solution)/shard_map/reduce_scatter | solution.py:283
  1171.3 822.3 %reduce-scatter.48.cloned.1.call-start = ((), (), s32[]{:S(2)}) async-start(), calls=%async_computation.38 | async-start | bytes 3981312 | tf_op jit(solution)/shard_map/reduce_scatter | solution.py:283
  1184.6 907.6 %reduce-scatter.62.cloned.1.call-start = ((), (), s32[]{:S(2)}) async-start(), calls=%async_computation.45 | async-start | bytes 5308416 | tf_op jit(solution)/shard_map/reduce_scatter | solution.py:289
  1189.8 1000.9 %reduce-scatter.64.cloned.1.call-start = ((), (), s32[]{:S(2)}) async-start(), calls=%async_computation.46 | async-start | bytes 5308416 | tf_op jit(solution)/shard_map/reduce_scatter | solution.py:289
  1195.1 1094.3 %reduce-scatter.66.cloned.1.call-start = ((), (), s32[]{:S(2)}) async-start(), calls=%async_computation.47 | async-start | bytes 5308416 | tf_op jit(solution)/shard_map/reduce_scatter | solution.py:289
  1200.4 1187.7 %reduce-scatter.68.cloned.1.call-start = ((), (), s32[]{:S(2)}) async-start(), calls=%async_computation.48 | async-start | bytes 5308416 | tf_op jit(solution)/shard_map/reduce_scatter | solution.py:289
  1205.6 1281.0 %reduce-scatter.70.cloned.1.call-start = ((), (), s32[]{:S(2)}) async-start(), calls=%async_computation.49 | async-start | bytes 5308416 | tf_op jit(solution)/shard_map/reduce_scatter | solution.py:289
  1210.8 1374.5 %reduce-scatter.72.cloned.1.call-start = ((), (), s32[]{:S(2)}) async-start(), calls=%async_computation.50 | async-start | bytes 5308416 | tf_op jit(solution)/shard_map/reduce_scatter | solution.py:289
  1215.8 1468.2 %reduce-scatter.74.cloned.1.call-start = ((), (), s32[]{:S(2)}) async-start(), calls=%async_computation.51 | async-start | bytes 5308416 | tf_op jit(solution)/shard_map/reduce_scatter | solution.py:292
  1220.7 1561.8 %reduce-scatter.76.cloned.1.call-start = ((), (), s32[]{:S(2)}) async-start(), calls=%async_computation.52 | async-start | bytes 5308416 | tf_op jit(solution)/shard_map/reduce_scatter | solution.py:292
  1225.9 1655.1 %reduce-scatter.78.cloned.1.call-start = ((), (), s32[]{:S(2)}) async-start(), calls=%async_computation.53 | async-start | bytes 5308416 | tf_op jit(solution)/shard_map/reduce_scatter | solution.py:292
  1230.9 1748.7 %reduce-scatter.80.cloned.1.call-start = ((), (), s32[]{:S(2)}) async-start(), calls=%async_computation.54 | async-start | bytes 5308416 | tf_op jit(solution)/shard_map/reduce_scatter | solution.py:292
  1235.9 1842.3 %reduce-scatter.82.cloned.1.call-start = ((), (), s32[]{:S(2)}) async-start(), calls=%async_computation.55 | async-start | bytes 5308416 | tf_op jit(solution)/shard_map/reduce_scatter | solution.py:292
  1240.9 1935.9 %reduce-scatter.84.cloned.1.call-start = ((), (), s32[]{:S(2)}) async-start(), calls=%async_computation.56 | async-start | bytes 5308416 | tf_op jit(solution)/shard_map/reduce_scatter | solution.py:292
  1246.0 2077.4 %all-reduce.10.cloned.1.call-start = ((), (), s32[]{:S(2)}) async-start(), calls=%async_computation.74 | async-start | bytes 7684096 | tf_op jit(solution)/shard_map/psum | solution.py:334
  1293.6 2134.8 %reduce-scatter.88.cloned.1.call-start = ((), (), s32[]{:S(2)}) async-start(), calls=%async_computation.70 | async-start | bytes 2433024 | tf_op jit(solution)/shard_map/reduce_scatter | solution.py:331
  1300.2 2151.4 %reduce-scatter.92.cloned.1.call-start = ((), (), s32[]{:S(2)}) async-start(), calls=%async_computation.72 | async-start | bytes 552960
  1502.8 1978.1 %reduce-scatter.90.cloned.1.call-start = ((), (), s32[]{:S(2)}) async-start(), calls=%async_computation.71 | async-start | bytes 1658880
  1997.3 1516.2 %reduce-scatter.94.cloned.1.call-start = ((), (), s32[]{:S(2)}) async-start(), calls=%async_computation.73 | async-start | bytes 2211840
  2590.3 955.0 %reduce-scatter.86.cloned.1.call-start = ((), (), s32[]{:S(2)}) async-start(), calls=%async_computation.57 | async-start | bytes 2211840 | tf_op jit(solution)/shard_map/reduce_scatter | solution.py:327
  (348 other events, 5909.5 us)
Sparse Core Ops, SparseCore 0:
  10.2 20.9 all-gather.30
  33.4 20.7 all-gather.32
  56.3 20.7 all-gather.34
  79.1 41.1 all-gather.28
  123.0 63.8 all-gather.36
  189.5 39.5 all-gather.38
  231.8 78.6 all-gather.40
  313.2 78.0 all-gather.42
  394.1 63.3 all-gather.44
  460.0 39.5 all-gather.46
  502.4 78.6 all-gather.48
  583.7 78.0 all-gather.50
  664.5 63.3 all-gather.52
  730.4 39.5 all-gather.54
  772.6 78.6 all-gather.56
  853.9 78.0 all-gather.58
  1106.2 62.1 reduce-scatter.49
  1171.7 63.0 reduce-scatter.51
  1238.1 63.2 reduce-scatter.53
  1304.6 63.0 reduce-scatter.55
  1371.1 63.0 reduce-scatter.57
  1437.5 63.0 reduce-scatter.59
  1504.2 78.0 reduce-scatter.37
  1585.8 78.6 reduce-scatter.39
  1668.1 78.6 reduce-scatter.41
  1750.3 78.7 reduce-scatter.43
  1832.5 78.7 reduce-scatter.45
  1914.9 78.6 reduce-scatter.47
  1997.3 94.8 reduce-scatter.61
  2095.7 95.0 reduce-scatter.63
  2194.4 95.0 reduce-scatter.65
  2293.1 94.9 reduce-scatter.67
  2391.6 94.9 reduce-scatter.69
  2490.3 94.9 reduce-scatter.71
  2588.9 94.9 reduce-scatter.73
  2687.4 94.9 reduce-scatter.75
  2786.0 94.9 reduce-scatter.77
  2884.6 94.9 reduce-scatter.79
  2983.2 94.9 reduce-scatter.81
  3081.8 94.9 reduce-scatter.83
  3183.1 140.1 all-reduce.9
  3330.0 98.3 reduce-scatter.87
  3431.4 20.1 reduce-scatter.91
  3454.2 26.6 reduce-scatter.89
  3484.1 29.3 reduce-scatter.93
  3515.9 29.3 reduce-scatter.85
where the time goes:
time: 3630 us; the launch traced here: 3620 us
  waiting for transfers between devices  2950 us (81%)
  matrix products  287 us (8%)
  local copies, waits for them, and re-layouts  124 us (3%)
  other arithmetic  122 us (3%)
  blocking collectives  93.5 us (3%)
  between operations  36.6 us (1%)
    reduce_scatter x6, waiting for transfers between devices, per_device(): lax.psum_scatter(matrices[2].astype(jnp.bfloat16), 'wide', scatter_dimens...  581 us
    reduce_scatter x6, waiting for transfers between devices, per_device(): lax.psum_scatter(matrices[3].astype(jnp.bfloat16), 'wide', scatter_dimens...  580 us
    reduce_scatter x6, waiting for transfers between devices, per_device(): lax.psum_scatter(matrices[0].astype(jnp.bfloat16), 'wide', scatter_dimens...  485 us
    all_gather x3, waiting for transfers between devices, layer_copy(): lax.all_gather(rows_expand[layer_at], 'wide', axis=0, tiled=True)  234 us
    all_gather x3, waiting for transfers between devices, layer_copy(): lax.all_gather(rows_shrink[layer_at], 'wide', axis=0, tiled=True)  214 us
    reduce_scatter x6, waiting for transfers between devices, per_device(): lax.psum_scatter(matrices[1].astype(jnp.bfloat16), 'wide', scatter_dimens...  195 us
    all_gather x3, waiting for transfers between devices, layer_copy(): lax.all_gather(rows_triple[layer_at], 'wide', axis=0, tiled=True)  174 us
    psum x1, waiting for transfers between devices, per_device(): lax.psum((head_sum, vector_sum, loss_running), ('wide', 'grp'))  138 us
  transfers between devices with their start and end apart: 46, of which 42 were waited for; matrix products, arithmetic and copies ran while one was open for 9% of the time, Pallas kernels for 0%

commit v1 on v0

v1 whole, which is shorter than its diff:
```python
import functools
from types import SimpleNamespace

import jax
import jax.numpy as jnp
from jax import lax
from jax.experimental import pallas as pl
from jax.experimental.pallas import tpu as pltpu
from jax.sharding import PartitionSpec as P

D = 768
HEADS = 12
HEAD_DIM = 64
FF = 3072
CLASSES = 1000
LAYERS = 3
STEP_INDEX = 10
S = 197
PAD = 208

EPS_NORM = 1e-06
CLIP = 0.1
BETA_ONE = 0.9
BETA_TWO = 0.95
ADAM_EPS = 1e-08
DECAY = 0.05
RATE_MATRIX = 0.03
RATE_OUTPUT = 0.2
RATE_VECTOR = 0.3
SMOOTH = 0.1

F32 = jnp.float32
BF = jnp.bfloat16
NN = (((1,), (0,)), ((), ()))
NT = (((1,), (1,)), ((), ()))
TN = (((0,), (0,)), ((), ()))
VMEM_SPEC = pl.BlockSpec(memory_space=pltpu.VMEM)
ANY_SPEC = pl.BlockSpec(memory_space=pl.ANY)
LIMIT = 61 * 1024 * 1024


def dot(left, right, form=NN):
    return lax.dot_general(left, right, form, preferred_element_type=F32)


def normalize(values, gain_row, shift_row):
    center = values - jnp.mean(values, -1, keepdims=True)
    spread = jnp.mean(center * center, -1, keepdims=True)
    return center * lax.rsqrt(spread + EPS_NORM) * gain_row + shift_row


def normalize_back(values, gain_row, grad):
    center = values - jnp.mean(values, -1, keepdims=True)
    spread = jnp.mean(center * center, -1, keepdims=True)
    scale = lax.rsqrt(spread + EPS_NORM)
    unit = center * scale
    d_unit = grad * gain_row
    d_values = scale * (
        d_unit
        - jnp.mean(d_unit, -1, keepdims=True)
        - unit * jnp.mean(d_unit * unit, -1, keepdims=True)
    )
    return (
        d_values,
        jnp.sum(grad * unit, 0, keepdims=True),
        jnp.sum(grad, 0, keepdims=True),
    )


def gelu_and_slope(u):
    x = jnp.abs(u) * 0.7071067811865476
    t = 1.0 / (1.0 + 0.3275911 * x)
    series = t * (
        0.254829592
        + t * (-0.284496736 + t * (1.421413741 + t * (-1.453152027 + t * 1.061405429)))
    )
    bell = jnp.exp(-0.5 * u * u)
    tail = 0.5 * series * bell
    share = jnp.where(u >= 0.0, 1.0 - tail, tail)
    return u * share, share + u * bell * 0.3989422804014327


class Plan:
    def __init__(self, mesh):
        self.wide, self.grp = mesh.shape["wide"], mesh.shape["grp"]
        self.n = self.wide * self.grp
        self.cube = self.wide == 8 and self.grp == 4

    def where(self):
        if not self.cube:
            return 0, 0, 0, 0
        wide, grp = lax.axis_index("wide"), lax.axis_index("grp")
        return wide // 2, wide % 2, grp // 2, grp % 2


CHIPS = (4, 2, 2)
BLOCK = D // 16
BLOCK_FF = FF // 32


def cols_shape(columns):
    return CHIPS + (BLOCK, columns)


ROWS_SHAPE = CHIPS + (2, BLOCK_FF, D)


def cut_of(columns):
    return (columns // 2 + 127) // 128 * 128


class Gather:
    def __init__(self, plan, by_cols, block, whole, send, recv):
        self.z, self.x, self.y, self.c = plan.where()
        self.by_cols, self.block, self.whole = by_cols, block, whole
        self.send, self.recv = send, recv
        self.width = block.shape[-1]

    def region(self, z, x, y, start, width):
        if self.by_cols:
            first = pl.multiple_of(self.c * self.width + start, 128)
            return self.whole.at[z, x, y, :, pl.ds(first, width)]
        return self.whole.at[z, x, y, self.c, :, pl.ds(start, width)]

    def copy(self, at):
        z, x, y, c = self.z, self.x, self.y, self.c
        width, cut, line = self.width, cut_of(self.width), slice(None)
        if at < 3:
            src, dst = self.block, self.region(z, x, y, 0, width)
            to = (jnp.bitwise_xor(z, at + 1) * 2 + x, y * 2 + c)
        else:
            src = dst = (
                lambda: self.region(line, x, y, 0, width),
                lambda: self.region(line, x, y, 0, width),
                lambda: self.region(line, x, 1 - y, 0, cut),
                lambda: self.region(line, 1 - x, y, cut, width - cut),
                lambda: self.region(line, x, y, 0, width),
                lambda: self.region(line, 1 - x, y, 0, width),
                lambda: self.region(line, x, 1 - y, 0, width),
                lambda: self.region(line, 1 - x, 1 - y, 0, cut),
                lambda: self.region(line, 1 - x, 1 - y, cut, width - cut),
            )[at - 3]()
            over_x, over_y, over_c = (z * 2 + 1 - x, y * 2 + c), (z * 2 + x, (1 - y) * 2 + c), (z * 2 + x, y * 2 + 1 - c)
            to = (over_x, over_y, over_x, over_y, over_c, over_c, over_c, over_c, over_c)[at - 3]
        return pltpu.make_async_remote_copy(
            src_ref=src,
            dst_ref=dst,
            send_sem=self.send.at[at],
            recv_sem=self.recv.at[at],
            device_id=to,
            device_id_type=pl.DeviceIdType.MESH,
        )

    def keep(self):
        here = self.region(self.z, self.x, self.y, 0, self.width)
        return pltpu.make_async_copy(self.block, here, self.send.at[12])

    def start(self, *which):
        for at in which:
            self.copy(at).start()

    def arrived(self, *which):
        for at in which:
            self.copy(at).wait_recv()

    def stage0(self):
        self.start(0, 1, 2)
        self.keep().start()

    def stage1(self):
        self.arrived(0, 1, 2)
        self.keep().wait()
        self.start(3, 4, 7)

    def stage2(self):
        self.arrived(3, 4)
        self.start(5, 6, 8, 9)

    def stage3(self):
        self.arrived(5, 6)
        self.start(10, 11)

    def finish(self):
        self.arrived(7, 8, 9, 10, 11)
        for at in range(12):
            self.copy(at).wait_send()


def cube_barrier(plan):
    z, x, y, c = plan.where()
    barrier = pltpu.get_barrier_semaphore()
    partners = [(jnp.bitwise_xor(z, k) * 2 + x, y * 2 + c) for k in (1, 2, 3)]
    partners += [
        (z * 2 + 1 - x, y * 2 + c),
        (z * 2 + x, (1 - y) * 2 + c),
        (z * 2 + x, y * 2 + 1 - c),
    ]
    for partner in partners:
        pl.semaphore_signal(barrier, inc=1, device_id=partner, device_id_type=pl.DeviceIdType.MESH)
    pl.semaphore_wait(barrier, len(partners))


def load(source, target, sem):
    copy = pltpu.make_async_copy(source, target, sem)
    copy.start()
    return copy


def start_all(copies):
    for copy in copies:
        copy.start()


def wait_all(copies):
    for copy in copies:
        copy.wait()


def weight(ref, first, width):
    cols = pl.ds(first if isinstance(first, int) else pl.multiple_of(first, 128), width)
    return ref[:, :, :, :, cols].reshape(D, width)


class SmallGather:
    def __init__(self, plan, block, whole, send, recv):
        self.z, self.x, self.y, self.c = plan.where()
        self.block, self.whole, self.send, self.recv = block, whole, send, recv

    def copy(self, at):
        z, x, y, c = self.z, self.x, self.y, self.c
        line = slice(None)
        if at < 3:
            src, dst = self.block, self.whole.at[z, x, y, c]
            to = (jnp.bitwise_xor(z, at + 1) * 2 + x, y * 2 + c)
        elif at == 3:
            src = dst = self.whole.at[line, x, y, c]
            to = (z * 2 + 1 - x, y * 2 + c)
        elif at == 4:
            src = dst = self.whole.at[line, line, y, c]
            to = (z * 2 + x, (1 - y) * 2 + c)
        else:
            src = dst = self.whole.at[line, line, line, c]
            to = (z * 2 + x, y * 2 + 1 - c)
        return pltpu.make_async_remote_copy(
            src_ref=src,
            dst_ref=dst,
            send_sem=self.send.at[at],
            recv_sem=self.recv.at[at],
            device_id=to,
            device_id_type=pl.DeviceIdType.MESH,
        )

    def keep(self):
        here = self.whole.at[self.z, self.x, self.y, self.c]
        return pltpu.make_async_copy(self.block, here, self.send.at[6])

    def stage0(self):
        for at in range(3):
            self.copy(at).start()
        self.keep().start()

    def stage1(self):
        for at in range(3):
            self.copy(at).wait_recv()
        self.keep().wait()
        self.copy(3).start()

    def stage2(self):
        self.copy(3).wait_recv()
        self.copy(4).start()

    def stage3(self):
        self.copy(4).wait_recv()
        self.copy(5).start()

    def finish(self):
        self.copy(5).wait_recv()
        for at in range(6):
            self.copy(at).wait_send()


FF_TILE = 512
HALF = BLOCK // 2
WIDTH = FF // 2
HEAD_ROWS = 16
HEAD_BLOCK = 32
FINAL = S + 2 + 4 * LAYERS


def saved_shapes(rows):
    heads = rows // PAD * HEADS
    return dict(
        h=((rows, D), F32),
        a=((rows, D), BF),
        t=((rows, 3 * D), BF),
        o=((rows, D), BF),
        p=((heads, PAD, PAD), BF),
        h1=((rows, D), F32),
        m=((rows, D), BF),
        z=((rows, FF), BF),
        slope=((rows, FF), BF),
    )


SAVED = tuple(saved_shapes(PAD))


def row(ref, at):
    return ref[pl.ds(at, 1)]


def share_shards(plan, r):
    z, x, y, c = plan.where()
    r.joined_f[:, :, : 3 * D] = r.triple[...]
    r.joined_f[:, :, 3 * D :] = r.output[...]
    mine = pl.ds(pl.multiple_of(c * HALF, 8), HALF)

    def part(core, width):
        return pl.ds(pl.multiple_of(core * width, 128), width)

    moves = [
        (r.patch.at[:, part(1 - c, D // 2)], r.patch_f.at[mine]),
        (r.joined_f.at[:, :, part(1 - c, WIDTH)], r.joined_b.at[:, mine]),
        (r.expand.at[:, :, part(1 - c, WIDTH)], r.expand_b.at[:, mine]),
    ]
    copies = [
        pltpu.make_async_remote_copy(
            src_ref=src,
            dst_ref=dst,
            send_sem=r.share_send.at[i],
            recv_sem=r.share_recv.at[i],
            device_id=(z * 2 + x, y * 2 + 1 - c),
            device_id_type=pl.DeviceIdType.MESH,
        )
        for i, (src, dst) in enumerate(moves)
    ]
    start_all(copies)
    r.patch_f[mine] = r.patch[:, part(c, D // 2)]
    r.joined_b[:, mine] = r.joined_f[:, :, part(c, WIDTH)]
    r.expand_b[:, mine] = r.expand[:, :, part(c, WIDTH)]
    r.shrink_block[...] = r.shrink[...].astype(BF)
    for copy, src, dst in zip(
        copies,
        (r.patch_f, r.joined_b, r.expand_b),
        (r.patch_block, r.joined_block, r.expand_block),
    ):
        copy.wait_recv()
        dst[...] = src[...].astype(BF)
    for copy in copies:
        copy.wait_send()


def head_part(r, image_total):
    images = r.h.shape[0] // PAD
    table = r.head[:D].astype(BF)
    r.first[...] = jnp.zeros_like(r.first)
    for image in range(images):
        r.first[image : image + 1] = r.h[image * PAD : image * PAD + 1]
    first = r.first[...]
    gain, shift = r.vectors[FINAL : FINAL + 1], r.vectors[FINAL + 1 : FINAL + 2]
    feature = normalize(first, gain, shift).astype(BF)
    logits = dot(feature, table) + r.head[D : D + 1]
    ids = lax.broadcasted_iota(jnp.int32, logits.shape, 1)
    shifted = logits - jnp.max(logits, -1, keepdims=True)
    log_prob = shifted - jnp.log(jnp.sum(jnp.exp(shifted), -1, keepdims=True))
    target = jnp.where(ids == r.labels[...], 1.0 - SMOOTH, 0.0) + SMOOTH / CLASSES
    weights = r.weights[...]
    loss = jnp.sum(weights * -jnp.sum(target * log_prob, -1, keepdims=True))
    d_logits = ((weights / image_total) * (jnp.exp(log_prob) - target)).astype(BF)
    d_feature = dot(d_logits, table, NT)
    r.d_logits[...] = jnp.zeros_like(r.d_logits)
    r.d_logits[:, :CLASSES] = d_logits.astype(F32)
    r.head_block[...] = jnp.zeros_like(r.head_block)
    feature = feature.astype(F32)
    for image in range(images):
        for j in range(6):
            at = image * 14 + j
            r.head_block[at : at + 1] = feature[image : image + 1, j * 128 : j * 128 + 128]
        for j in range(8):
            at = image * 14 + 6 + j
            r.head_block[at : at + 1] = r.d_logits[image : image + 1, j * 128 : j * 128 + 128]
    d_first, d_gain, d_shift = normalize_back(first, gain, d_feature)
    r.g[...] = jnp.zeros_like(r.g)
    for image in range(images):
        r.g[image * PAD : image * PAD + 1] = d_first[image : image + 1]
    r.tail[...] = jnp.zeros_like(r.tail)
    r.tail[0:1] = jnp.full((1, D), loss, F32)
    r.tail[1:2] = d_gain
    r.tail[2:3] = d_shift


def forward_kernel(plan, names, *refs):
    r = SimpleNamespace(**dict(zip(names, refs)))
    cube = plan.cube
    images = r.images.shape[0]
    patch, joined, expand, shrink = range(4)
    wholes = (r.patch_whole, r.joined_whole, r.expand_whole, r.shrink_whole)
    weights = (r.patch_w, r.joined_w, r.expand_w, r.shrink_w)
    if cube:
        blocks = (r.patch_block, r.joined_block, r.expand_block, r.shrink_block)
        cube_barrier(plan)
        share_shards(plan, r)
        r.count[...] = jnp.full((8, 128), jnp.sum(r.weights[...]), F32)
        counting = SmallGather(plan, r.count, r.counts, r.count_send, r.count_recv)

    def unit(kind, layer):
        if kind == patch:
            return Gather(plan, True, blocks[0], wholes[0], r.send.at[0], r.recv.at[0])
        at = 3 * layer + kind
        block, whole = blocks[kind].at[layer], wholes[kind].at[layer]
        return Gather(plan, kind != shrink, block, whole, r.send.at[at], r.recv.at[at])

    def ready(kind, layer):
        if cube:
            unit(kind, layer).finish()
        whole = wholes[kind] if kind == patch else wholes[kind].at[layer]
        return load(whole, weights[kind], r.loads.at[kind])

    held = (r.h, r.a, r.t, r.o, r.p, r.h1, r.m, r.z, r.slope)
    kept = (r.keep_h, r.keep_a, r.keep_t, r.keep_o, r.keep_p, r.keep_h1, r.keep_m, r.keep_z, r.keep_slope)
    h_, a_, t_, o_, p_, h1_, m_, z_, slope_ = range(9)

    def saves(layer, *which):
        return [pltpu.make_async_copy(held[k], kept[k].at[layer], r.saves.at[k]) for k in which]

    if cube:
        unit(patch, 0).stage0()
        counting.stage0()
        unit(joined, 0).stage0()
        unit(patch, 0).stage1()
        unit(expand, 0).stage0()
        unit(joined, 0).stage1()
        unit(patch, 0).stage2()
        unit(shrink, 0).stage0()
        unit(expand, 0).stage1()
        unit(joined, 0).stage2()
        unit(patch, 0).stage3()
    ready(patch, 0).wait()
    for image in range(images):
        at = image * PAD
        r.h[at : at + 1] = r.vectors[0:1] + r.vectors[S : S + 1]
        embedded = dot(r.images[image], weight(r.patch_w, 0, D))
        r.h[at + 1 : at + S] = embedded + r.vectors[S + 1 : S + 2] + r.vectors[1:S]
        r.h[at + S : at + PAD] = jnp.zeros((PAD - S, D), F32)

    low_lane = lax.broadcasted_iota(jnp.int32, (PAD, 128), 1) < HEAD_DIM
    real_key = lax.broadcasted_iota(jnp.int32, (PAD, PAD), 0) < S

    @pl.loop(0, LAYERS)
    def _(layer):
        more = layer < LAYERS - 1
        base = S + 2 + 4 * layer
        if cube:
            pl.when(more)(lambda: unit(joined, layer + 1).stage0())
            unit(shrink, layer).stage1()
            unit(expand, layer).stage2()
            unit(joined, layer).stage3()
        start_all(saves(layer, h_))

        @pl.when(layer > 0)
        def _():
            wait_all(saves(layer, a_, t_, o_, p_, h1_, m_))

        r.a[...] = normalize(r.h[...], row(r.vectors, base), row(r.vectors, base + 1)).astype(BF)
        ready(joined, layer).wait()

        @pl.loop(0, 3)
        def _(j):
            cols = pl.ds(pl.multiple_of(j * D, 128), D)
            r.t[:, cols] = dot(r.a[...], weight(r.joined_w, j * D, D)).astype(BF)

        start_all(saves(layer, a_, t_))

        @pl.loop(0, images * (HEADS // 2))
        def _(step):
            image, pair = step // (HEADS // 2), step % (HEADS // 2)
            rows = pl.ds(pl.multiple_of(image * PAD, 16), PAD)
            lanes = [pl.ds(pl.multiple_of(pair * 128 + part * D, 128), 128) for part in range(3)]
            q, key, v = (r.t[rows, lane] for lane in lanes)
            zero = jnp.zeros_like(key)
            outs = []
            for which in range(2):
                part = jnp.where(low_lane, key, zero) if which == 0 else jnp.where(low_lane, zero, key)
                scores = dot(part, q, NT) * HEAD_DIM**-0.5
                scores = jnp.where(real_key, scores, -1e30)
                top = jnp.max(scores, 0, keepdims=True)
                e = jnp.exp(scores - top)
                p = (e * (1.0 / jnp.sum(e, 0, keepdims=True))).astype(BF)
                r.p[step * 2 + which] = p
                outs.append(dot(p, v, TN))
            r.o[rows, lanes[0]] = jnp.where(low_lane, outs[0], outs[1]).astype(BF)

        start_all(saves(layer, o_, p_))
        r.h1[...] = r.h[...] + dot(r.o[...], weight(r.joined_w, 3 * D, D))
        start_all(saves(layer, h1_))
        if cube:
            @pl.when(more)
            def _():
                unit(expand, layer + 1).stage0()
                unit(joined, layer + 1).stage1()

            unit(shrink, layer).stage2()
            unit(expand, layer).stage3()
            pl.when(layer == 0)(counting.stage1)
            pl.when(layer == 1)(counting.stage3)
        r.m[...] = normalize(r.h1[...], row(r.vectors, base + 2), row(r.vectors, base + 3)).astype(BF)
        start_all(saves(layer, m_))
        wait_all(saves(layer, h_))
        r.h[...] = r.h1[...]

        @pl.when(layer > 0)
        def _():
            wait_all(saves(layer, z_, slope_))

        ready(expand, layer).wait()

        @pl.loop(0, FF // FF_TILE)
        def _(j):
            cols = pl.ds(pl.multiple_of(j * FF_TILE, 128), FF_TILE)
            u = dot(r.m[...], weight(r.expand_w, j * FF_TILE, FF_TILE))
            z, slope = gelu_and_slope(u)
            r.z[:, cols] = z.astype(BF)
            r.slope[:, cols] = slope.astype(BF)

        start_all(saves(layer, z_, slope_))
        if cube:
            @pl.when(more)
            def _():
                unit(shrink, layer + 1).stage0()
                unit(expand, layer + 1).stage1()
                unit(joined, layer + 1).stage2()

            unit(shrink, layer).stage3()
            pl.when(layer == 0)(counting.stage2)
            pl.when(layer == 1)(counting.finish)
        ready(shrink, layer).wait()

        @pl.loop(0, 4)
        def _(j):
            cols = pl.ds(pl.multiple_of(j * D, 128), D)
            r.h[...] += dot(r.z[:, cols], r.shrink_w[j].reshape(D, D))

    if cube:
        r.total[...] = jnp.sum(r.counts[...].reshape(-1, 8, 128), 0)
        image_total = r.total[0:1, 0:1]
    else:
        image_total = r.count_in[0:1, 0:1]
    head_part(r, image_total)
    wait_all(saves(LAYERS - 1, a_, t_, o_, p_, h1_, m_, z_, slope_))


def pallas(kernel, name, inputs, outputs, scratch, **params):
    names = list(inputs) + list(outputs) + list(scratch)
    outs = pl.pallas_call(
        functools.partial(kernel, names),
        out_shape=[jax.ShapeDtypeStruct(shape, kind) for shape, kind, _ in outputs.values()],
        in_specs=[spec for _, spec in inputs.values()],
        out_specs=[spec for _, _, spec in outputs.values()],
        scratch_shapes=list(scratch.values()),
        compiler_params=pltpu.CompilerParams(vmem_limit_bytes=LIMIT, **params),
        name=name,
    )(*[value for value, _ in inputs.values()])
    return SimpleNamespace(**dict(zip(outputs, outs)))


def given_in(spec, **values):
    return {name: (value, spec) for name, value in values.items()}


def vmem(kind, **shapes):
    return {name: pltpu.VMEM(shape, kind) for name, shape in shapes.items()}


def dma(**counts):
    return {name: pltpu.SemaphoreType.DMA(count) for name, count in counts.items()}


def forward(plan, shards, args, gathered, count):
    rows = args["images"].shape[0] * PAD
    shapes = saved_shapes(rows)
    whole = dict(
        patch_whole=cols_shape(D),
        joined_whole=(LAYERS,) + cols_shape(FF),
        expand_whole=(LAYERS,) + cols_shape(FF),
        shrink_whole=(LAYERS,) + ROWS_SHAPE,
    )
    inputs = given_in(VMEM_SPEC, **args)
    outputs = {}
    if plan.cube:
        inputs.update(given_in(VMEM_SPEC, **shards))
        outputs.update({name: (shape, BF, ANY_SPEC) for name, shape in whole.items()})
    else:
        inputs.update(given_in(ANY_SPEC, **dict(zip(whole, gathered))))
        inputs.update(given_in(VMEM_SPEC, count_in=count))
    for name, (shape, kind) in shapes.items():
        outputs["keep_" + name] = ((LAYERS,) + shape, kind, ANY_SPEC)
    outputs.update(
        g=((rows, D), F32, VMEM_SPEC),
        tail=((8, D), F32, VMEM_SPEC),
        head_block=((HEAD_BLOCK, 128), F32, VMEM_SPEC),
        total=((8, 128), F32, VMEM_SPEC),
    )
    scratch = vmem(
        BF,
        patch_w=cols_shape(D),
        joined_w=cols_shape(FF),
        expand_w=cols_shape(FF),
        shrink_w=ROWS_SHAPE,
    )
    scratch.update({name: pltpu.VMEM(shape, kind) for name, (shape, kind) in shapes.items()})
    scratch.update(vmem(F32, first=(HEAD_ROWS, D), d_logits=(HEAD_ROWS, 1024)))
    scratch.update(dma(saves=(9,), loads=(4,)))
    extra = {}
    if plan.cube:
        scratch.update(
            vmem(
                F32,
                joined_f=(LAYERS, HALF, FF),
                joined_b=(LAYERS, BLOCK, WIDTH),
                expand_b=(LAYERS, BLOCK, WIDTH),
                patch_f=(BLOCK, D // 2),
                count=(8, 128),
                counts=CHIPS + (2, 8, 128),
            )
        )
        scratch.update(
            vmem(
                BF,
                patch_block=(BLOCK, D // 2),
                joined_block=(LAYERS, BLOCK, WIDTH),
                expand_block=(LAYERS, BLOCK, WIDTH),
                shrink_block=(LAYERS, BLOCK_FF, D),
            )
        )
        scratch.update(
            dma(send=(10, 13), recv=(10, 12), share_send=(3,), share_recv=(3,), count_send=(7,), count_recv=(7,))
        )
        extra = dict(collective_id=1, has_side_effects=True)
    got = pallas(functools.partial(forward_kernel, plan), "forward", inputs, outputs, scratch, **extra)
    if not plan.cube:
        for name, value in zip(whole, gathered):
            setattr(got, name, value)
        got.total = count
    return got


UNITS = 3 * LAYERS
TAIL = 512
SEND = 4
VEC_ROWS = 256


def relative(plan):
    z, x, y, c = plan.where()
    return c, (z * 2 + x) * 2 + y


def place(plan, slot, core, chip):
    my_core, my_chip = relative(plan)
    at = jnp.bitwise_xor(my_chip, chip)
    other = jnp.bitwise_xor(my_core, core)
    return slot + (SEND - slot) * other, at // 4, at % 4


def store_cols(plan, out, slot, tile, width, value, half=WIDTH):
    per_half = half // width
    lanes = pl.ds(pl.multiple_of((tile % per_half) * width, 128), width)
    for b in range(16):
        rows = value[b * BLOCK : (b + 1) * BLOCK].astype(BF)
        out[(*place(plan, slot, tile // per_half, b), slice(None), lanes)] = rows


def store_rows(plan, out, slot, tile, value):
    for b in range(4):
        at = place(plan, slot, b % 2, tile * 2 + b // 2)
        for part in range(2):
            first = b * BLOCK_FF + part * BLOCK
            out[(*at, slice(None), pl.ds(part * D, D))] = value[first : first + BLOCK].astype(BF)


def store_vectors(plan, out, slot, value):
    for b in range(32):
        rows = value[b * 8 : b * 8 + 8]
        block = jnp.concatenate([rows[:, j * 128 : j * 128 + 128] for j in range(6)], 0)
        out[(*place(plan, slot, b % 2, b // 2), slice(None), pl.ds(D // 2, 128))] = block.astype(BF)


class Reduce:
    def __init__(self, plan, bufs, unit, width=WIDTH):
        self.plan, self.bufs, self.unit, self.width = plan, bufs, unit, width
        self.z, self.x, self.y, self.c = plan.where()
        self.cut = width // 2
        self.slot, self.three, self.two = unit % 4, unit % 3, unit % 2

    def copy(self, at):
        z, x, y, c = self.z, self.x, self.y, self.c
        bufs, slot, three, width, cut = self.bufs, self.slot, self.three, self.width, self.cut
        line = slice(None)
        full, left, right = pl.ds(0, width), pl.ds(0, cut), pl.ds(cut, width - cut)
        over_x, over_y, over_c = (
            (z * 2 + 1 - x, y * 2 + c),
            (z * 2 + x, (1 - y) * 2 + c),
            (z * 2 + x, y * 2 + 1 - c),
        )
        unit = bufs.unit
        if at == 0:
            src, dst, to = unit.at[SEND, :, :, :, full], bufs.core.at[:, :, :, full], over_c
        elif at == 1:
            src, dst, to = unit.at[slot, :, 3, :, left], bufs.near.at[three, :, :, left], over_x
        elif at == 2:
            src, dst, to = unit.at[slot, :, 3, :, right], bufs.far.at[three, :, :, left], over_y
        elif at == 3:
            src, dst, to = unit.at[slot, :, 1, :, full], bufs.y.at[three, :, :, full], over_y
        elif at == 4:
            src, dst, to = unit.at[slot, :, 2, :, full], bufs.x.at[three, :, :, full], over_x
        elif at < 8:
            k = at - 4
            src = bufs.line.at[self.two, k, :, full]
            dst = bufs.z.at[slot, k - 1, :, full]
            to = (jnp.bitwise_xor(z, k) * 2 + x, y * 2 + c)
        else:
            rows = pl.ds(pl.multiple_of((1 - c) * HALF, 8), HALF)
            if width == WIDTH:
                src, dst = bufs.total.at[self.two, rows], bufs.owned.at[self.unit, c]
            else:
                cols = pl.ds(0, D // 2)
                src, dst = bufs.total.at[self.two, rows, cols], bufs.patch.at[c]
            to = over_c
        return pltpu.make_async_remote_copy(
            src_ref=src,
            dst_ref=dst,
            send_sem=bufs.send.at[slot, at],
            recv_sem=bufs.recv.at[slot, at],
            device_id=to,
            device_id_type=pl.DeviceIdType.MESH,
        )

    def own(self, by_rows):
        bufs, c = self.bufs, self.c
        sem = bufs.send
        if by_rows:
            return [
                pltpu.make_async_copy(
                    bufs.total.at[self.two, pl.ds(part * HALF, HALF)],
                    bufs.owned.at[self.unit, part],
                    sem.at[self.slot, 9 + part],
                )
                for part in range(2)
            ]
        rows = pl.ds(pl.multiple_of(c * HALF, 8), HALF)
        if self.width == WIDTH:
            src, dst = bufs.total.at[self.two, rows], bufs.owned.at[self.unit, c]
        else:
            src, dst = bufs.total.at[self.two, rows, pl.ds(0, D // 2)], bufs.patch.at[c]
        return [pltpu.make_async_copy(src, dst, sem.at[self.slot, 9])]

    def credit(self):
        return self.bufs.credit

    def stage0(self):
        @pl.when(self.unit > 0)
        def _():
            pl.semaphore_wait(self.credit(), 1)

        self.copy(0).start()

    def stage1(self):
        unit, core, slot = self.bufs.unit, self.bufs.core, self.slot
        cols = pl.ds(0, self.width)
        self.copy(0).wait_recv()

        def add(z, chip):
            both = unit[slot, z, chip, :, cols].astype(F32) + core[z, chip, :, cols].astype(F32)
            unit[slot, z, chip, :, cols] = both.astype(BF)

        pl.loop(0, 4)(lambda z: add(z, 3))
        self.copy(1).start()
        self.copy(2).start()
        pl.loop(0, 12)(lambda i: add(i // 3, i % 3))

        @pl.when(self.unit < UNITS)
        def _():
            z, x, y, c = self.z, self.x, self.y, self.c
            pl.semaphore_signal(
                self.credit(),
                inc=1,
                device_id=(z * 2 + x, y * 2 + 1 - c),
                device_id_type=pl.DeviceIdType.MESH,
            )

    def stage2(self):
        unit, slot, cut = self.bufs.unit, self.slot, self.cut
        left, right = pl.ds(0, cut), pl.ds(cut, self.width - cut)
        self.copy(1).wait_recv()
        self.copy(2).wait_recv()

        @pl.loop(0, 4)
        def _(z):
            for chip, cols, landed in ((1, left, self.bufs.near), (2, right, self.bufs.far)):
                got = landed[self.three, z, :, left].astype(F32)
                unit[slot, z, chip, :, cols] = (unit[slot, z, chip, :, cols].astype(F32) + got).astype(BF)

        self.copy(3).start()
        self.copy(4).start()
        self.copy(1).wait_send()
        self.copy(2).wait_send()

    def stage3(self):
        bufs, cols = self.bufs, pl.ds(0, self.width)
        self.copy(3).wait_recv()
        self.copy(4).wait_recv()

        @pl.loop(0, 4)
        def _(z):
            bufs.line[self.two, z, :, cols] = (
                bufs.unit[self.slot, z, 0, :, cols].astype(F32)
                + bufs.y[self.three, z, :, cols].astype(F32)
                + bufs.x[self.three, z, :, cols].astype(F32)
            ).astype(BF)

        for at in (5, 6, 7):
            self.copy(at).start()
        self.copy(3).wait_send()
        self.copy(4).wait_send()

    def stage4(self, by_rows):
        bufs, cols = self.bufs, pl.ds(0, self.width)
        for at in (5, 6, 7):
            self.copy(at).wait_recv()
        total = bufs.line[self.two, 0, :, cols].astype(F32)
        for k in range(3):
            total = total + bufs.z[self.slot, k, :, cols].astype(F32)
        bufs.total[self.two, :, cols] = total
        bufs.squares[0:1, cols] += jnp.sum(total * total, 0, keepdims=True)
        if not by_rows:
            self.copy(8).start()
        start_all(self.own(by_rows))
        for at in (5, 6, 7):
            self.copy(at).wait_send()

    def stage5(self, by_rows):
        if not by_rows:
            self.copy(8).wait()
        wait_all(self.own(by_rows))


def backward_kernel(plan, names, *refs):
    r = SimpleNamespace(**dict(zip(names, refs)))
    cube = plan.cube
    images = r.images.shape[0]
    loads = [
        (r.keep_z, r.vm_z),
        (r.shrink_whole, r.shrink_w),
        (r.keep_slope, r.vm_slope),
        (r.expand_whole, r.expand_w),
        (r.keep_m, r.vm_m),
        (r.keep_h1, r.vm_h1),
        (r.keep_o, r.vm_o),
        (r.keep_t, r.vm_t),
        (r.keep_p, r.vm_p),
        (r.keep_a, r.vm_a),
        (r.keep_h, r.vm_h),
        (r.joined_whole, r.expand_w),
    ]
    z_, shrink_, slope_, expand_, m_, h1_, o_, t_, p_, a_, h_, joined_ = range(12)
    top = LAYERS - 1

    def fetch(which, layer):
        src, dst = loads[which]
        return pltpu.make_async_copy(src.at[layer], dst, r.loads.at[which])

    def start(layer, *which):
        for k in which:
            fetch(k, layer).start()

    def wait(layer, *which):
        for k in which:
            fetch(k, layer).wait()

    first_g = load(r.g_in, r.g, r.loads.at[joined_ + 1])
    start(top, *range(joined_))
    if cube:
        cube_barrier(plan)
        r.squares[...] = jnp.zeros_like(r.squares)
        head_rows = SmallGather(plan, r.head_block, r.head_rows, r.head_send, r.head_recv)
        head_rows.stage0()
    r.vectors[...] = jnp.zeros_like(r.vectors)
    r.vectors[FINAL : FINAL + 2] = r.tail_in[1:3]
    first_g.wait()

    def tick(it, kind):
        unit = 3 * it + kind
        if not cube:
            copies = [
                pltpu.make_async_copy(r.unit.at[(unit % 4, SEND)[i]], r.full.at[unit, i], r.loads.at[joined_ + 1 + i])
                for i in range(2)
            ]
            start_all(copies)
            wait_all(copies)
            return

        def when(back, do):
            if kind >= back:
                do()
            else:
                pl.when(unit >= back)(do)

        def by_rows(back):
            return (kind - back) % 3 == 0

        when(1, lambda: Reduce(plan, r, unit - 1).stage1())
        Reduce(plan, r, unit).stage0()
        when(2, lambda: Reduce(plan, r, unit - 2).stage2())
        when(3, lambda: Reduce(plan, r, unit - 3).stage3())
        when(5, lambda: Reduce(plan, r, unit - 5).stage5(by_rows(5)))
        when(4, lambda: Reduce(plan, r, unit - 4).stage4(by_rows(4)))

    def sent(unit):
        if cube:
            pl.when(unit > 0)(lambda: Reduce(plan, r, unit - 1).copy(0).wait_send())

    low_lane = lax.broadcasted_iota(jnp.int32, (PAD, 128), 1) < HEAD_DIM
    scale = HEAD_DIM**-0.5

    @pl.loop(0, LAYERS)
    def _(it):
        layer = top - it
        below = it < LAYERS - 1
        base = S + 2 + 4 * layer
        r.gr[...] = r.g[...].astype(BF)
        wait(layer, z_)
        slot = (3 * it) % 4
        sent(3 * it)

        @pl.loop(0, 8)
        def _(j):
            cols = pl.ds(pl.multiple_of(j * (D // 2), 128), D // 2)
            store_rows(plan, r.unit, slot, j, dot(r.vm_z[:, cols], r.gr[...], TN))

        tick(it, 0)
        if cube:
            pl.when(it == 0)(head_rows.stage1)
            pl.when(it == 1)(head_rows.finish)
        wait(layer, shrink_, slope_, expand_, m_, h1_)
        pl.when(below)(lambda: start(layer - 1, z_))
        slot_e = (3 * it + 1) % 4
        r.g1[...] = jnp.zeros_like(r.g1)
        sent(3 * it + 1)

        @pl.loop(0, 4)
        def _(j):
            cols = pl.ds(pl.multiple_of(j * D, 128), D)
            dz = dot(r.gr[...], r.shrink_w[j].reshape(D, D), NT)
            du = (dz * r.vm_slope[:, cols].astype(F32)).astype(BF)
            r.g1[...] += dot(du, weight(r.expand_w, j * D, D), NT)
            store_cols(plan, r.unit, slot_e, j, D, dot(r.vm_m[...], du, TN))

        start(layer, joined_)
        pl.when(below)(lambda: start(layer - 1, shrink_, slope_, m_))
        tick(it, 1)
        if cube:
            pl.when(it == 0)(head_rows.stage2)
        d_h1, d_gain, d_shift = normalize_back(r.vm_h1[...], row(r.params, base + 2), r.g1[...])
        r.g1[...] = r.g[...] + d_h1
        r.vectors[pl.ds(base + 2, 1)] = d_gain
        r.vectors[pl.ds(base + 3, 1)] = d_shift
        pl.when(below)(lambda: start(layer - 1, h1_))

        r.gr[...] = r.g1[...].astype(BF)
        slot_t = (3 * it + 2) % 4
        wait(layer, o_)
        sent(3 * it + 2)
        store_cols(plan, r.unit, slot_t, 3, D, dot(r.vm_o[...], r.gr[...], TN))
        wait(layer, joined_)
        r.do[...] = dot(r.gr[...], weight(r.expand_w, 3 * D, D), NT).astype(BF)
        wait(layer, t_, p_, a_, h_)

        @pl.loop(0, images * (HEADS // 2))
        def _(step):
            image, pair = step // (HEADS // 2), step % (HEADS // 2)
            rows = pl.ds(pl.multiple_of(image * PAD, 16), PAD)
            lanes = [pl.ds(pl.multiple_of(pair * 128 + part * D, 128), 128) for part in range(3)]
            q, key, v = (r.vm_t[rows, lane] for lane in lanes)
            do = r.do[rows, lanes[0]]
            zero = jnp.zeros_like(v)
            dqs, dks, dvs = [], [], []
            for which in range(2):
                part = jnp.where(low_lane, v, zero) if which == 0 else jnp.where(low_lane, zero, v)
                p_low = r.vm_p[step * 2 + which]
                p = p_low.astype(F32)
                dvs.append(dot(p_low, do))
                dp = dot(part, do, NT)
                ds = (p * (dp - jnp.sum(p * dp, 0, keepdims=True))).astype(BF)
                dqs.append(dot(ds, key, TN))
                dks.append(dot(ds, q))
            r.dt[rows, lanes[0]] = (jnp.where(low_lane, dqs[0], dqs[1]) * scale).astype(BF)
            r.dt[rows, lanes[1]] = (jnp.where(low_lane, dks[0], dks[1]) * scale).astype(BF)
            r.dt[rows, lanes[2]] = jnp.where(low_lane, dvs[0], dvs[1]).astype(BF)

        pl.when(below)(lambda: start(layer - 1, o_, t_, p_))
        r.g[...] = jnp.zeros_like(r.g)

        @pl.loop(0, 3)
        def _(j):
            cols = pl.ds(pl.multiple_of(j * D, 128), D)
            store_cols(plan, r.unit, slot_t, j, D, dot(r.vm_a[...], r.dt[:, cols], TN))
            r.g[...] += dot(r.dt[:, cols], weight(r.expand_w, j * D, D), NT)

        tick(it, 2)
        if cube:
            pl.when(it == 0)(head_rows.stage3)
        d_h, d_gain, d_shift = normalize_back(r.vm_h[...], row(r.params, base), r.g[...])
        r.g[...] = r.g1[...] + d_h
        r.vectors[pl.ds(base, 1)] = d_gain
        r.vectors[pl.ds(base + 1, 1)] = d_shift
        pl.when(below)(lambda: start(layer - 1, a_, h_, expand_))

    slot = UNITS % 4
    sent(jnp.int32(UNITS))
    for part in range(2):
        half = D // 2
        value = jnp.zeros((D, half), F32)
        for image in range(images):
            rows = r.g[image * PAD + 1 : image * PAD + S, part * half : (part + 1) * half]
            value = value + dot(r.images[image], rows.astype(BF), TN)
        store_cols(plan, r.unit, slot, part, half, value, half)
    pos = r.g[:PAD]
    for image in range(1, images):
        pos = pos + r.g[image * PAD : (image + 1) * PAD]
    r.vectors[:S] = pos[:S]
    r.vectors[S : S + 1] = pos[:1]
    r.vectors[S + 1 : S + 2] = jnp.sum(pos[1:S], 0, keepdims=True)
    if not cube:
        copies = [
            pltpu.make_async_copy(r.unit.at[(slot, SEND)[i]], r.full.at[UNITS, i], r.loads.at[i])
            for i in range(2)
        ]
        copies.append(pltpu.make_async_copy(r.vectors, r.vector_rows, r.loads.at[2]))
        start_all(copies)
        wait_all(copies)
        return
    store_vectors(plan, r.unit, slot, r.vectors[...])

    def stage(unit, which):
        width = WIDTH if unit < UNITS else TAIL
        done = Reduce(plan, r, jnp.int32(unit), width)
        by_rows = unit % 3 == 0 and unit < UNITS
        (
            done.stage0,
            done.stage1,
            done.stage2,
            done.stage3,
            lambda: done.stage4(by_rows),
            lambda: done.stage5(by_rows),
        )[which]()

    for ahead in range(5):
        for which in (1, 0, 2, 3, 5, 4):
            unit = UNITS + ahead - which
            if unit <= UNITS:
                stage(unit, which)
    r.tail_block[:BLOCK] = r.total[UNITS % 2, :, D // 2 : TAIL]
    line = lax.broadcasted_iota(jnp.int32, (8, 128), 0)
    squares, loss = jnp.sum(r.squares[...]), r.tail_in[0:1, 0:128]
    r.tail_block[BLOCK:] = jnp.where(line == 0, squares, jnp.where(line == 1, loss, 0.0))
    gather = SmallGather(plan, r.tail_block, r.vector_rows, r.tail_send, r.tail_recv)
    gather.stage0()
    gather.stage1()
    gather.stage2()
    gather.stage3()
    stage(UNITS, 5)
    Reduce(plan, r, jnp.int32(UNITS), TAIL).copy(0).wait_send()
    gather.finish()


def backward(plan, images, params, done):
    rows = done.g.shape[0]
    shapes = saved_shapes(rows)
    inputs = given_in(VMEM_SPEC, images=images, params=params, tail_in=done.tail)
    if plan.cube:
        inputs.update(given_in(VMEM_SPEC, head_block=done.head_block))
    inputs.update(
        given_in(
            ANY_SPEC,
            g_in=done.g,
            joined_whole=done.joined_whole,
            expand_whole=done.expand_whole,
            shrink_whole=done.shrink_whole,
        )
    )
    inputs.update({"keep_" + name: (getattr(done, "keep_" + name), ANY_SPEC) for name in SAVED})
    if plan.cube:
        outputs = dict(
            owned=((UNITS, 2, HALF, WIDTH), F32, ANY_SPEC),
            patch=((2, HALF, D // 2), F32, ANY_SPEC),
            vector_rows=(CHIPS + (2, BLOCK + 8, 128), F32, ANY_SPEC),
            head_rows=(CHIPS + (2, HEAD_BLOCK, 128), F32, ANY_SPEC),
        )
    else:
        outputs = dict(
            full=((UNITS + 1, 2, 4, 4, BLOCK, WIDTH), BF, ANY_SPEC),
            vector_rows=((VEC_ROWS, D), F32, ANY_SPEC),
        )
    scratch = {"vm_" + name: pltpu.VMEM(shape, kind) for name, (shape, kind) in shapes.items()}
    scratch.update(
        vmem(
            BF,
            expand_w=cols_shape(FF),
            shrink_w=ROWS_SHAPE,
            gr=(rows, D),
            do=(rows, D),
            dt=(rows, 3 * D),
            unit=(SEND + 1, 4, 4, BLOCK, WIDTH),
        )
    )
    scratch.update(vmem(F32, g=(rows, D), g1=(rows, D), vectors=(VEC_ROWS, D)))
    scratch.update(dma(loads=(15,)))
    extra = {}
    if plan.cube:
        scratch.update(
            vmem(
                BF,
                core=(4, 4, BLOCK, WIDTH),
                near=(3, 4, BLOCK, WIDTH // 2),
                far=(3, 4, BLOCK, WIDTH // 2),
                x=(3, 4, BLOCK, WIDTH),
                y=(3, 4, BLOCK, WIDTH),
                z=(4, 3, BLOCK, WIDTH),
                line=(2, 4, BLOCK, WIDTH),
            )
        )
        scratch.update(
            vmem(F32, total=(2, BLOCK, WIDTH), squares=(8, WIDTH), tail_block=(BLOCK + 8, 128))
        )
        scratch.update(
            dma(send=(4, 11), recv=(4, 11), head_send=(7,), head_recv=(7,), tail_send=(7,), tail_recv=(7,))
        )
        scratch.update(credit=pltpu.SemaphoreType.REGULAR)
        extra = dict(collective_id=2, has_side_effects=True)
    return pallas(functools.partial(backward_kernel, plan), "backward", inputs, outputs, scratch, **extra)


PARAMS = ("patch", "triple", "output", "expand", "shrink", "vector", "head")
KINDS = ("w_", "m_", "s_")


def adam_update(master, moment, square, gradient, step_rate):
    moment_new = BETA_ONE * moment + (1.0 - BETA_ONE) * gradient
    square_new = BETA_TWO * square + (1.0 - BETA_TWO) * gradient * gradient
    moment_hat = moment_new / (1.0 - BETA_ONE**STEP_INDEX)
    square_hat = square_new / (1.0 - BETA_TWO**STEP_INDEX)
    master_new = master - step_rate * (
        moment_hat / (jnp.sqrt(square_hat) + ADAM_EPS) + DECAY * master
    )
    return (master_new, moment_new, square_new)


def head_matrices(ref, images):
    def take(first, count):
        devices = ref.shape[0] // HEAD_BLOCK
        pieces = [
            jnp.concatenate(
                [
                    ref[pl.ds(image * 14 + first + j, devices, stride=HEAD_BLOCK), :]
                    for j in range(count)
                ],
                1,
            )
            for image in range(images)
        ]
        return jnp.concatenate(pieces, 0).astype(BF)

    return take(0, 6), take(6, 8)


def update_kernel(images, names, *refs):
    r = SimpleNamespace(**dict(zip(names, refs)))
    named = dict(zip(names, refs))
    groups = [
        [(named[kind + name], named["vm_" + kind + name], named["to_" + kind + name]) for kind in KINDS]
        for name in PARAMS
    ]
    patch, triple, output, expand, shrink, vector, head = range(7)

    def moves(group, back):
        return [
            pltpu.make_async_copy(*((buf, out) if back else (src, buf)), r.sems.at[3 * group + k])
            for k, (src, buf, out) in enumerate(groups[group])
        ]

    order = (head, shrink, expand, triple, output, patch, vector)
    for group in order:
        start_all(moves(group, False))

    tile = jnp.sum(r.tails[:, BLOCK:, :], 0)
    features, d_logits = head_matrices(r.head_rows, images)
    r.features[...] = features
    r.d_logits[...] = d_logits
    alike = (dot(features, features, NT) + 1.0) * dot(d_logits, d_logits, NT)
    norm = jnp.sqrt(tile[0:1, 0:1] + jnp.sum(alike))
    clip = CLIP / jnp.maximum(norm, CLIP)
    line = lax.broadcasted_iota(jnp.int32, (8, 128), 0)
    r.scalars[...] = jnp.where(line == 0, norm, tile[1:2])

    def step(group, at, gradient, rate):
        bufs = [buf for _, buf, _ in groups[group]]
        new = adam_update(*[buf[at] for buf in bufs], gradient * clip, rate)
        for buf, value in zip(bufs, new):
            buf[at] = value

    def finish(group):
        start_all(moves(group, True))

    every = slice(None)
    wait_all(moves(head, False))

    @pl.loop(0, D // 128)
    def _(j):
        rows = pl.ds(pl.multiple_of(j * 128, 128), 128)
        gradient = dot(r.features[:, rows], r.d_logits[...], TN)
        step(head, (rows, every), gradient[:, :CLASSES], RATE_MATRIX)

    bias = jnp.sum(d_logits.astype(F32), 0, keepdims=True)[:, :CLASSES]
    step(head, (slice(D, D + 1), every), bias, RATE_MATRIX)
    r.bias_grad[...] = bias * clip
    finish(head)
    wait_all(moves(shrink, False))

    @pl.loop(0, LAYERS)
    def _(layer):
        unit = 3 * (LAYERS - 1 - layer)
        for k in range(4):
            gradient = r.owned[unit, k % 2, :, pl.ds(k // 2 * D, D)]
            step(shrink, (layer, pl.ds(k * HALF, HALF), every), gradient, RATE_MATRIX)

    finish(shrink)
    wait_all(moves(expand, False))

    @pl.loop(0, LAYERS)
    def _(layer):
        unit = 3 * (LAYERS - 1 - layer) + 1
        for k in range(2):
            step(expand, (layer, every, pl.ds(k * WIDTH, WIDTH)), r.owned[unit, k], RATE_MATRIX)

    finish(expand)
    wait_all(moves(triple, False))
    wait_all(moves(output, False))

    @pl.loop(0, LAYERS)
    def _(layer):
        unit = 3 * (LAYERS - 1 - layer) + 2
        step(triple, (layer, every, pl.ds(0, WIDTH)), r.owned[unit, 0], RATE_MATRIX)
        step(triple, (layer, every, pl.ds(WIDTH, D)), r.owned[unit, 1, :, pl.ds(0, D)], RATE_MATRIX)
        step(output, (layer, every, every), r.owned[unit, 1, :, pl.ds(D, D)], RATE_OUTPUT)

    finish(triple)
    finish(output)
    wait_all(moves(patch, False))
    for k in range(2):
        step(patch, (every, pl.ds(k * (D // 2), D // 2)), r.patch_grad[k], RATE_MATRIX)
    finish(patch)
    count = groups[vector][0][0].shape[0]
    for d in range(-(-count // 8)):
        for j in range(6):
            r.vector_grad[8 * d : 8 * d + 8, 128 * j : 128 * j + 128] = r.tails[d, 8 * j : 8 * j + 8, :]
    wait_all(moves(vector, False))
    step(vector, (every, every), r.vector_grad[:count], RATE_VECTOR)
    finish(vector)
    for group in order:
        wait_all(moves(group, True))


def update(plan, images, states, got):
    inputs, outputs, scratch = {}, {}, {}
    for name, state in zip(PARAMS, states):
        for kind, value in zip(KINDS, state):
            inputs[kind + name] = (value, ANY_SPEC)
            outputs["to_" + kind + name] = (value.shape, F32, ANY_SPEC)
            scratch["vm_" + kind + name] = pltpu.VMEM(value.shape, F32)
    inputs.update(
        given_in(
            VMEM_SPEC,
            owned=got.owned,
            patch_grad=got.patch,
            tails=got.vector_rows.reshape(plan.n, BLOCK + 8, 128),
            head_rows=got.head_rows.reshape(plan.n * HEAD_BLOCK, 128),
        )
    )
    outputs.update(scalars=((8, 128), F32, VMEM_SPEC), bias_grad=((1, CLASSES), F32, VMEM_SPEC))
    scratch.update(vmem(BF, features=(plan.n * images, D), d_logits=(plan.n * images, 1024)))
    scratch.update(vmem(F32, vector_grad=(VEC_ROWS, D)))
    scratch.update(dma(sems=(3 * len(PARAMS),)))
    new = pallas(functools.partial(update_kernel, images), "update", inputs, outputs, scratch)
    states = [[getattr(new, "to_" + kind + name) for kind in KINDS] for name in PARAMS]
    return new.scalars[0, 0], new.scalars[1, 0], states, new.bias_grad[0]


AXES = ("wide", "grp")


def update_whole(plan, images, states, got, done):
    full = got.full.reshape(UNITS + 1, 2, 16, BLOCK, WIDTH)
    layers = full[:UNITS].reshape(LAYERS, 3, 2, 16, BLOCK, WIDTH)[::-1]

    def scattered(whole):
        axis = whole.ndim - 2
        return lax.psum_scatter(whole, AXES, scatter_dimension=axis, tiled=True).astype(F32)

    def from_cols(part):
        joined = jnp.concatenate([part[..., 0, :, :, :], part[..., 1, :, :, :]], -1)
        return joined.reshape(part.shape[:-4] + (D, -1))

    shrink = layers[:, 0].reshape(LAYERS, 2, 16, BLOCK, 2, D).transpose(0, 2, 1, 4, 3, 5)
    joined = scattered(from_cols(layers[:, 2]))
    rows_all = lax.all_gather(done.head_block, AXES, axis=0)[:, : 14 * images]
    rows_all = rows_all.reshape(plan.n * images, 14 * 128).astype(BF)
    features, d_logits = rows_all[:, :D], rows_all[:, D : D + CLASSES]
    bias = jnp.sum(d_logits.astype(F32), 0)[None]
    split = [
        scattered(from_cols(full[UNITS, ..., : D // 2])),
        joined[:, :, : 3 * D],
        joined[:, :, 3 * D :],
        scattered(from_cols(layers[:, 1])),
        scattered(shrink.reshape(LAYERS, FF, D)),
    ]
    same = [
        lax.psum(got.vector_rows[: states[5][0].shape[0]], AXES),
        jnp.concatenate([dot(features, d_logits, TN), bias], 0),
    ]
    squares = lax.psum(sum(jnp.sum(g * g) for g in split), AXES) + sum(jnp.sum(g * g) for g in same)
    norm = jnp.sqrt(squares)
    clip = CLIP / jnp.maximum(norm, CLIP)
    rates = [RATE_MATRIX] * 2 + [RATE_OUTPUT] + [RATE_MATRIX] * 2 + [RATE_VECTOR, RATE_MATRIX]
    states = [
        adam_update(*state, gradient * clip, rate)
        for state, gradient, rate in zip(states, split + same, rates)
    ]
    return norm, lax.psum(done.tail[0, 0], AXES), states, bias[0] * clip


def per_device(plan, images, slot_mask, labels, *params):
    states = [params[3 * k : 3 * k + 3] for k in range(7)]
    patch, triple, output, expand, shrink, vector, head = (state[0] for state in states)
    count = images.shape[0]
    pad_rows = ((0, HEAD_ROWS - count), (0, 0))
    weights = slot_mask.astype(F32)
    args = dict(
        images=images,
        vectors=vector,
        head=head,
        labels=jnp.pad(labels[:, None], pad_rows),
        weights=jnp.pad(weights[:, None], pad_rows),
    )
    if plan.cube:
        shards = dict(patch=patch, triple=triple, output=output, expand=expand, shrink=shrink)
        done = forward(plan, shards, args, None, None)
    else:

        def whole(shard, shape):
            axis = shard.ndim - 2
            gathered = lax.all_gather(shard.astype(BF), AXES, axis=axis, tiled=True)
            return gathered.reshape(shard.shape[:axis] + shape)

        gathered = [
            whole(patch, cols_shape(D)),
            whole(jnp.concatenate([triple, output], 2), cols_shape(FF)),
            whole(expand, cols_shape(FF)),
            whole(shrink, ROWS_SHAPE),
        ]
        total = jnp.full((8, 128), lax.psum(jnp.sum(weights), AXES), F32)
        done = forward(plan, None, args, gathered, total)
    got = backward(plan, images, vector, done)
    if plan.cube:
        norm, loss, states, bias_grad = update(plan, count, states, got)
    else:
        norm, loss, states, bias_grad = update_whole(plan, count, states, got, done)
    return (
        loss,
        done.total[0, 0],
        norm,
        *(value for state in states for value in state),
        bias_grad,
    )


def solution(mesh):
    plan = Plan(mesh)
    rows = P(AXES, None)
    layers = P(None, AXES, None)
    in_specs = (P(AXES, None, None), P(AXES), P(AXES)) + (rows,) * 3 + (layers,) * 12 + (P(),) * 6
    out_specs = (P(),) * 3 + (rows,) * 3 + (layers,) * 12 + (P(),) * 7
    return jax.shard_map(
        functools.partial(per_device, plan),
        mesh=mesh,
        in_specs=in_specs,
        out_specs=out_specs,
        check_vma=False,
    )
```

time: 3630 us -> 502 us (0.14)
  waiting for transfers between devices: 2950 us -> 0 us
  Pallas kernels: 0 us -> 493 us
  matrix products: 287 us -> 0 us
  other arithmetic: 122 us -> 0.66 us
  local copies, waits for them, and re-layouts: 124 us -> 6.45 us
  blocking collectives: 93.5 us -> 0 us
    reduce_scatter x26 -> x0, waiting for transfers between devices: 1970 us -> none  [the longest x6 581 us: per_device(): lax.psum_scatter(matrices[2].astype(jnp.bfloat16), 'wide', scatter_dimens...]
    all_gather x16 -> x0, waiting for transfers between devices: 764 us -> none  [the longest x3 234 us: layer_copy(): lax.all_gather(rows_expand[layer_at], 'wide', axis=0, tiled=True)]
    pallas_call x0 -> x3, Pallas kernels: none -> 493 us  [pallas(): pl.pallas_call(functools.partial(kernel, names), out_shape=[jax.ShapeDtyp...]
    dot_general x116 -> x0, matrix products: 287 us -> none  [the longest x6 57.1 us: layer_forward(): jnp.einsum('bsd,df->bsf', normed_two, w_expand, preferred_element_type=jn...]
    psum x1 -> x0, waiting for transfers between devices: 138 us -> none  [per_device(): lax.psum((head_sum, vector_sum, loss_running), ('wide', 'grp'))]
    psum x2 -> x0, blocking collectives: 79.7 us -> none  [the longest x1 40.1 us: per_device(): lax.psum((head_sum, vector_sum, loss_running), ('wide', 'grp'))]
    unnamed x49 -> x0, waiting for transfers between devices: 79.1 us -> none
    unnamed x711 -> x1, local copies, waits for them, and re-layouts: 66 us -> 1.95 us
  transfers between devices with their start and end apart: 46 -> 0, of which waited for: 42 -> 0; matrix products, arithmetic and copies ran while one was open for 9% -> 0% of each run, Pallas kernels for 0% -> 0%
where the time goes in v1:
time: 502 us; the launch traced here: 501 us
  Pallas kernels  493 us (98%)
  local copies, waits for them, and re-layouts  6.45 us (1%)
    pallas_call x3, Pallas kernels, pallas(): pl.pallas_call(functools.partial(kernel, names), out_shape=[jax.ShapeDtyp...  493 us

profile of v1, /device:TPU:0, one launch (start us, length us, event | category | flops | bytes accessed | tf_op | source)
XLA Modules:
  0.0 500.9 jit_solution(5939906517365220352)
XLA Ops:
  0.7 0.7 convert_bitcast_fusion
  1.3 0.1 copy.50
  1.4 0.7 copy.49
  2.2 0.6 pad.8.refs_3_
  2.8 0.6 pad.9.refs_4_
  3.4 2.0 copy.52.refs_0_
  5.3 225.9 %forward.1 = (bf16[4,2,2,48,768]{4,3,2,1,0:T(8,128)(2,1)}, bf16[3,4,2,2,48,3072]{5,4,3,2,1,0:T(8,128)(2,1)}, bf16[3,4,2,2,48,3072]{5,4,3,2,1,0:T(8,128)(2,1)}, b...) custom-call(bf16[2,196,768]{2,1,0:T(8,128)(2,1)} %copy.52.refs_0_, ...), custom_call_target="tpu_custom_call" | custom-call | tf_op jit(solution)/shard_map/forward/pallas_call | solution.py:554
  231.2 1.2 slice.10
  232.4 249.8 %backward.1 = (f32[9,2,24,1536]{3,2,1,0:T(8,128)}, f32[2,24,384]{2,1,0:T(8,128)}, f32[4,2,2,2,56,128]{5,4,3,2,1,0:T(8,128)}, f32[4,2,2,2,32,128]{5,4,3,2,1,0:T(8,128)}) custom-call(bf16[2,196,768]{2,1,0:T(8,128)(2,1)} %copy.52.refs_0_, f32[213,768]{1,0:T(8,128)} %refs_15_.1, f32[8,768]{1,0:T(8,128)} %get-tuple-element.68.refs_2_, ...), custom_call_target="tpu_custom_call" | custom-call | tf_op jit(solution)/shard_map/backward/pallas_call | solution.py:554
  482.2 17.4 %update.1 = (f32[24,768]{1,0:T(8,128)}, f32[24,768]{1,0:T(8,128)}, f32[24,768]{1,0:T(8,128)}, f32[3,24,2304]{2,1,0:T(8,128)}, f32[3,24,2304]{2,1,0:T(8,128)}, /*...) custom-call(f32[24,768]{1,0:T(8,128)} %refs_0_.3, ...), custom_call_target="tpu_custom_call" | custom-call | tf_op jit(solution)/shard_map/update/pallas_call | solution.py:554
  499.6 1.3 fusion

commit v2 on v1

--- a/solution.py
+++ b/solution.py
@@ -105,16 +105,49 @@
 ROWS_SHAPE = CHIPS + (2, BLOCK_FF, D)
 
 
+def other_part(width):
+    return width // 6 // 128 * 128
+
+
 def cut_of(columns):
-    return (columns // 2 + 127) // 128 * 128
+    return columns // 2 // 128 * 128
+
+
+def over_links(plan):
+    z, x, y, c = plan.where()
+
+    def at(z, x, y, c):
+        return (z * 2 + x, y * 2 + c)
+
+    return SimpleNamespace(
+        z1=at(jnp.bitwise_xor(z, 1), x, y, c),
+        z3=at(jnp.bitwise_xor(z, 3), x, y, c),
+        x=at(z, 1 - x, y, c),
+        y=at(z, x, 1 - y, c),
+        core=at(z, x, y, 1 - c),
+    )
+
+
+def remote(src, dst, send, recv, to):
+    return pltpu.make_async_remote_copy(
+        src_ref=src,
+        dst_ref=dst,
+        send_sem=send,
+        recv_sem=recv,
+        device_id=to,
+        device_id_type=pl.DeviceIdType.MESH,
+    )
 
 
 class Gather:
     def __init__(self, plan, by_cols, block, whole, send, recv):
         self.z, self.x, self.y, self.c = plan.where()
+        self.to = over_links(plan)
         self.by_cols, self.block, self.whole = by_cols, block, whole
         self.send, self.recv = send, recv
         self.width = block.shape[-1]
+        self.other = other_part(self.width)
+        self.most = self.width - self.other
 
     def region(self, z, x, y, start, width):
         if self.by_cols:
@@ -122,68 +155,109 @@
             return self.whole.at[z, x, y, :, pl.ds(first, width)]
         return self.whole.at[z, x, y, self.c, :, pl.ds(start, width)]
 
+    def part(self, start, width):
+        return self.block.at[:, pl.ds(start, width)]
+
     def copy(self, at):
-        z, x, y, c = self.z, self.x, self.y, self.c
-        width, cut, line = self.width, cut_of(self.width), slice(None)
-        if at < 3:
-            src, dst = self.block, self.region(z, x, y, 0, width)
-            to = (jnp.bitwise_xor(z, at + 1) * 2 + x, y * 2 + c)
+        z, x, y, to = self.z, self.x, self.y, self.to
+        z1, z3, line = jnp.bitwise_xor(z, 1), jnp.bitwise_xor(z, 3), slice(None)
+        most, other, region = self.most, self.other, self.region
+        cut, cut_other = cut_of(most), most + max(cut_of(other), 128)
+        landed = at
+        if at in (0, 1):
+            src, dst = self.part(0, most), region(z, x, y, 0, most)
+            device = (to.z1, to.z3)[at]
+        elif at in (8, 9):
+            src, dst = self.part(most, other), region(z, x, y, most, other)
+            device = (to.x, to.y)[at - 8]
         else:
-            src = dst = (
-                lambda: self.region(line, x, y, 0, width),
-                lambda: self.region(line, x, y, 0, width),
-                lambda: self.region(line, x, 1 - y, 0, cut),
-                lambda: self.region(line, 1 - x, y, cut, width - cut),
-                lambda: self.region(line, x, y, 0, width),
-                lambda: self.region(line, 1 - x, y, 0, width),
-                lambda: self.region(line, x, 1 - y, 0, width),
-                lambda: self.region(line, 1 - x, 1 - y, 0, cut),
-                lambda: self.region(line, 1 - x, 1 - y, cut, width - cut),
-            )[at - 3]()
-            over_x, over_y, over_c = (z * 2 + 1 - x, y * 2 + c), (z * 2 + x, (1 - y) * 2 + c), (z * 2 + x, y * 2 + 1 - c)
-            to = (over_x, over_y, over_x, over_y, over_c, over_c, over_c, over_c, over_c)[at - 3]
-        return pltpu.make_async_remote_copy(
-            src_ref=src,
-            dst_ref=dst,
-            send_sem=self.send.at[at],
-            recv_sem=self.recv.at[at],
-            device_id=to,
-            device_id_type=pl.DeviceIdType.MESH,
-        )
+            src, device = {
+                2: lambda: (region(z3, x, y, 0, most), to.z1),
+                3: lambda: (region(z1, x, y, 0, most), to.z3),
+                4: lambda: (region(line, x, y, 0, most), to.x),
+                5: lambda: (region(line, x, y, 0, most), to.y),
+                6: lambda: (region(line, x, 1 - y, 0, cut), to.x),
+                7: lambda: (region(line, 1 - x, y, cut, most - cut), to.y),
+                10: lambda: (region(z, x, 1 - y, most, cut_other - most), to.x),
+                11: lambda: (region(z, 1 - x, y, cut_other, self.width - cut_other), to.y),
+                12: lambda: (region(z, line, line, most, other), to.z1),
+                13: lambda: (region(z, line, line, most, other), to.z3),
+                14: lambda: (region(z3, line, line, most, other), to.z1),
+                15: lambda: (region(z1, line, line, most, other), to.z3),
+                16: lambda: (region(line, x, y, 0, most), to.core),
+                17: lambda: (region(line, 1 - x, y, 0, most), to.core),
+                18: lambda: (region(line, x, 1 - y, 0, most), to.core),
+                19: lambda: (region(line, 1 - x, 1 - y, 0, cut), to.core),
+                20: lambda: (region(line, 1 - x, 1 - y, cut, most - cut), to.core),
+                21: lambda: (region(line, line, line, most, other), to.core),
+            }[at]()
+            dst = src
+            if at in (3, 15):
+                landed = at - 1
+        return remote(src, dst, self.send.at[at], self.recv.at[landed], device)
+
+    def exists(self, at):
+        if at in (8, 9, 10, 12, 13, 14, 15, 21):
+            return self.other > 0
+        return at != 11 or self.other > 128
 
     def keep(self):
         here = self.region(self.z, self.x, self.y, 0, self.width)
-        return pltpu.make_async_copy(self.block, here, self.send.at[12])
+        return pltpu.make_async_copy(self.block, here, self.send.at[22])
 
     def start(self, *which):
         for at in which:
-            self.copy(at).start()
+            if self.exists(at):
+                self.copy(at).start()
 
     def arrived(self, *which):
         for at in which:
-            self.copy(at).wait_recv()
+            if self.exists(at):
+                self.copy(at).wait_recv()
+
+    def in_middle(self, do):
+        pl.when((self.z == 1) | (self.z == 2))(do)
 
     def stage0(self):
-        self.start(0, 1, 2)
+        self.start(0, 1, 8, 9)
         self.keep().start()
 
     def stage1(self):
-        self.arrived(0, 1, 2)
+        self.arrived(0, 1)
+        self.in_middle(lambda: self.start(2, 3))
+        self.arrived(8, 9)
+        self.start(10, 11)
         self.keep().wait()
-        self.start(3, 4, 7)
 
     def stage2(self):
-        self.arrived(3, 4)
-        self.start(5, 6, 8, 9)
+        self.arrived(2)
+        self.start(4, 5, 16)
+        self.arrived(10, 11)
+        self.start(12, 13)
 
     def stage3(self):
-        self.arrived(5, 6)
-        self.start(10, 11)
+        self.arrived(4, 5)
+        self.start(6, 7, 17, 18)
+        self.arrived(12, 13)
+        self.in_middle(lambda: self.start(14, 15))
+
+    def stage4(self):
+        self.arrived(6, 7)
+        self.start(19, 20)
+        self.arrived(14)
+        self.start(21)
 
     def finish(self):
-        self.arrived(7, 8, 9, 10, 11)
-        for at in range(12):
-            self.copy(at).wait_send()
+        self.arrived(16, 17, 18, 19, 20, 21)
+        passed = (2, 3, 14, 15)
+
+        def sent(which):
+            for at in which:
+                if self.exists(at):
+                    self.copy(at).wait_send()
+
+        sent([at for at in range(22) if at not in passed])
+        self.in_middle(lambda: sent(passed))
 
 
 def cube_barrier(plan):
@@ -424,17 +498,23 @@
         return [pltpu.make_async_copy(held[k], kept[k].at[layer], r.saves.at[k]) for k in which]
 
     if cube:
-        unit(patch, 0).stage0()
+        first = [unit(patch, 0), unit(joined, 0), unit(expand, 0), unit(shrink, 0), unit(joined, 1)]
+        first[0].stage0()
         counting.stage0()
-        unit(joined, 0).stage0()
-        unit(patch, 0).stage1()
-        unit(expand, 0).stage0()
-        unit(joined, 0).stage1()
-        unit(patch, 0).stage2()
-        unit(shrink, 0).stage0()
-        unit(expand, 0).stage1()
-        unit(joined, 0).stage2()
-        unit(patch, 0).stage3()
+        first[1].stage0()
+        first[0].stage1()
+        first[2].stage0()
+        first[1].stage1()
+        first[0].stage2()
+        first[3].stage0()
+        first[2].stage1()
+        first[1].stage2()
+        first[0].stage3()
+        first[4].stage0()
+        first[3].stage1()
+        first[2].stage2()
+        first[1].stage3()
+        first[0].stage4()
     ready(patch, 0).wait()
     for image in range(images):
         at = image * PAD
@@ -451,10 +531,14 @@
         more = layer < LAYERS - 1
         base = S + 2 + 4 * layer
         if cube:
-            pl.when(more)(lambda: unit(joined, layer + 1).stage0())
-            unit(shrink, layer).stage1()
-            unit(expand, layer).stage2()
-            unit(joined, layer).stage3()
+            @pl.when(more)
+            def _():
+                unit(expand, layer + 1).stage0()
+                unit(joined, layer + 1).stage1()
+
+            unit(shrink, layer).stage2()
+            unit(expand, layer).stage3()
+            unit(joined, layer).stage4()
         start_all(saves(layer, h_))
 
         @pl.when(layer > 0)
@@ -471,8 +555,7 @@
 
         start_all(saves(layer, a_, t_))
 
-        @pl.loop(0, images * (HEADS // 2))
-        def _(step):
+        def heads(step):
             image, pair = step // (HEADS // 2), step % (HEADS // 2)
             rows = pl.ds(pl.multiple_of(image * PAD, 16), PAD)
             lanes = [pl.ds(pl.multiple_of(pair * 128 + part * D, 128), 128) for part in range(3)]
@@ -490,17 +573,22 @@
                 outs.append(dot(p, v, TN))
             r.o[rows, lanes[0]] = jnp.where(low_lane, outs[0], outs[1]).astype(BF)
 
+        half = images * (HEADS // 2) // 2
+        pl.loop(0, half)(heads)
+        if cube:
+            @pl.when(more)
+            def _():
+                unit(shrink, layer + 1).stage0()
+                unit(expand, layer + 1).stage1()
+                unit(joined, layer + 1).stage2()
+
+        pl.loop(half, 2 * half)(heads)
         start_all(saves(layer, o_, p_))
         r.h1[...] = r.h[...] + dot(r.o[...], weight(r.joined_w, 3 * D, D))
         start_all(saves(layer, h1_))
         if cube:
-            @pl.when(more)
-            def _():
-                unit(expand, layer + 1).stage0()
-                unit(joined, layer + 1).stage1()
-
-            unit(shrink, layer).stage2()
-            unit(expand, layer).stage3()
+            unit(shrink, layer).stage3()
+            unit(expand, layer).stage4()
             pl.when(layer == 0)(counting.stage1)
             pl.when(layer == 1)(counting.stage3)
         r.m[...] = normalize(r.h1[...], row(r.vectors, base + 2), row(r.vectors, base + 3)).astype(BF)
@@ -524,13 +612,15 @@
 
         start_all(saves(layer, z_, slope_))
         if cube:
+            pl.when(layer < LAYERS - 2)(lambda: unit(joined, layer + 2).stage0())
+
             @pl.when(more)
             def _():
-                unit(shrink, layer + 1).stage0()
-                unit(expand, layer + 1).stage1()
-                unit(joined, layer + 1).stage2()
-
-            unit(shrink, layer).stage3()
+                unit(shrink, layer + 1).stage1()
+                unit(expand, layer + 1).stage2()
+                unit(joined, layer + 1).stage3()
+
+            unit(shrink, layer).stage4()
             pl.when(layer == 0)(counting.stage2)
             pl.when(layer == 1)(counting.finish)
         ready(shrink, layer).wait()
@@ -633,7 +723,7 @@
             )
         )
         scratch.update(
-            dma(send=(10, 13), recv=(10, 12), share_send=(3,), share_recv=(3,), count_send=(7,), count_recv=(7,))
+            dma(send=(10, 23), recv=(10, 22), share_send=(3,), share_recv=(3,), count_send=(7,), count_recv=(7,))
         )
         extra = dict(collective_id=1, has_side_effects=True)
     got = pallas(functools.partial(forward_kernel, plan), "forward", inputs, outputs, scratch, **extra)
@@ -689,159 +779,230 @@
     def __init__(self, plan, bufs, unit, width=WIDTH):
         self.plan, self.bufs, self.unit, self.width = plan, bufs, unit, width
         self.z, self.x, self.y, self.c = plan.where()
-        self.cut = width // 2
+        self.to = over_links(plan)
+        self.other = other_part(width) if width == WIDTH else 0
+        self.most = width - self.other
+        self.cut, self.cut_other = cut_of(self.most), cut_of(self.other)
         self.slot, self.three, self.two = unit % 4, unit % 3, unit % 2
 
     def copy(self, at):
-        z, x, y, c = self.z, self.x, self.y, self.c
-        bufs, slot, three, width, cut = self.bufs, self.slot, self.three, self.width, self.cut
+        b, slot, three, to, c = self.bufs, self.slot, self.three, self.to, self.c
+        most, cut, cut_other = self.most, self.cut, self.cut_other
         line = slice(None)
-        full, left, right = pl.ds(0, width), pl.ds(0, cut), pl.ds(cut, width - cut)
-        over_x, over_y, over_c = (
-            (z * 2 + 1 - x, y * 2 + c),
-            (z * 2 + x, (1 - y) * 2 + c),
-            (z * 2 + x, y * 2 + 1 - c),
-        )
-        unit = bufs.unit
-        if at == 0:
-            src, dst, to = unit.at[SEND, :, :, :, full], bufs.core.at[:, :, :, full], over_c
-        elif at == 1:
-            src, dst, to = unit.at[slot, :, 3, :, left], bufs.near.at[three, :, :, left], over_x
-        elif at == 2:
-            src, dst, to = unit.at[slot, :, 3, :, right], bufs.far.at[three, :, :, left], over_y
-        elif at == 3:
-            src, dst, to = unit.at[slot, :, 1, :, full], bufs.y.at[three, :, :, full], over_y
-        elif at == 4:
-            src, dst, to = unit.at[slot, :, 2, :, full], bufs.x.at[three, :, :, full], over_x
-        elif at < 8:
-            k = at - 4
-            src = bufs.line.at[self.two, k, :, full]
-            dst = bufs.z.at[slot, k - 1, :, full]
-            to = (jnp.bitwise_xor(z, k) * 2 + x, y * 2 + c)
+        full, main = pl.ds(0, self.width), pl.ds(0, most)
+        left, right, low = pl.ds(0, cut), pl.ds(cut, most - cut), pl.ds(0, most - cut)
+        other = pl.ds(most, self.other)
+        own = b.unit.at[slot]
+        if at == 17:
+            rows = pl.ds(pl.multiple_of((1 - c) * HALF, 8), HALF)
+            if self.width == WIDTH:
+                src, dst = b.total.at[self.two, rows], b.owned.at[self.unit, c]
+            else:
+                src, dst = b.total.at[self.two, rows, pl.ds(0, D // 2)], b.patch.at[c]
+            device = to.core
         else:
-            rows = pl.ds(pl.multiple_of((1 - c) * HALF, 8), HALF)
-            if width == WIDTH:
-                src, dst = bufs.total.at[self.two, rows], bufs.owned.at[self.unit, c]
+            src, dst, device = {
+                0: lambda: (b.unit.at[SEND, :, :, :, full], b.core.at[:, :, :, full], to.core),
+                1: lambda: (own.at[:, 3, :, left], b.near.at[three, :, :, left], to.x),
+                2: lambda: (own.at[:, 3, :, right], b.far.at[three, :, :, low], to.y),
+                3: lambda: (own.at[:, 1, :, main], b.y.at[three, :, :, main], to.y),
+                4: lambda: (own.at[:, 2, :, main], b.x.at[three, :, :, main], to.x),
+                5: lambda: (b.line.at[three, 2, :, main], b.main_two.at[three, 0, :, main], to.z1),
+                6: lambda: (b.line.at[three, 2, :, main], b.main_two.at[three, 1, :, main], to.z3),
+                7: lambda: (b.line.at[three, 1, :, main], b.main_one.at[slot, 0, :, main], to.z1),
+                8: lambda: (b.line.at[three, 3, :, main], b.main_one.at[slot, 1, :, main], to.z3),
+                9: lambda: (own.at[2, :, :, other], b.other_two.at[three, 0], to.z1),
+                10: lambda: (own.at[2, :, :, other], b.other_two.at[three, 1], to.z3),
+                11: lambda: (own.at[1, :, :, other], b.other_one.at[slot, 0], to.z1),
+                12: lambda: (own.at[3, :, :, other], b.other_one.at[slot, 1], to.z3),
+                13: lambda: (b.plane.at[three, 3, :, pl.ds(0, cut_other)], b.other_near.at[three], to.x),
+                14: lambda: (b.plane.at[three, 3, :, pl.ds(cut_other, cut_other)], b.other_far.at[three], to.y),
+                15: lambda: (b.plane.at[three, 1], b.other_y.at[three], to.y),
+                16: lambda: (b.plane.at[three, 2], b.other_x.at[three], to.x),
+            }[at]()
+        return remote(src, dst, b.send.at[slot, at], b.recv.at[slot, at], device)
+
+    def own(self, by_rows):
+        b, c = self.bufs, self.c
+        total = b.total.at[self.two]
+        if by_rows:
+            moves = [(total.at[pl.ds(k * HALF, HALF)], b.owned.at[self.unit, k]) for k in range(2)]
+        else:
+            rows = pl.ds(pl.multiple_of(c * HALF, 8), HALF)
+            if self.width == WIDTH:
+                moves = [(total.at[rows], b.owned.at[self.unit, c])]
             else:
-                cols = pl.ds(0, D // 2)
-                src, dst = bufs.total.at[self.two, rows, cols], bufs.patch.at[c]
-            to = over_c
-        return pltpu.make_async_remote_copy(
-            src_ref=src,
-            dst_ref=dst,
-            send_sem=bufs.send.at[slot, at],
-            recv_sem=bufs.recv.at[slot, at],
-            device_id=to,
-            device_id_type=pl.DeviceIdType.MESH,
-        )
-
-    def own(self, by_rows):
-        bufs, c = self.bufs, self.c
-        sem = bufs.send
-        if by_rows:
-            return [
-                pltpu.make_async_copy(
-                    bufs.total.at[self.two, pl.ds(part * HALF, HALF)],
-                    bufs.owned.at[self.unit, part],
-                    sem.at[self.slot, 9 + part],
-                )
-                for part in range(2)
-            ]
-        rows = pl.ds(pl.multiple_of(c * HALF, 8), HALF)
-        if self.width == WIDTH:
-            src, dst = bufs.total.at[self.two, rows], bufs.owned.at[self.unit, c]
-        else:
-            src, dst = bufs.total.at[self.two, rows, pl.ds(0, D // 2)], bufs.patch.at[c]
-        return [pltpu.make_async_copy(src, dst, sem.at[self.slot, 9])]
-
-    def credit(self):
-        return self.bufs.credit
+                moves = [(total.at[rows, pl.ds(0, D // 2)], b.patch.at[c])]
+        return [
+            pltpu.make_async_copy(src, dst, b.send.at[self.slot, 18 + k])
+            for k, (src, dst) in enumerate(moves)
+        ]
+
+    def start(self, *which):
+        for at in which:
+            self.copy(at).start()
+
+    def arrived(self, *which):
+        for at in which:
+            self.copy(at).wait_recv()
+
+    def sent(self, *which):
+        for at in which:
+            self.copy(at).wait_send()
+
+    def by_place(self, middle, end):
+        inside = (self.z == 1) | (self.z == 2)
+        if middle:
+            pl.when(inside)(middle)
+        if end:
+            pl.when(jnp.logical_not(inside))(end)
 
     def stage0(self):
         @pl.when(self.unit > 0)
         def _():
-            pl.semaphore_wait(self.credit(), 1)
-
-        self.copy(0).start()
+            pl.semaphore_wait(self.bufs.credit, 1)
+
+        self.start(0)
 
     def stage1(self):
         unit, core, slot = self.bufs.unit, self.bufs.core, self.slot
         cols = pl.ds(0, self.width)
-        self.copy(0).wait_recv()
+        self.arrived(0)
 
         def add(z, chip):
             both = unit[slot, z, chip, :, cols].astype(F32) + core[z, chip, :, cols].astype(F32)
             unit[slot, z, chip, :, cols] = both.astype(BF)
 
         pl.loop(0, 4)(lambda z: add(z, 3))
-        self.copy(1).start()
-        self.copy(2).start()
+        self.start(1, 2)
         pl.loop(0, 12)(lambda i: add(i // 3, i % 3))
+        if self.other:
+            self.by_place(lambda: self.start(10), lambda: self.start(9))
 
         @pl.when(self.unit < UNITS)
         def _():
-            z, x, y, c = self.z, self.x, self.y, self.c
             pl.semaphore_signal(
-                self.credit(),
-                inc=1,
-                device_id=(z * 2 + x, y * 2 + 1 - c),
-                device_id_type=pl.DeviceIdType.MESH,
+                self.bufs.credit, inc=1, device_id=self.to.core, device_id_type=pl.DeviceIdType.MESH
             )
 
     def stage2(self):
-        unit, slot, cut = self.bufs.unit, self.slot, self.cut
-        left, right = pl.ds(0, cut), pl.ds(cut, self.width - cut)
-        self.copy(1).wait_recv()
-        self.copy(2).wait_recv()
+        b, slot, three, most, cut = self.bufs, self.slot, self.three, self.most, self.cut
+        unit = b.unit
+        left, right, low = pl.ds(0, cut), pl.ds(cut, most - cut), pl.ds(0, most - cut)
+        self.arrived(1, 2)
 
         @pl.loop(0, 4)
         def _(z):
-            for chip, cols, landed in ((1, left, self.bufs.near), (2, right, self.bufs.far)):
-                got = landed[self.three, z, :, left].astype(F32)
-                unit[slot, z, chip, :, cols] = (unit[slot, z, chip, :, cols].astype(F32) + got).astype(BF)
-
-        self.copy(3).start()
-        self.copy(4).start()
-        self.copy(1).wait_send()
-        self.copy(2).wait_send()
+            got = b.near[three, z, :, left].astype(F32)
+            unit[slot, z, 1, :, left] = (unit[slot, z, 1, :, left].astype(F32) + got).astype(BF)
+            got = b.far[three, z, :, low].astype(F32)
+            unit[slot, z, 2, :, right] = (unit[slot, z, 2, :, right].astype(F32) + got).astype(BF)
+
+        self.start(3, 4)
+        self.sent(1, 2)
+        if not self.other:
+            return
+        other = pl.ds(most, self.other)
+
+        def pass_on():
+            self.arrived(9, 10)
+            for z, k in ((3, 0), (1, 1)):
+                for chip in range(4):
+                    got = b.other_two[three, k, chip].astype(F32)
+                    unit[slot, z, chip, :, other] = (
+                        unit[slot, z, chip, :, other].astype(F32) + got
+                    ).astype(BF)
+
+        self.by_place(pass_on, None)
+        self.start(11, 12)
 
     def stage3(self):
-        bufs, cols = self.bufs, pl.ds(0, self.width)
-        self.copy(3).wait_recv()
-        self.copy(4).wait_recv()
+        b, slot, three, main = self.bufs, self.slot, self.three, pl.ds(0, self.most)
+        self.arrived(3, 4)
 
         @pl.loop(0, 4)
         def _(z):
-            bufs.line[self.two, z, :, cols] = (
-                bufs.unit[self.slot, z, 0, :, cols].astype(F32)
-                + bufs.y[self.three, z, :, cols].astype(F32)
-                + bufs.x[self.three, z, :, cols].astype(F32)
+            b.line[three, z, :, main] = (
+                b.unit[slot, z, 0, :, main].astype(F32)
+                + b.y[three, z, :, main].astype(F32)
+                + b.x[three, z, :, main].astype(F32)
             ).astype(BF)
 
-        for at in (5, 6, 7):
-            self.copy(at).start()
-        self.copy(3).wait_send()
-        self.copy(4).wait_send()
-
-    def stage4(self, by_rows):
-        bufs, cols = self.bufs, pl.ds(0, self.width)
-        for at in (5, 6, 7):
-            self.copy(at).wait_recv()
-        total = bufs.line[self.two, 0, :, cols].astype(F32)
-        for k in range(3):
-            total = total + bufs.z[self.slot, k, :, cols].astype(F32)
-        bufs.total[self.two, :, cols] = total
-        bufs.squares[0:1, cols] += jnp.sum(total * total, 0, keepdims=True)
+        self.by_place(lambda: self.start(6), lambda: self.start(5))
+        self.sent(3, 4)
+        if not self.other:
+            return
+        self.arrived(11, 12)
+        for chip in range(4):
+            b.plane[three, chip] = (
+                b.unit[slot, 0, chip, :, pl.ds(self.most, self.other)].astype(F32)
+                + b.other_one[slot, 0, chip].astype(F32)
+                + b.other_one[slot, 1, chip].astype(F32)
+            ).astype(BF)
+        self.start(13, 14)
+        self.by_place(lambda: self.sent(10), lambda: self.sent(9))
+        self.sent(11, 12)
+
+    def stage4(self):
+        b, three, main = self.bufs, self.three, pl.ds(0, self.most)
+
+        def pass_on():
+            self.arrived(5, 6)
+            for z, k in ((3, 0), (1, 1)):
+                got = b.main_two[three, k, :, main].astype(F32)
+                b.line[three, z, :, main] = (b.line[three, z, :, main].astype(F32) + got).astype(BF)
+
+        self.by_place(pass_on, None)
+        self.start(7, 8)
+        if not self.other:
+            return
+        self.arrived(13, 14)
+        half = self.cut_other
+        for chip, cols, got in (
+            (1, pl.ds(0, half), b.other_near),
+            (2, pl.ds(half, half), b.other_far),
+        ):
+            both = b.plane[three, chip, :, cols].astype(F32) + got[three].astype(F32)
+            b.plane[three, chip, :, cols] = both.astype(BF)
+        self.start(15, 16)
+        self.sent(13, 14)
+
+    def stage5(self, by_rows):
+        b, slot, three, two = self.bufs, self.slot, self.three, self.two
+        main = pl.ds(0, self.most)
+        self.arrived(7, 8)
+        total = b.line[three, 0, :, main].astype(F32)
+        for k in range(2):
+            total = total + b.main_one[slot, k, :, main].astype(F32)
+        b.total[two, :, main] = total
+        b.squares[0:1, main] += jnp.sum(total * total, 0, keepdims=True)
+        if self.other:
+            self.arrived(15, 16)
+            other = pl.ds(self.most, self.other)
+            total = (
+                b.plane[three, 0].astype(F32)
+                + b.other_y[three].astype(F32)
+                + b.other_x[three].astype(F32)
+            )
+            b.total[two, :, other] = total
+            b.squares[0:1, other] += jnp.sum(total * total, 0, keepdims=True)
         if not by_rows:
-            self.copy(8).start()
+            self.start(17)
         start_all(self.own(by_rows))
-        for at in (5, 6, 7):
-            self.copy(at).wait_send()
-
-    def stage5(self, by_rows):
+        self.by_place(lambda: self.sent(6), lambda: self.sent(5))
+        self.sent(7, 8)
+        if self.other:
+            self.sent(15, 16)
+
+    def stage6(self, by_rows):
         if not by_rows:
-            self.copy(8).wait()
+            self.copy(17).wait()
         wait_all(self.own(by_rows))
+
+
+POINTS = 4
+ENTRY = (0, 1, 3)
+STAGE_ORDER = (1, 0, 2, 3, 4, 6, 5)
 
 
 def backward_kernel(plan, names, *refs):
@@ -888,32 +1049,55 @@
     r.vectors[FINAL : FINAL + 2] = r.tail_in[1:3]
     first_g.wait()
 
-    def tick(it, kind):
-        unit = 3 * it + kind
+    def run(unit, stage, by_rows, width=WIDTH):
+        unit = Reduce(plan, r, unit, width)
+        (
+            unit.stage0,
+            unit.stage1,
+            unit.stage2,
+            unit.stage3,
+            unit.stage4,
+            lambda: unit.stage5(by_rows),
+            lambda: unit.stage6(by_rows),
+        )[stage]()
+
+    def point(it, at):
         if not cube:
-            copies = [
-                pltpu.make_async_copy(r.unit.at[(unit % 4, SEND)[i]], r.full.at[unit, i], r.loads.at[joined_ + 1 + i])
-                for i in range(2)
-            ]
-            start_all(copies)
-            wait_all(copies)
+            for kind in range(3):
+                if ENTRY[kind] == at:
+                    unit = 3 * it + kind
+                    copies = [
+                        pltpu.make_async_copy(
+                            r.unit.at[(unit % 4, SEND)[i]],
+                            r.full.at[unit, i],
+                            r.loads.at[joined_ + 1 + i],
+                        )
+                        for i in range(2)
+                    ]
+                    start_all(copies)
+                    wait_all(copies)
             return
-
-        def when(back, do):
-            if kind >= back:
-                do()
-            else:
-                pl.when(unit >= back)(do)
-
-        def by_rows(back):
-            return (kind - back) % 3 == 0
-
-        when(1, lambda: Reduce(plan, r, unit - 1).stage1())
-        Reduce(plan, r, unit).stage0()
-        when(2, lambda: Reduce(plan, r, unit - 2).stage2())
-        when(3, lambda: Reduce(plan, r, unit - 3).stage3())
-        when(5, lambda: Reduce(plan, r, unit - 5).stage5(by_rows(5)))
-        when(4, lambda: Reduce(plan, r, unit - 4).stage4(by_rows(4)))
+        for stage in STAGE_ORDER:
+            for kind in range(3):
+                past, phase = divmod(ENTRY[kind] + stage, POINTS)
+                if phase != at:
+                    continue
+                unit = 3 * (it - past) + kind
+                if past:
+                    pl.when(it >= past)(functools.partial(run, unit, stage, kind == 0))
+                else:
+                    run(unit, stage, kind == 0)
+
+    def drain():
+        at = 0
+        while at <= 5:
+            for stage in STAGE_ORDER:
+                for past, kind in ((2, 0), (2, 1), (2, 2), (1, 0), (1, 1), (1, 2)):
+                    if POINTS * past + at - ENTRY[kind] == stage:
+                        run(jnp.int32(UNITS - 3 * past + kind), stage, kind == 0)
+                if at == stage:
+                    run(jnp.int32(UNITS), stage, False, TAIL)
+            at += 1
 
     def sent(unit):
         if cube:
@@ -937,7 +1121,7 @@
             cols = pl.ds(pl.multiple_of(j * (D // 2), 128), D // 2)
             store_rows(plan, r.unit, slot, j, dot(r.vm_z[:, cols], r.gr[...], TN))
 
-        tick(it, 0)
+        point(it, 0)
         if cube:
             pl.when(it == 0)(head_rows.stage1)
             pl.when(it == 1)(head_rows.finish)
@@ -957,7 +1141,7 @@
 
         start(layer, joined_)
         pl.when(below)(lambda: start(layer - 1, shrink_, slope_, m_))
-        tick(it, 1)
+        point(it, 1)
         if cube:
             pl.when(it == 0)(head_rows.stage2)
         d_h1, d_gain, d_shift = normalize_back(r.vm_h1[...], row(r.params, base + 2), r.g1[...])
@@ -975,8 +1159,7 @@
         r.do[...] = dot(r.gr[...], weight(r.expand_w, 3 * D, D), NT).astype(BF)
         wait(layer, t_, p_, a_, h_)
 
-        @pl.loop(0, images * (HEADS // 2))
-        def _(step):
+        def heads(step):
             image, pair = step // (HEADS // 2), step % (HEADS // 2)
             rows = pl.ds(pl.multiple_of(image * PAD, 16), PAD)
             lanes = [pl.ds(pl.multiple_of(pair * 128 + part * D, 128), 128) for part in range(3)]
@@ -997,6 +1180,10 @@
             r.dt[rows, lanes[1]] = (jnp.where(low_lane, dks[0], dks[1]) * scale).astype(BF)
             r.dt[rows, lanes[2]] = jnp.where(low_lane, dvs[0], dvs[1]).astype(BF)
 
+        half = images * (HEADS // 2) // 2
+        pl.loop(0, half)(heads)
+        point(it, 2)
+        pl.loop(half, 2 * half)(heads)
         pl.when(below)(lambda: start(layer - 1, o_, t_, p_))
         r.g[...] = jnp.zeros_like(r.g)
 
@@ -1006,7 +1193,7 @@
             store_cols(plan, r.unit, slot_t, j, D, dot(r.vm_a[...], r.dt[:, cols], TN))
             r.g[...] += dot(r.dt[:, cols], weight(r.expand_w, j * D, D), NT)
 
-        tick(it, 2)
+        point(it, 3)
         if cube:
             pl.when(it == 0)(head_rows.stage3)
         d_h, d_gain, d_shift = normalize_back(r.vm_h[...], row(r.params, base), r.g[...])
@@ -1041,24 +1228,7 @@
         return
     store_vectors(plan, r.unit, slot, r.vectors[...])
 
-    def stage(unit, which):
-        width = WIDTH if unit < UNITS else TAIL
-        done = Reduce(plan, r, jnp.int32(unit), width)
-        by_rows = unit % 3 == 0 and unit < UNITS
-        (
-            done.stage0,
-            done.stage1,
-            done.stage2,
-            done.stage3,
-            lambda: done.stage4(by_rows),
-            lambda: done.stage5(by_rows),
-        )[which]()
-
-    for ahead in range(5):
-        for which in (1, 0, 2, 3, 5, 4):
-            unit = UNITS + ahead - which
-            if unit <= UNITS:
-                stage(unit, which)
+    drain()
     r.tail_block[:BLOCK] = r.total[UNITS % 2, :, D // 2 : TAIL]
     line = lax.broadcasted_iota(jnp.int32, (8, 128), 0)
     squares, loss = jnp.sum(r.squares[...]), r.tail_in[0:1, 0:128]
@@ -1068,7 +1238,7 @@
     gather.stage1()
     gather.stage2()
     gather.stage3()
-    stage(UNITS, 5)
+    run(jnp.int32(UNITS), 6, False, TAIL)
     Reduce(plan, r, jnp.int32(UNITS), TAIL).copy(0).wait_send()
     gather.finish()
 
@@ -1117,23 +1287,33 @@
     scratch.update(dma(loads=(15,)))
     extra = {}
     if plan.cube:
+        other = other_part(WIDTH)
+        most = WIDTH - other
         scratch.update(
             vmem(
                 BF,
                 core=(4, 4, BLOCK, WIDTH),
-                near=(3, 4, BLOCK, WIDTH // 2),
-                far=(3, 4, BLOCK, WIDTH // 2),
-                x=(3, 4, BLOCK, WIDTH),
-                y=(3, 4, BLOCK, WIDTH),
-                z=(4, 3, BLOCK, WIDTH),
-                line=(2, 4, BLOCK, WIDTH),
+                near=(3, 4, BLOCK, cut_of(most)),
+                far=(3, 4, BLOCK, most - cut_of(most)),
+                x=(3, 4, BLOCK, most),
+                y=(3, 4, BLOCK, most),
+                line=(3, 4, BLOCK, most),
+                main_two=(3, 2, BLOCK, most),
+                main_one=(4, 2, BLOCK, most),
+                other_two=(3, 2, 4, BLOCK, other),
+                other_one=(4, 2, 4, BLOCK, other),
+                plane=(3, 4, BLOCK, other),
+                other_near=(3, BLOCK, cut_of(other)),
+                other_far=(3, BLOCK, other - cut_of(other)),
+                other_x=(3, BLOCK, other),
+                other_y=(3, BLOCK, other),
             )
         )
         scratch.update(
             vmem(F32, total=(2, BLOCK, WIDTH), squares=(8, WIDTH), tail_block=(BLOCK + 8, 128))
         )
         scratch.update(
-            dma(send=(4, 11), recv=(4, 11), head_send=(7,), head_recv=(7,), tail_send=(7,), tail_recv=(7,))
+            dma(send=(4, 20), recv=(4, 18), head_send=(7,), head_recv=(7,), tail_send=(7,), tail_recv=(7,))
         )
         scratch.update(credit=pltpu.SemaphoreType.REGULAR)
         extra = dict(collective_id=2, has_side_effects=True)

time: 502 us -> 458 us (0.912)
  Pallas kernels: 493 us -> 449 us
    pallas_call x3, Pallas kernels: 493 us -> 449 us  [pallas(): pl.pallas_call(functools.partial(kernel, names), out_shape=[jax.ShapeDtyp...]
where the time goes in v2:
time: 458 us; the launch traced here: 457 us
  Pallas kernels  449 us (98%)
  local copies, waits for them, and re-layouts  6.45 us (1%)
    pallas_call x3, Pallas kernels, pallas(): pl.pallas_call(functools.partial(kernel, names), out_shape=[jax.ShapeDtyp...  449 us

profile of v2, /device:TPU:0, one launch (start us, length us, event | category | flops | bytes accessed | tf_op | source)
XLA Modules:
  0.0 456.9 jit_solution(337069366952142657)
XLA Ops:
  0.7 0.7 convert_bitcast_fusion
  1.3 0.1 copy.50
  1.4 0.7 copy.49
  2.2 0.6 pad.8.refs_3_
  2.8 0.6 pad.9.refs_4_
  3.4 2.0 copy.52.refs_0_
  5.3 211.8 %forward.1 = (bf16[4,2,2,48,768]{4,3,2,1,0:T(8,128)(2,1)}, bf16[3,4,2,2,48,3072]{5,4,3,2,1,0:T(8,128)(2,1)}, bf16[3,4,2,2,48,3072]{5,4,3,2,1,0:T(8,128)(2,1)}, b...) custom-call(bf16[2,196,768]{2,1,0:T(8,128)(2,1)} %copy.52.refs_0_, ...), custom_call_target="tpu_custom_call" | custom-call | tf_op jit(solution)/shard_map/forward/pallas_call | solution.py:644
  217.2 1.2 slice.10
  218.4 219.9 %backward.1 = (f32[9,2,24,1536]{3,2,1,0:T(8,128)}, f32[2,24,384]{2,1,0:T(8,128)}, f32[4,2,2,2,56,128]{5,4,3,2,1,0:T(8,128)}, f32[4,2,2,2,32,128]{5,4,3,2,1,0:T(8,128)}) custom-call(bf16[2,196,768]{2,1,0:T(8,128)(2,1)} %copy.52.refs_0_, f32[213,768]{1,0:T(8,128)} %refs_15_.1, f32[8,768]{1,0:T(8,128)} %get-tuple-element.68.refs_2_, ...), custom_call_target="tpu_custom_call" | custom-call | tf_op jit(solution)/shard_map/backward/pallas_call | solution.py:644
  438.2 17.4 %update.1 = (f32[24,768]{1,0:T(8,128)}, f32[24,768]{1,0:T(8,128)}, f32[24,768]{1,0:T(8,128)}, f32[3,24,2304]{2,1,0:T(8,128)}, f32[3,24,2304]{2,1,0:T(8,128)}, /*...) custom-call(f32[24,768]{1,0:T(8,128)} %refs_0_.3, ...), custom_call_target="tpu_custom_call" | custom-call | tf_op jit(solution)/shard_map/update/pallas_call | solution.py:644
  455.6 1.3 fusion

commit v3 on v2

--- a/solution.py
+++ b/solution.py
@@ -36,7 +36,7 @@
 TN = (((0,), (0,)), ((), ()))
 VMEM_SPEC = pl.BlockSpec(memory_space=pltpu.VMEM)
 ANY_SPEC = pl.BlockSpec(memory_space=pl.ANY)
-LIMIT = 61 * 1024 * 1024
+LIMIT = 62 * 1024 * 1024
 
 
 def dot(left, right, form=NN):
@@ -85,6 +85,9 @@
         self.wide, self.grp = mesh.shape["wide"], mesh.shape["grp"]
         self.n = self.wide * self.grp
         self.cube = self.wide == 8 and self.grp == 4
+
+    def me(self):
+        return lax.axis_index("wide") * self.grp + lax.axis_index("grp")
 
     def where(self):
         if not self.cube:
@@ -357,8 +360,32 @@
 HALF = BLOCK // 2
 WIDTH = FF // 2
 HEAD_ROWS = 16
-HEAD_BLOCK = 32
 FINAL = S + 2 + 4 * LAYERS
+TOP = LAYERS - 1
+CLASS_PAD = 1024
+
+Z_, M_, O_, Q_, A_ = (slice(0, FF),) + tuple(slice(FF + k * D, FF + k * D + D) for k in range(4))
+FEATURE_, LOGIT_ = slice(FF + 4 * D, FF + 5 * D), slice(FF + 5 * D, FF + 5 * D + CLASS_PAD)
+SLOPE_, H1_, G_ = slice(0, FF), slice(FF, FF + D), slice(FF + D, FF + 2 * D)
+PIECES = (D, CLASS_PAD, FF, D, D, FF, D, D, D, D)
+PER_IMAGE = sum(PIECES) // 128
+
+
+def rows_block(images):
+    return -(-PER_IMAGE * images // 16) * 16
+
+
+def class_rows(ref, source):
+    ref[...] = jnp.zeros_like(ref)
+    for image in range(source.shape[0] // PAD):
+        ref[image : image + 1] = source[image * PAD : image * PAD + 1]
+
+
+def by_head(rows, image):
+    head = lax.broadcasted_iota(jnp.int32, (16, D), 0)
+    lane = lax.broadcasted_iota(jnp.int32, (16, D), 1)
+    mine = (lane >= head * HEAD_DIM) & (lane < head * HEAD_DIM + HEAD_DIM)
+    return mine, jnp.where(mine, rows[image : image + 1], 0.0)
 
 
 def saved_shapes(rows):
@@ -424,13 +451,8 @@
         copy.wait_send()
 
 
-def head_part(r, image_total):
-    images = r.h.shape[0] // PAD
+def head_part(r, first, image_total):
     table = r.head[:D].astype(BF)
-    r.first[...] = jnp.zeros_like(r.first)
-    for image in range(images):
-        r.first[image : image + 1] = r.h[image * PAD : image * PAD + 1]
-    first = r.first[...]
     gain, shift = r.vectors[FINAL : FINAL + 1], r.vectors[FINAL + 1 : FINAL + 2]
     feature = normalize(first, gain, shift).astype(BF)
     logits = dot(feature, table) + r.head[D : D + 1]
@@ -444,19 +466,10 @@
     d_feature = dot(d_logits, table, NT)
     r.d_logits[...] = jnp.zeros_like(r.d_logits)
     r.d_logits[:, :CLASSES] = d_logits.astype(F32)
-    r.head_block[...] = jnp.zeros_like(r.head_block)
-    feature = feature.astype(F32)
-    for image in range(images):
-        for j in range(6):
-            at = image * 14 + j
-            r.head_block[at : at + 1] = feature[image : image + 1, j * 128 : j * 128 + 128]
-        for j in range(8):
-            at = image * 14 + 6 + j
-            r.head_block[at : at + 1] = r.d_logits[image : image + 1, j * 128 : j * 128 + 128]
+    r.top_b[:, FEATURE_] = feature
+    r.top_b[:, LOGIT_] = r.d_logits[...].astype(BF)
     d_first, d_gain, d_shift = normalize_back(first, gain, d_feature)
-    r.g[...] = jnp.zeros_like(r.g)
-    for image in range(images):
-        r.g[image * PAD : image * PAD + 1] = d_first[image : image + 1]
+    r.top_f[:, G_] = d_first
     r.tail[...] = jnp.zeros_like(r.tail)
     r.tail[0:1] = jnp.full((1, D), loss, F32)
     r.tail[1:2] = d_gain
@@ -526,16 +539,12 @@
     low_lane = lax.broadcasted_iota(jnp.int32, (PAD, 128), 1) < HEAD_DIM
     real_key = lax.broadcasted_iota(jnp.int32, (PAD, PAD), 0) < S
 
-    @pl.loop(0, LAYERS)
+    @pl.loop(0, TOP)
     def _(layer):
-        more = layer < LAYERS - 1
         base = S + 2 + 4 * layer
         if cube:
-            @pl.when(more)
-            def _():
-                unit(expand, layer + 1).stage0()
-                unit(joined, layer + 1).stage1()
-
+            unit(expand, layer + 1).stage0()
+            unit(joined, layer + 1).stage1()
             unit(shrink, layer).stage2()
             unit(expand, layer).stage3()
             unit(joined, layer).stage4()
@@ -576,11 +585,9 @@
         half = images * (HEADS // 2) // 2
         pl.loop(0, half)(heads)
         if cube:
-            @pl.when(more)
-            def _():
-                unit(shrink, layer + 1).stage0()
-                unit(expand, layer + 1).stage1()
-                unit(joined, layer + 1).stage2()
+            unit(shrink, layer + 1).stage0()
+            unit(expand, layer + 1).stage1()
+            unit(joined, layer + 1).stage2()
 
         pl.loop(half, 2 * half)(heads)
         start_all(saves(layer, o_, p_))
@@ -612,14 +619,11 @@
 
         start_all(saves(layer, z_, slope_))
         if cube:
-            pl.when(layer < LAYERS - 2)(lambda: unit(joined, layer + 2).stage0())
-
-            @pl.when(more)
-            def _():
-                unit(shrink, layer + 1).stage1()
-                unit(expand, layer + 1).stage2()
-                unit(joined, layer + 1).stage3()
-
+            pl.when(layer < TOP - 1)(lambda: unit(joined, layer + 2).stage0())
+
+            unit(shrink, layer + 1).stage1()
+            unit(expand, layer + 1).stage2()
+            unit(joined, layer + 1).stage3()
             unit(shrink, layer).stage4()
             pl.when(layer == 0)(counting.stage2)
             pl.when(layer == 1)(counting.finish)
@@ -629,14 +633,65 @@
         def _(j):
             cols = pl.ds(pl.multiple_of(j * D, 128), D)
             r.h[...] += dot(r.z[:, cols], r.shrink_w[j].reshape(D, D))
+
+    base = S + 2 + 4 * TOP
+    if cube:
+        unit(shrink, TOP).stage2()
+        unit(expand, TOP).stage3()
+        unit(joined, TOP).stage4()
+    start_all(saves(TOP, h_))
+    wait_all(saves(TOP, a_, t_) + saves(0, o_, p_, h1_, m_))
+    r.a[...] = normalize(r.h[...], row(r.vectors, base), row(r.vectors, base + 1)).astype(BF)
+    class_rows(r.first, r.h)
+    first = r.first[...]
+    r.top_b[:, A_] = normalize(first, row(r.vectors, base), row(r.vectors, base + 1)).astype(BF)
+    ready(joined, TOP).wait()
+    for j in (1, 2):
+        r.t[:, j * D : j * D + D] = dot(r.a[...], weight(r.joined_w, j * D, D)).astype(BF)
+    start_all(saves(TOP, a_, t_))
+    query = dot(r.top_b[:, A_], weight(r.joined_w, 0, D)).astype(BF)
+    r.top_b[:, Q_] = query
+    if cube:
+        unit(shrink, TOP).stage3()
+        unit(expand, TOP).stage4()
+    query = query.astype(F32)
+    real = lax.broadcasted_iota(jnp.int32, (PAD, 16), 0) < S
+    r.class_row[...] = jnp.zeros_like(r.class_row)
+    for image in range(images):
+        rows = slice(image * PAD, image * PAD + PAD)
+        mine, spread = by_head(query, image)
+        scores = dot(r.t[rows, D : 2 * D], spread.astype(BF), NT) * HEAD_DIM**-0.5
+        scores = jnp.where(real, scores, -1e30)
+        e = jnp.exp(scores - jnp.max(scores, 0, keepdims=True))
+        p = (e * (1.0 / jnp.sum(e, 0, keepdims=True))).astype(BF)
+        r.top_p[image] = p
+        out = jnp.where(mine, dot(p, r.t[rows, 2 * D :], TN), 0.0)
+        r.class_row[image : image + 1] = jnp.sum(out, 0, keepdims=True)
+    attended = r.class_row[...].astype(BF)
+    r.top_b[:, O_] = attended
+    h1 = first + dot(attended, weight(r.joined_w, 3 * D, D))
+    r.top_f[:, H1_] = h1
+    r.top_b[:, M_] = normalize(h1, row(r.vectors, base + 2), row(r.vectors, base + 3)).astype(BF)
+    ready(expand, TOP).wait()
+    for j in range(4):
+        cols = slice(j * D, j * D + D)
+        z, slope = gelu_and_slope(dot(r.top_b[:, M_], weight(r.expand_w, j * D, D)))
+        r.top_b[:, cols] = z.astype(BF)
+        r.top_f[:, cols] = slope
+    if cube:
+        unit(shrink, TOP).stage4()
+    ready(shrink, TOP).wait()
+    last = h1
+    for j in range(4):
+        last = last + dot(r.top_b[:, j * D : j * D + D], r.shrink_w[j].reshape(D, D))
 
     if cube:
         r.total[...] = jnp.sum(r.counts[...].reshape(-1, 8, 128), 0)
         image_total = r.total[0:1, 0:1]
     else:
         image_total = r.count_in[0:1, 0:1]
-    head_part(r, image_total)
-    wait_all(saves(LAYERS - 1, a_, t_, o_, p_, h1_, m_, z_, slope_))
+    head_part(r, last, image_total)
+    wait_all(saves(TOP, h_, a_, t_) + saves(0, z_, slope_))
 
 
 def pallas(kernel, name, inputs, outputs, scratch, **params):
@@ -683,11 +738,13 @@
         inputs.update(given_in(ANY_SPEC, **dict(zip(whole, gathered))))
         inputs.update(given_in(VMEM_SPEC, count_in=count))
     for name, (shape, kind) in shapes.items():
-        outputs["keep_" + name] = ((LAYERS,) + shape, kind, ANY_SPEC)
+        deep = LAYERS if name in ("h", "a", "t") else TOP
+        outputs["keep_" + name] = ((deep,) + shape, kind, ANY_SPEC)
     outputs.update(
-        g=((rows, D), F32, VMEM_SPEC),
+        top_b=((HEAD_ROWS, LOGIT_.stop), BF, VMEM_SPEC),
+        top_f=((HEAD_ROWS, G_.stop), F32, VMEM_SPEC),
+        top_p=((rows // PAD, PAD, 16), BF, VMEM_SPEC),
         tail=((8, D), F32, VMEM_SPEC),
-        head_block=((HEAD_BLOCK, 128), F32, VMEM_SPEC),
         total=((8, 128), F32, VMEM_SPEC),
     )
     scratch = vmem(
@@ -698,7 +755,7 @@
         shrink_w=ROWS_SHAPE,
     )
     scratch.update({name: pltpu.VMEM(shape, kind) for name, (shape, kind) in shapes.items()})
-    scratch.update(vmem(F32, first=(HEAD_ROWS, D), d_logits=(HEAD_ROWS, 1024)))
+    scratch.update(vmem(F32, first=(HEAD_ROWS, D), class_row=(HEAD_ROWS, D), d_logits=(HEAD_ROWS, CLASS_PAD)))
     scratch.update(dma(saves=(9,), loads=(4,)))
     extra = {}
     if plan.cube:
@@ -734,7 +791,8 @@
     return got
 
 
-UNITS = 3 * LAYERS
+UNITS = 3 * TOP + 1
+KEYS = D
 TAIL = 512
 SEND = 4
 VEC_ROWS = 256
@@ -795,10 +853,7 @@
         own = b.unit.at[slot]
         if at == 17:
             rows = pl.ds(pl.multiple_of((1 - c) * HALF, 8), HALF)
-            if self.width == WIDTH:
-                src, dst = b.total.at[self.two, rows], b.owned.at[self.unit, c]
-            else:
-                src, dst = b.total.at[self.two, rows, pl.ds(0, D // 2)], b.patch.at[c]
+            src, dst = self.result(rows)
             device = to.core
         else:
             src, dst, device = {
@@ -822,17 +877,22 @@
             }[at]()
         return remote(src, dst, b.send.at[slot, at], b.recv.at[slot, at], device)
 
+    def result(self, rows):
+        b, c = self.bufs, self.c
+        total = b.total.at[self.two]
+        if self.width == WIDTH:
+            return total.at[rows], b.owned.at[self.unit - 1, c]
+        if self.width == KEYS:
+            return total.at[rows, pl.ds(0, KEYS)], b.keys.at[c]
+        return total.at[rows, pl.ds(0, D // 2)], b.patch.at[c]
+
     def own(self, by_rows):
         b, c = self.bufs, self.c
         total = b.total.at[self.two]
         if by_rows:
-            moves = [(total.at[pl.ds(k * HALF, HALF)], b.owned.at[self.unit, k]) for k in range(2)]
+            moves = [(total.at[pl.ds(k * HALF, HALF)], b.owned.at[self.unit - 1, k]) for k in range(2)]
         else:
-            rows = pl.ds(pl.multiple_of(c * HALF, 8), HALF)
-            if self.width == WIDTH:
-                moves = [(total.at[rows], b.owned.at[self.unit, c])]
-            else:
-                moves = [(total.at[rows, pl.ds(0, D // 2)], b.patch.at[c])]
+            moves = [self.result(pl.ds(pl.multiple_of(c * HALF, 8), HALF))]
         return [
             pltpu.make_async_copy(src, dst, b.send.at[self.slot, 18 + k])
             for k, (src, dst) in enumerate(moves)
@@ -1024,7 +1084,6 @@
         (r.joined_whole, r.expand_w),
     ]
     z_, shrink_, slope_, expand_, m_, h1_, o_, t_, p_, a_, h_, joined_ = range(12)
-    top = LAYERS - 1
 
     def fetch(which, layer):
         src, dst = loads[which]
@@ -1038,16 +1097,14 @@
         for k in which:
             fetch(k, layer).wait()
 
-    first_g = load(r.g_in, r.g, r.loads.at[joined_ + 1])
-    start(top, *range(joined_))
+    start(TOP, shrink_, expand_, t_, a_, h_)
+    start(TOP - 1, z_, slope_, m_, h1_, o_, p_)
     if cube:
         cube_barrier(plan)
         r.squares[...] = jnp.zeros_like(r.squares)
-        head_rows = SmallGather(plan, r.head_block, r.head_rows, r.head_send, r.head_recv)
-        head_rows.stage0()
+        top_rows = SmallGather(plan, r.rows_block, r.top_rows, r.rows_send, r.rows_recv)
     r.vectors[...] = jnp.zeros_like(r.vectors)
     r.vectors[FINAL : FINAL + 2] = r.tail_in[1:3]
-    first_g.wait()
 
     def run(unit, stage, by_rows, width=WIDTH):
         unit = Reduce(plan, r, unit, width)
@@ -1065,7 +1122,7 @@
         if not cube:
             for kind in range(3):
                 if ENTRY[kind] == at:
-                    unit = 3 * it + kind
+                    unit = 3 * it - 2 + kind
                     copies = [
                         pltpu.make_async_copy(
                             r.unit.at[(unit % 4, SEND)[i]],
@@ -1082,39 +1139,136 @@
                 past, phase = divmod(ENTRY[kind] + stage, POINTS)
                 if phase != at:
                     continue
-                unit = 3 * (it - past) + kind
+                unit = 3 * (it - past) - 2 + kind
                 if past:
-                    pl.when(it >= past)(functools.partial(run, unit, stage, kind == 0))
+                    pl.when(it > past)(functools.partial(run, unit, stage, kind == 0))
                 else:
                     run(unit, stage, kind == 0)
+                if past and kind == 2:
+                    pl.when(it == past)(functools.partial(run, unit, stage, False, KEYS))
 
     def drain():
         at = 0
         while at <= 5:
             for stage in STAGE_ORDER:
-                for past, kind in ((2, 0), (2, 1), (2, 2), (1, 0), (1, 1), (1, 2)):
+                for past, kind in ((1, 0), (1, 1), (1, 2), (2, 0), (2, 1), (2, 2)):
                     if POINTS * past + at - ENTRY[kind] == stage:
                         run(jnp.int32(UNITS - 3 * past + kind), stage, kind == 0)
                 if at == stage:
                     run(jnp.int32(UNITS), stage, False, TAIL)
             at += 1
 
-    def sent(unit):
+    def sent(unit, width=WIDTH):
         if cube:
-            pl.when(unit > 0)(lambda: Reduce(plan, r, unit - 1).copy(0).wait_send())
+            Reduce(plan, r, unit - 1, width).copy(0).wait_send()
 
     low_lane = lax.broadcasted_iota(jnp.int32, (PAD, 128), 1) < HEAD_DIM
     scale = HEAD_DIM**-0.5
 
-    @pl.loop(0, LAYERS)
+    base = S + 2 + 4 * TOP
+    g = r.top_f[:, G_]
+    g_low = g.astype(BF)
+    wait(TOP, shrink_)
+    for j in range(4):
+        cols = slice(j * D, j * D + D)
+        dz = dot(g_low, r.shrink_w[j].reshape(D, D), NT)
+        r.top_du[:, cols] = (dz * r.top_f[:, cols]).astype(BF)
+    start(TOP - 1, shrink_)
+    wait(TOP, expand_)
+    d_m = jnp.zeros((HEAD_ROWS, D), F32)
+    for j in range(4):
+        d_m = d_m + dot(r.top_du[:, j * D : j * D + D], weight(r.expand_w, j * D, D), NT)
+    start(TOP, joined_)
+    d_h1, d_gain, d_shift = normalize_back(r.top_f[:, H1_], row(r.params, base + 2), d_m)
+    r.vectors[base + 2 : base + 3] = d_gain
+    r.vectors[base + 3 : base + 4] = d_shift
+    g1 = g + d_h1
+    g1_low = g1.astype(BF)
+    wait(TOP, joined_)
+    d_o = dot(g1_low, weight(r.expand_w, 3 * D, D), NT).astype(BF).astype(F32)
+    query = r.top_b[:, Q_].astype(F32)
+    wait(TOP, t_, a_, h_)
+    r.class_row[...] = jnp.zeros_like(r.class_row)
+    for image in range(images):
+        rows = slice(image * PAD, image * PAD + PAD)
+        mine, spread_o = by_head(d_o, image)
+        _, spread_q = by_head(query, image)
+        spread_o, spread_q = spread_o.astype(BF), spread_q.astype(BF)
+        p_low = r.top_p[image]
+        p = p_low.astype(F32)
+        r.dt[rows, 2 * D :] = dot(p_low, spread_o).astype(BF)
+        dp = dot(r.vm_t[rows, 2 * D :], spread_o, NT)
+        ds = (p * (dp - jnp.sum(p * dp, 0, keepdims=True))).astype(BF)
+        r.dt[rows, D : 2 * D] = (dot(ds, spread_q) * HEAD_DIM**-0.5).astype(BF)
+        d_q = jnp.where(mine, dot(ds, r.vm_t[rows, D : 2 * D], TN), 0.0)
+        r.class_row[image : image + 1] = jnp.sum(d_q, 0, keepdims=True) * HEAD_DIM**-0.5
+    start(TOP - 1, t_)
+    for part in range(2):
+        value = dot(r.vm_a[...], r.dt[:, (part + 1) * D : (part + 2) * D], TN)
+        store_cols(plan, r.unit, 0, part, KEYS, value, KEYS)
+    if cube:
+        run(jnp.int32(0), 0, False, KEYS)
+    else:
+        copies = [
+            pltpu.make_async_copy(r.unit.at[(0, SEND)[i]], r.full.at[0, i], r.loads.at[joined_ + 1 + i])
+            for i in range(2)
+        ]
+        start_all(copies)
+        wait_all(copies)
+    start(TOP - 1, a_)
+    d_q = r.class_row[...].astype(BF)
+    sources = (
+        r.top_b[:, FEATURE_],
+        r.top_b[:, LOGIT_],
+        r.top_b[:, Z_],
+        g_low,
+        r.top_b[:, M_],
+        r.top_du[...],
+        r.top_b[:, O_],
+        g1_low,
+        r.top_b[:, A_],
+        d_q,
+    )
+    r.rows_f[...] = jnp.zeros_like(r.rows_f)
+    first = 0
+    for source in sources:
+        value = source.astype(F32)
+        for j in range(value.shape[1] // 128):
+            for image in range(images):
+                at = image * PER_IMAGE + first + j
+                r.rows_f[at : at + 1] = value[image : image + 1, j * 128 : j * 128 + 128]
+        first += value.shape[1] // 128
+    r.rows_block[...] = r.rows_f[...].astype(BF)
+    if cube:
+        top_rows.stage0()
+    else:
+        save = load(r.rows_block, r.top_rows, r.loads.at[joined_ + 1])
+        save.wait()
+    r.g1[...] = dot(r.dt[:, D : 2 * D], weight(r.expand_w, D, D), NT)
+    r.g1[...] += dot(r.dt[:, 2 * D :], weight(r.expand_w, 2 * D, D), NT)
+    d_a = dot(d_q, weight(r.expand_w, 0, D), NT)
+    for image in range(images):
+        r.g1[image * PAD : image * PAD + 1] += d_a[image : image + 1]
+    start(TOP - 1, expand_)
+    d_h, d_gain, d_shift = normalize_back(r.vm_h[...], row(r.params, base), r.g1[...])
+    r.g[...] = d_h
+    for image in range(images):
+        r.g[image * PAD : image * PAD + 1] += g1[image : image + 1]
+    r.vectors[base : base + 1] = d_gain
+    r.vectors[base + 1 : base + 2] = d_shift
+    start(TOP - 1, h_)
+
+    @pl.loop(1, LAYERS)
     def _(it):
-        layer = top - it
-        below = it < LAYERS - 1
+        layer = TOP - it
+        below = it < TOP
+        unit_s = 3 * it - 2
         base = S + 2 + 4 * layer
         r.gr[...] = r.g[...].astype(BF)
         wait(layer, z_)
-        slot = (3 * it) % 4
-        sent(3 * it)
+        slot = unit_s % 4
+        pl.when(it == 1)(lambda: sent(unit_s, KEYS))
+        pl.when(it > 1)(lambda: sent(unit_s))
 
         @pl.loop(0, 8)
         def _(j):
@@ -1123,27 +1277,33 @@
 
         point(it, 0)
         if cube:
-            pl.when(it == 0)(head_rows.stage1)
-            pl.when(it == 1)(head_rows.finish)
+            pl.when(it == 1)(top_rows.stage1)
         wait(layer, shrink_, slope_, expand_, m_, h1_)
         pl.when(below)(lambda: start(layer - 1, z_))
-        slot_e = (3 * it + 1) % 4
+        slot_e = (unit_s + 1) % 4
         r.g1[...] = jnp.zeros_like(r.g1)
-        sent(3 * it + 1)
+        sent(unit_s + 1)
 
         @pl.loop(0, 4)
         def _(j):
             cols = pl.ds(pl.multiple_of(j * D, 128), D)
             dz = dot(r.gr[...], r.shrink_w[j].reshape(D, D), NT)
             du = (dz * r.vm_slope[:, cols].astype(F32)).astype(BF)
-            r.g1[...] += dot(du, weight(r.expand_w, j * D, D), NT)
+            r.vm_slope[:, cols] = du
             store_cols(plan, r.unit, slot_e, j, D, dot(r.vm_m[...], du, TN))
 
-        start(layer, joined_)
-        pl.when(below)(lambda: start(layer - 1, shrink_, slope_, m_))
+        pl.when(below)(lambda: start(layer - 1, shrink_, m_))
         point(it, 1)
         if cube:
-            pl.when(it == 0)(head_rows.stage2)
+            pl.when(it == 1)(top_rows.stage2)
+
+        @pl.loop(0, 4)
+        def _(j):
+            cols = pl.ds(pl.multiple_of(j * D, 128), D)
+            r.g1[...] += dot(r.vm_slope[:, cols], weight(r.expand_w, j * D, D), NT)
+
+        start(layer, joined_)
+        pl.when(below)(lambda: start(layer - 1, slope_))
         d_h1, d_gain, d_shift = normalize_back(r.vm_h1[...], row(r.params, base + 2), r.g1[...])
         r.g1[...] = r.g[...] + d_h1
         r.vectors[pl.ds(base + 2, 1)] = d_gain
@@ -1151,9 +1311,9 @@
         pl.when(below)(lambda: start(layer - 1, h1_))
 
         r.gr[...] = r.g1[...].astype(BF)
-        slot_t = (3 * it + 2) % 4
+        slot_t = (unit_s + 2) % 4
         wait(layer, o_)
-        sent(3 * it + 2)
+        sent(unit_s + 2)
         store_cols(plan, r.unit, slot_t, 3, D, dot(r.vm_o[...], r.gr[...], TN))
         wait(layer, joined_)
         r.do[...] = dot(r.gr[...], weight(r.expand_w, 3 * D, D), NT).astype(BF)
@@ -1183,6 +1343,8 @@
         half = images * (HEADS // 2) // 2
         pl.loop(0, half)(heads)
         point(it, 2)
+        if cube:
+            pl.when(it == 1)(top_rows.stage3)
         pl.loop(half, 2 * half)(heads)
         pl.when(below)(lambda: start(layer - 1, o_, t_, p_))
         r.g[...] = jnp.zeros_like(r.g)
@@ -1191,11 +1353,16 @@
         def _(j):
             cols = pl.ds(pl.multiple_of(j * D, 128), D)
             store_cols(plan, r.unit, slot_t, j, D, dot(r.vm_a[...], r.dt[:, cols], TN))
-            r.g[...] += dot(r.dt[:, cols], weight(r.expand_w, j * D, D), NT)
 
         point(it, 3)
         if cube:
-            pl.when(it == 0)(head_rows.stage3)
+            pl.when(it == 1)(top_rows.finish)
+
+        @pl.loop(0, 3)
+        def _(j):
+            cols = pl.ds(pl.multiple_of(j * D, 128), D)
+            r.g[...] += dot(r.dt[:, cols], weight(r.expand_w, j * D, D), NT)
+
         d_h, d_gain, d_shift = normalize_back(r.vm_h[...], row(r.params, base), r.g[...])
         r.g[...] = r.g1[...] + d_h
         r.vectors[pl.ds(base, 1)] = d_gain
@@ -1244,15 +1411,21 @@
 
 
 def backward(plan, images, params, done):
-    rows = done.g.shape[0]
+    rows = images.shape[0] * PAD
     shapes = saved_shapes(rows)
-    inputs = given_in(VMEM_SPEC, images=images, params=params, tail_in=done.tail)
-    if plan.cube:
-        inputs.update(given_in(VMEM_SPEC, head_block=done.head_block))
+    inputs = given_in(
+        VMEM_SPEC,
+        images=images,
+        params=params,
+        tail_in=done.tail,
+        top_b=done.top_b,
+        top_f=done.top_f,
+        top_p=done.top_p,
+    )
+    block = rows_block(images.shape[0])
     inputs.update(
         given_in(
             ANY_SPEC,
-            g_in=done.g,
             joined_whole=done.joined_whole,
             expand_whole=done.expand_whole,
             shrink_whole=done.shrink_whole,
@@ -1261,15 +1434,17 @@
     inputs.update({"keep_" + name: (getattr(done, "keep_" + name), ANY_SPEC) for name in SAVED})
     if plan.cube:
         outputs = dict(
-            owned=((UNITS, 2, HALF, WIDTH), F32, ANY_SPEC),
+            owned=((UNITS - 1, 2, HALF, WIDTH), F32, ANY_SPEC),
+            keys=((2, HALF, KEYS), F32, ANY_SPEC),
             patch=((2, HALF, D // 2), F32, ANY_SPEC),
             vector_rows=(CHIPS + (2, BLOCK + 8, 128), F32, ANY_SPEC),
-            head_rows=(CHIPS + (2, HEAD_BLOCK, 128), F32, ANY_SPEC),
+            top_rows=(CHIPS + (2, block, 128), BF, ANY_SPEC),
         )
     else:
         outputs = dict(
             full=((UNITS + 1, 2, 4, 4, BLOCK, WIDTH), BF, ANY_SPEC),
             vector_rows=((VEC_ROWS, D), F32, ANY_SPEC),
+            top_rows=((block, 128), BF, ANY_SPEC),
         )
     scratch = {"vm_" + name: pltpu.VMEM(shape, kind) for name, (shape, kind) in shapes.items()}
     scratch.update(
@@ -1281,9 +1456,20 @@
             do=(rows, D),
             dt=(rows, 3 * D),
             unit=(SEND + 1, 4, 4, BLOCK, WIDTH),
+            top_du=(HEAD_ROWS, FF),
+            rows_block=(block, 128),
         )
     )
-    scratch.update(vmem(F32, g=(rows, D), g1=(rows, D), vectors=(VEC_ROWS, D)))
+    scratch.update(
+        vmem(
+            F32,
+            g=(rows, D),
+            g1=(rows, D),
+            vectors=(VEC_ROWS, D),
+            class_row=(HEAD_ROWS, D),
+            rows_f=(block, 128),
+        )
+    )
     scratch.update(dma(loads=(15,)))
     extra = {}
     if plan.cube:
@@ -1313,7 +1499,7 @@
             vmem(F32, total=(2, BLOCK, WIDTH), squares=(8, WIDTH), tail_block=(BLOCK + 8, 128))
         )
         scratch.update(
-            dma(send=(4, 20), recv=(4, 18), head_send=(7,), head_recv=(7,), tail_send=(7,), tail_recv=(7,))
+            dma(send=(4, 20), recv=(4, 18), rows_send=(7,), rows_recv=(7,), tail_send=(7,), tail_recv=(7,))
         )
         scratch.update(credit=pltpu.SemaphoreType.REGULAR)
         extra = dict(collective_id=2, has_side_effects=True)
@@ -1335,25 +1521,33 @@
     return (master_new, moment_new, square_new)
 
 
-def head_matrices(ref, images):
-    def take(first, count):
-        devices = ref.shape[0] // HEAD_BLOCK
-        pieces = [
+def class_matrices(ref, images, devices, stride):
+    first, found = 0, []
+    for columns in PIECES:
+        count = columns // 128
+        parts = [
             jnp.concatenate(
                 [
-                    ref[pl.ds(image * 14 + first + j, devices, stride=HEAD_BLOCK), :]
+                    ref[pl.ds(image * PER_IMAGE + first + j, devices, stride=stride), :]
                     for j in range(count)
                 ],
                 1,
             )
             for image in range(images)
         ]
-        return jnp.concatenate(pieces, 0).astype(BF)
-
-    return take(0, 6), take(6, 8)
-
-
-def update_kernel(images, names, *refs):
+        found.append(jnp.concatenate(parts, 0).astype(BF))
+        first += count
+    return found
+
+
+def own_columns(value, first, count):
+    at = lax.broadcasted_iota(jnp.int32, (value.shape[1], 128), 0)
+    to = lax.broadcasted_iota(jnp.int32, (value.shape[1], 128), 1)
+    chosen = jnp.where((at == to + first) & (to < count), 1.0, 0.0).astype(BF)
+    return dot(value, chosen).astype(BF)
+
+
+def update_kernel(plan, images, names, *refs):
     r = SimpleNamespace(**dict(zip(names, refs)))
     named = dict(zip(names, refs))
     groups = [
@@ -1373,11 +1567,21 @@
         start_all(moves(group, False))
 
     tile = jnp.sum(r.tails[:, BLOCK:, :], 0)
-    features, d_logits = head_matrices(r.head_rows, images)
+    r.rows_f[...] = r.top_rows[...].astype(F32)
+    stride = r.top_rows.shape[0] // plan.n
+    found = class_matrices(r.rows_f, images, plan.n, stride)
+    features, d_logits, z, g, m, du, o, g1, a, dq = found
     r.features[...] = features
     r.d_logits[...] = d_logits
     alike = (dot(features, features, NT) + 1.0) * dot(d_logits, d_logits, NT)
+    for left, right in ((z, g), (m, du), (o, g1), (a, dq)):
+        alike = alike + dot(left, left, NT) * dot(right, right, NT)
     norm = jnp.sqrt(tile[0:1, 0:1] + jnp.sum(alike))
+    me = plan.me()
+
+    def top_grad(left, right, rows):
+        return dot(own_columns(left, me * rows, rows), right, TN)[:rows]
+
     clip = CLIP / jnp.maximum(norm, CLIP)
     line = lax.broadcasted_iota(jnp.int32, (8, 128), 0)
     r.scalars[...] = jnp.where(line == 0, norm, tile[1:2])
@@ -1406,9 +1610,11 @@
     finish(head)
     wait_all(moves(shrink, False))
 
-    @pl.loop(0, LAYERS)
+    step(shrink, (TOP, every, every), top_grad(z, g, BLOCK_FF), RATE_MATRIX)
+
+    @pl.loop(0, TOP)
     def _(layer):
-        unit = 3 * (LAYERS - 1 - layer)
+        unit = 3 * (TOP - 1 - layer)
         for k in range(4):
             gradient = r.owned[unit, k % 2, :, pl.ds(k // 2 * D, D)]
             step(shrink, (layer, pl.ds(k * HALF, HALF), every), gradient, RATE_MATRIX)
@@ -1416,9 +1622,11 @@
     finish(shrink)
     wait_all(moves(expand, False))
 
-    @pl.loop(0, LAYERS)
+    step(expand, (TOP, every, every), top_grad(m, du, HALF), RATE_MATRIX)
+
+    @pl.loop(0, TOP)
     def _(layer):
-        unit = 3 * (LAYERS - 1 - layer) + 1
+        unit = 3 * (TOP - 1 - layer) + 1
         for k in range(2):
             step(expand, (layer, every, pl.ds(k * WIDTH, WIDTH)), r.owned[unit, k], RATE_MATRIX)
 
@@ -1426,9 +1634,14 @@
     wait_all(moves(triple, False))
     wait_all(moves(output, False))
 
-    @pl.loop(0, LAYERS)
+    step(output, (TOP, every, every), top_grad(o, g1, HALF), RATE_OUTPUT)
+    step(triple, (TOP, every, pl.ds(0, D)), top_grad(a, dq, HALF), RATE_MATRIX)
+    for k in range(2):
+        step(triple, (TOP, every, pl.ds((k + 1) * D, D)), r.keys[k], RATE_MATRIX)
+
+    @pl.loop(0, TOP)
     def _(layer):
-        unit = 3 * (LAYERS - 1 - layer) + 2
+        unit = 3 * (TOP - 1 - layer) + 2
         step(triple, (layer, every, pl.ds(0, WIDTH)), r.owned[unit, 0], RATE_MATRIX)
         step(triple, (layer, every, pl.ds(WIDTH, D)), r.owned[unit, 1, :, pl.ds(0, D)], RATE_MATRIX)
         step(output, (layer, every, every), r.owned[unit, 1, :, pl.ds(D, D)], RATE_OUTPUT)
@@ -1463,14 +1676,15 @@
             owned=got.owned,
             patch_grad=got.patch,
             tails=got.vector_rows.reshape(plan.n, BLOCK + 8, 128),
-            head_rows=got.head_rows.reshape(plan.n * HEAD_BLOCK, 128),
+            keys=got.keys,
+            top_rows=got.top_rows.reshape(-1, 128),
         )
     )
     outputs.update(scalars=((8, 128), F32, VMEM_SPEC), bias_grad=((1, CLASSES), F32, VMEM_SPEC))
     scratch.update(vmem(BF, features=(plan.n * images, D), d_logits=(plan.n * images, 1024)))
-    scratch.update(vmem(F32, vector_grad=(VEC_ROWS, D)))
+    scratch.update(vmem(F32, vector_grad=(VEC_ROWS, D), rows_f=(plan.n * rows_block(images), 128)))
     scratch.update(dma(sems=(3 * len(PARAMS),)))
-    new = pallas(functools.partial(update_kernel, images), "update", inputs, outputs, scratch)
+    new = pallas(functools.partial(update_kernel, plan, images), "update", inputs, outputs, scratch)
     states = [[getattr(new, "to_" + kind + name) for kind in KINDS] for name in PARAMS]
     return new.scalars[0, 0], new.scalars[1, 0], states, new.bias_grad[0]
 
@@ -1480,7 +1694,7 @@
 
 def update_whole(plan, images, states, got, done):
     full = got.full.reshape(UNITS + 1, 2, 16, BLOCK, WIDTH)
-    layers = full[:UNITS].reshape(LAYERS, 3, 2, 16, BLOCK, WIDTH)[::-1]
+    layers = full[1:UNITS].reshape(TOP, 3, 2, 16, BLOCK, WIDTH)[::-1]
 
     def scattered(whole):
         axis = whole.ndim - 2
@@ -1490,18 +1704,30 @@
         joined = jnp.concatenate([part[..., 0, :, :, :], part[..., 1, :, :, :]], -1)
         return joined.reshape(part.shape[:-4] + (D, -1))
 
-    shrink = layers[:, 0].reshape(LAYERS, 2, 16, BLOCK, 2, D).transpose(0, 2, 1, 4, 3, 5)
+    shrink = layers[:, 0].reshape(TOP, 2, 16, BLOCK, 2, D).transpose(0, 2, 1, 4, 3, 5)
     joined = scattered(from_cols(layers[:, 2]))
-    rows_all = lax.all_gather(done.head_block, AXES, axis=0)[:, : 14 * images]
-    rows_all = rows_all.reshape(plan.n * images, 14 * 128).astype(BF)
-    features, d_logits = rows_all[:, :D], rows_all[:, D : D + CLASSES]
+    rows_all = lax.all_gather(got.top_rows, AXES, axis=0)[:, : PER_IMAGE * images]
+    rows_all = rows_all.reshape(plan.n * images, PER_IMAGE * 128)
+    ends = [sum(PIECES[: k + 1]) for k in range(len(PIECES))]
+    features, d_logits, z, g, m, du, o, g1, a, dq = jnp.split(rows_all, ends[:-1], axis=1)
+    d_logits = d_logits[:, :CLASSES]
     bias = jnp.sum(d_logits.astype(F32), 0)[None]
+
+    def top_grad(left, right):
+        whole = dot(left, right, TN)
+        count = whole.shape[0] // plan.n
+        return lax.dynamic_slice_in_dim(whole, plan.me() * count, count)
+
+    def with_top(below, top):
+        return jnp.concatenate([below, top[None]], 0)
+
+    keys = scattered(from_cols(full[0, ..., :KEYS]))
     split = [
         scattered(from_cols(full[UNITS, ..., : D // 2])),
-        joined[:, :, : 3 * D],
-        joined[:, :, 3 * D :],
-        scattered(from_cols(layers[:, 1])),
-        scattered(shrink.reshape(LAYERS, FF, D)),
+        with_top(joined[:, :, : 3 * D], jnp.concatenate([top_grad(a, dq), keys], 1)),
+        with_top(joined[:, :, 3 * D :], top_grad(o, g1)),
+        with_top(scattered(from_cols(layers[:, 1])), top_grad(m, du)),
+        with_top(scattered(shrink.reshape(TOP, FF, D)), top_grad(z, g)),
     ]
     same = [
         lax.psum(got.vector_rows[: states[5][0].shape[0]], AXES),

time: 458 us -> 422 us (0.921); the launches traced: 457 us -> 416 us
  Pallas kernels: 449 us -> 407 us
    pallas_call x3, Pallas kernels: 449 us -> 407 us  [pallas(): pl.pallas_call(functools.partial(kernel, names), out_shape=[jax.ShapeDtyp...]
where the time goes in v3:
time: 422 us; the launch traced here: 416 us
  Pallas kernels  407 us (96%)
  local copies, waits for them, and re-layouts  6.45 us (2%)
    pallas_call x3, Pallas kernels, pallas(): pl.pallas_call(functools.partial(kernel, names), out_shape=[jax.ShapeDtyp...  407 us

profile of v3, /device:TPU:0, one launch (start us, length us, event | category | flops | bytes accessed | tf_op | source)
XLA Modules:
  0.0 415.7 jit_solution(16431906466733346)
XLA Ops:
  0.7 0.7 convert_bitcast_fusion
  1.3 0.1 copy.50
  1.4 0.7 copy.49
  2.2 0.6 pad.8.refs_3_
  2.8 0.6 pad.9.refs_4_
  3.4 2.0 copy.52.refs_0_
  5.3 200.3 %forward.1 = (bf16[4,2,2,48,768]{4,3,2,1,0:T(8,128)(2,1)}, bf16[3,4,2,2,48,3072]{5,4,3,2,1,0:T(8,128)(2,1)}, bf16[3,4,2,2,48,3072]{5,4,3,2,1,0:T(8,128)(2,1)}, b...) custom-call(bf16[2,196,768]{2,1,0:T(8,128)(2,1)} %copy.52.refs_0_, ...), custom_call_target="tpu_custom_call" | custom-call | tf_op jit(solution)/shard_map/forward/pallas_call | solution.py:699
  205.7 1.2 slice.10
  206.8 189.6 %backward.1 = (f32[6,2,24,1536]{3,2,1,0:T(8,128)}, f32[2,24,768]{2,1,0:T(8,128)}, f32[2,24,384]{2,1,0:T(8,128)}, f32[4,2,2,2,56,128]{5,4,3,2,1,0:T(8,128)}, bf16[4,2,2,2,208,128]{5,4,3,2,1,0:T(8,128)(2,1)}) custom-call(bf16[2,196,768]{2,1,0:T(8,128)(2,1)} %copy.52.refs_0_, f32[213,768]{1,0:T(8,128)} %refs_15_.1, f32[8,768]{1,0:T(8,128)} %get-tuple-element.70.refs_2_, ...), custom_call_target="tpu_custom_call" | custom-call | tf_op jit(solution)/shard_map/backward/pallas_call | solution.py:699
  396.4 17.6 %update.1 = (f32[24,768]{1,0:T(8,128)}, f32[24,768]{1,0:T(8,128)}, f32[24,768]{1,0:T(8,128)}, f32[3,24,2304]{2,1,0:T(8,128)}, f32[3,24,2304]{2,1,0:T(8,128)}, /*...) custom-call(f32[24,768]{1,0:T(8,128)} %refs_0_.3, ...), custom_call_target="tpu_custom_call" | custom-call | tf_op jit(solution)/shard_map/update/pallas_call | solution.py:699
  414.0 1.3 fusion

commit v4 on v3

--- a/solution.py
+++ b/solution.py
@@ -151,6 +151,7 @@
         self.width = block.shape[-1]
         self.other = other_part(self.width)
         self.most = self.width - self.other
+        self.cut = (self.most // 2 + 127) // 128 * 128
 
     def region(self, z, x, y, start, width):
         if self.by_cols:
@@ -165,7 +166,7 @@
         z, x, y, to = self.z, self.x, self.y, self.to
         z1, z3, line = jnp.bitwise_xor(z, 1), jnp.bitwise_xor(z, 3), slice(None)
         most, other, region = self.most, self.other, self.region
-        cut, cut_other = cut_of(most), most + max(cut_of(other), 128)
+        cut, cut_other = self.cut, most + max(cut_of(other), 128)
         landed = at
         if at in (0, 1):
             src, dst = self.part(0, most), region(z, x, y, 0, most)
@@ -439,7 +440,6 @@
     r.patch_f[mine] = r.patch[:, part(c, D // 2)]
     r.joined_b[:, mine] = r.joined_f[:, :, part(c, WIDTH)]
     r.expand_b[:, mine] = r.expand[:, :, part(c, WIDTH)]
-    r.shrink_block[...] = r.shrink[...].astype(BF)
     for copy, src, dst in zip(
         copies,
         (r.patch_f, r.joined_b, r.expand_b),
@@ -451,16 +451,24 @@
         copy.wait_send()
 
 
+def class_column(ref, kind):
+    line = lax.broadcasted_iota(jnp.int32, (HEAD_ROWS, 1), 0)
+    column = jnp.zeros((HEAD_ROWS, 1), kind)
+    for image in range(ref.shape[0]):
+        column = jnp.where(line == image, ref[image].astype(kind), column)
+    return column
+
+
 def head_part(r, first, image_total):
-    table = r.head[:D].astype(BF)
+    table = r.table[...]
     gain, shift = r.vectors[FINAL : FINAL + 1], r.vectors[FINAL + 1 : FINAL + 2]
     feature = normalize(first, gain, shift).astype(BF)
     logits = dot(feature, table) + r.head[D : D + 1]
     ids = lax.broadcasted_iota(jnp.int32, logits.shape, 1)
     shifted = logits - jnp.max(logits, -1, keepdims=True)
     log_prob = shifted - jnp.log(jnp.sum(jnp.exp(shifted), -1, keepdims=True))
-    target = jnp.where(ids == r.labels[...], 1.0 - SMOOTH, 0.0) + SMOOTH / CLASSES
-    weights = r.weights[...]
+    target = jnp.where(ids == class_column(r.labels, jnp.int32), 1.0 - SMOOTH, 0.0) + SMOOTH / CLASSES
+    weights = class_column(r.mask, F32)
     loss = jnp.sum(weights * -jnp.sum(target * log_prob, -1, keepdims=True))
     d_logits = ((weights / image_total) * (jnp.exp(log_prob) - target)).astype(BF)
     d_feature = dot(d_logits, table, NT)
@@ -476,6 +484,80 @@
     r.tail[2:3] = d_shift
 
 
+def top_backward(plan, r):
+    images = r.images.shape[0]
+    base = S + 2 + 4 * TOP
+    g = r.top_f[:, G_]
+    g_low = g.astype(BF)
+    for j in range(4):
+        cols = slice(j * D, j * D + D)
+        dz = dot(g_low, r.shrink_w[j].reshape(D, D), NT)
+        r.top_du[:, cols] = (dz * r.top_f[:, cols]).astype(BF)
+    d_m = jnp.zeros((HEAD_ROWS, D), F32)
+    for j in range(4):
+        d_m = d_m + dot(r.top_du[:, j * D : j * D + D], weight(r.expand_w, j * D, D), NT)
+    d_h1, d_gain, d_shift = normalize_back(r.top_f[:, H1_], row(r.vectors, base + 2), d_m)
+    r.tail[5:6] = d_gain
+    r.tail[6:7] = d_shift
+    g1 = g + d_h1
+    g1_low = g1.astype(BF)
+    d_o = dot(g1_low, weight(r.joined_w, 3 * D, D), NT).astype(BF).astype(F32)
+    query = r.top_b[:, Q_].astype(F32)
+    r.class_row[...] = jnp.zeros_like(r.class_row)
+    for image in range(images):
+        rows = slice(image * PAD, image * PAD + PAD)
+        mine, spread_o = by_head(d_o, image)
+        _, spread_q = by_head(query, image)
+        spread_o, spread_q = spread_o.astype(BF), spread_q.astype(BF)
+        p_low = r.top_p[image]
+        p = p_low.astype(F32)
+        r.d_keys[rows, D:] = dot(p_low, spread_o).astype(BF)
+        dp = dot(r.t[rows, 2 * D :], spread_o, NT)
+        ds = (p * (dp - jnp.sum(p * dp, 0, keepdims=True))).astype(BF)
+        r.d_keys[rows, :D] = (dot(ds, spread_q) * HEAD_DIM**-0.5).astype(BF)
+        d_q = jnp.where(mine, dot(ds, r.t[rows, D : 2 * D], TN), 0.0)
+        r.class_row[image : image + 1] = jnp.sum(d_q, 0, keepdims=True) * HEAD_DIM**-0.5
+    for part in range(2):
+        value = dot(r.a[...], r.d_keys[:, part * D : part * D + D], TN)
+        store_cols(plan, r.keys_block, 0, part, D, value, D, 1)
+    keys = load(r.keys_block, r.keys_out, r.loads.at[0])
+    d_q = r.class_row[...].astype(BF)
+    r.g[...] = dot(r.d_keys[:, :D], weight(r.joined_w, D, D), NT)
+    r.g[...] += dot(r.d_keys[:, D:], weight(r.joined_w, 2 * D, D), NT)
+    d_a = dot(d_q, weight(r.joined_w, 0, D), NT)
+    for image in range(images):
+        r.g[image * PAD : image * PAD + 1] += d_a[image : image + 1]
+    d_h, d_gain, d_shift = normalize_back(r.h[...], row(r.vectors, base), r.g[...])
+    r.g[...] = d_h
+    for image in range(images):
+        r.g[image * PAD : image * PAD + 1] += g1[image : image + 1]
+    r.tail[3:4] = d_gain
+    r.tail[4:5] = d_shift
+    sources = (
+        r.top_b[:, FEATURE_],
+        r.top_b[:, LOGIT_],
+        r.top_b[:, Z_],
+        g_low,
+        r.top_b[:, M_],
+        r.top_du[...],
+        r.top_b[:, O_],
+        g1_low,
+        r.top_b[:, A_],
+        d_q,
+    )
+    r.rows_f[...] = jnp.zeros_like(r.rows_f)
+    first = 0
+    for source in sources:
+        value = source.astype(F32)
+        for j in range(value.shape[1] // 128):
+            for image in range(images):
+                at = image * PER_IMAGE + first + j
+                r.rows_f[at : at + 1] = value[image : image + 1, j * 128 : j * 128 + 128]
+        first += value.shape[1] // 128
+    r.rows_block[...] = r.rows_f[...].astype(BF)
+    keys.wait()
+
+
 def forward_kernel(plan, names, *refs):
     r = SimpleNamespace(**dict(zip(names, refs)))
     cube = plan.cube
@@ -486,8 +568,9 @@
     if cube:
         blocks = (r.patch_block, r.joined_block, r.expand_block, r.shrink_block)
         cube_barrier(plan)
+        r.shrink_block[...] = r.shrink[...].astype(BF)
         share_shards(plan, r)
-        r.count[...] = jnp.full((8, 128), jnp.sum(r.weights[...]), F32)
+        r.count[...] = jnp.full((8, 128), jnp.sum(class_column(r.mask, F32)), F32)
         counting = SmallGather(plan, r.count, r.counts, r.count_send, r.count_recv)
 
     def unit(kind, layer):
@@ -528,6 +611,7 @@
         first[2].stage2()
         first[1].stage3()
         first[0].stage4()
+    r.table[...] = r.head[:D].astype(BF)
     ready(patch, 0).wait()
     for image in range(images):
         at = image * PAD
@@ -691,6 +775,7 @@
     else:
         image_total = r.count_in[0:1, 0:1]
     head_part(r, last, image_total)
+    top_backward(plan, r)
     wait_all(saves(TOP, h_, a_, t_) + saves(0, z_, slope_))
 
 
@@ -720,7 +805,7 @@
     return {name: pltpu.SemaphoreType.DMA(count) for name, count in counts.items()}
 
 
-def forward(plan, shards, args, gathered, count):
+def forward(plan, shards, args, scalars, gathered, count):
     rows = args["images"].shape[0] * PAD
     shapes = saved_shapes(rows)
     whole = dict(
@@ -730,6 +815,7 @@
         shrink_whole=(LAYERS,) + ROWS_SHAPE,
     )
     inputs = given_in(VMEM_SPEC, **args)
+    inputs.update(given_in(pl.BlockSpec(memory_space=pltpu.SMEM), **scalars))
     outputs = {}
     if plan.cube:
         inputs.update(given_in(VMEM_SPEC, **shards))
@@ -741,21 +827,36 @@
         deep = LAYERS if name in ("h", "a", "t") else TOP
         outputs["keep_" + name] = ((deep,) + shape, kind, ANY_SPEC)
     outputs.update(
-        top_b=((HEAD_ROWS, LOGIT_.stop), BF, VMEM_SPEC),
-        top_f=((HEAD_ROWS, G_.stop), F32, VMEM_SPEC),
-        top_p=((rows // PAD, PAD, 16), BF, VMEM_SPEC),
+        g=((rows, D), F32, VMEM_SPEC),
+        rows_block=((rows_block(rows // PAD), 128), BF, VMEM_SPEC),
+        keys_out=((2, 4, 4, BLOCK, D), BF, ANY_SPEC),
         tail=((8, D), F32, VMEM_SPEC),
         total=((8, 128), F32, VMEM_SPEC),
     )
     scratch = vmem(
         BF,
+        table=(D, CLASSES),
+        top_b=(HEAD_ROWS, LOGIT_.stop),
+        top_p=(rows // PAD, PAD, 16),
+        top_du=(HEAD_ROWS, FF),
+        d_keys=(rows, 2 * D),
+        keys_block=(2, 4, 4, BLOCK, D),
         patch_w=cols_shape(D),
         joined_w=cols_shape(FF),
         expand_w=cols_shape(FF),
         shrink_w=ROWS_SHAPE,
     )
     scratch.update({name: pltpu.VMEM(shape, kind) for name, (shape, kind) in shapes.items()})
-    scratch.update(vmem(F32, first=(HEAD_ROWS, D), class_row=(HEAD_ROWS, D), d_logits=(HEAD_ROWS, CLASS_PAD)))
+    scratch.update(
+        vmem(
+            F32,
+            first=(HEAD_ROWS, D),
+            class_row=(HEAD_ROWS, D),
+            d_logits=(HEAD_ROWS, CLASS_PAD),
+            top_f=(HEAD_ROWS, G_.stop),
+            rows_f=(rows_block(rows // PAD), 128),
+        )
+    )
     scratch.update(dma(saves=(9,), loads=(4,)))
     extra = {}
     if plan.cube:
@@ -803,19 +904,19 @@
     return c, (z * 2 + x) * 2 + y
 
 
-def place(plan, slot, core, chip):
+def place(plan, slot, core, chip, send=SEND):
     my_core, my_chip = relative(plan)
     at = jnp.bitwise_xor(my_chip, chip)
     other = jnp.bitwise_xor(my_core, core)
-    return slot + (SEND - slot) * other, at // 4, at % 4
-
-
-def store_cols(plan, out, slot, tile, width, value, half=WIDTH):
+    return slot + (send - slot) * other, at // 4, at % 4
+
+
+def store_cols(plan, out, slot, tile, width, value, half=WIDTH, send=SEND):
     per_half = half // width
     lanes = pl.ds(pl.multiple_of((tile % per_half) * width, 128), width)
     for b in range(16):
         rows = value[b * BLOCK : (b + 1) * BLOCK].astype(BF)
-        out[(*place(plan, slot, tile // per_half, b), slice(None), lanes)] = rows
+        out[(*place(plan, slot, tile // per_half, b, send), slice(None), lanes)] = rows
 
 
 def store_rows(plan, out, slot, tile, value):
@@ -1097,14 +1198,19 @@
         for k in which:
             fetch(k, layer).wait()
 
-    start(TOP, shrink_, expand_, t_, a_, h_)
-    start(TOP - 1, z_, slope_, m_, h1_, o_, p_)
+    loaded = [
+        load(r.g_in, r.g, r.loads.at[joined_ + 1]),
+        load(r.keys_in.at[0], r.unit.at[0, :, :, :, pl.ds(0, KEYS)], r.loads.at[joined_ + 2]),
+        load(r.keys_in.at[1], r.unit.at[SEND, :, :, :, pl.ds(0, KEYS)], r.loads.at[joined_ + 3]),
+    ]
+    start(TOP - 1, *range(joined_))
     if cube:
         cube_barrier(plan)
         r.squares[...] = jnp.zeros_like(r.squares)
         top_rows = SmallGather(plan, r.rows_block, r.top_rows, r.rows_send, r.rows_recv)
     r.vectors[...] = jnp.zeros_like(r.vectors)
     r.vectors[FINAL : FINAL + 2] = r.tail_in[1:3]
+    r.vectors[FINAL - 4 : FINAL] = r.tail_in[3:7]
 
     def run(unit, stage, by_rows, width=WIDTH):
         unit = Reduce(plan, r, unit, width)
@@ -1165,49 +1271,10 @@
     low_lane = lax.broadcasted_iota(jnp.int32, (PAD, 128), 1) < HEAD_DIM
     scale = HEAD_DIM**-0.5
 
-    base = S + 2 + 4 * TOP
-    g = r.top_f[:, G_]
-    g_low = g.astype(BF)
-    wait(TOP, shrink_)
-    for j in range(4):
-        cols = slice(j * D, j * D + D)
-        dz = dot(g_low, r.shrink_w[j].reshape(D, D), NT)
-        r.top_du[:, cols] = (dz * r.top_f[:, cols]).astype(BF)
-    start(TOP - 1, shrink_)
-    wait(TOP, expand_)
-    d_m = jnp.zeros((HEAD_ROWS, D), F32)
-    for j in range(4):
-        d_m = d_m + dot(r.top_du[:, j * D : j * D + D], weight(r.expand_w, j * D, D), NT)
-    start(TOP, joined_)
-    d_h1, d_gain, d_shift = normalize_back(r.top_f[:, H1_], row(r.params, base + 2), d_m)
-    r.vectors[base + 2 : base + 3] = d_gain
-    r.vectors[base + 3 : base + 4] = d_shift
-    g1 = g + d_h1
-    g1_low = g1.astype(BF)
-    wait(TOP, joined_)
-    d_o = dot(g1_low, weight(r.expand_w, 3 * D, D), NT).astype(BF).astype(F32)
-    query = r.top_b[:, Q_].astype(F32)
-    wait(TOP, t_, a_, h_)
-    r.class_row[...] = jnp.zeros_like(r.class_row)
-    for image in range(images):
-        rows = slice(image * PAD, image * PAD + PAD)
-        mine, spread_o = by_head(d_o, image)
-        _, spread_q = by_head(query, image)
-        spread_o, spread_q = spread_o.astype(BF), spread_q.astype(BF)
-        p_low = r.top_p[image]
-        p = p_low.astype(F32)
-        r.dt[rows, 2 * D :] = dot(p_low, spread_o).astype(BF)
-        dp = dot(r.vm_t[rows, 2 * D :], spread_o, NT)
-        ds = (p * (dp - jnp.sum(p * dp, 0, keepdims=True))).astype(BF)
-        r.dt[rows, D : 2 * D] = (dot(ds, spread_q) * HEAD_DIM**-0.5).astype(BF)
-        d_q = jnp.where(mine, dot(ds, r.vm_t[rows, D : 2 * D], TN), 0.0)
-        r.class_row[image : image + 1] = jnp.sum(d_q, 0, keepdims=True) * HEAD_DIM**-0.5
-    start(TOP - 1, t_)
-    for part in range(2):
-        value = dot(r.vm_a[...], r.dt[:, (part + 1) * D : (part + 2) * D], TN)
-        store_cols(plan, r.unit, 0, part, KEYS, value, KEYS)
+    wait_all(loaded)
     if cube:
         run(jnp.int32(0), 0, False, KEYS)
+        top_rows.stage0()
     else:
         copies = [
             pltpu.make_async_copy(r.unit.at[(0, SEND)[i]], r.full.at[0, i], r.loads.at[joined_ + 1 + i])
@@ -1215,48 +1282,6 @@
         ]
         start_all(copies)
         wait_all(copies)
-    start(TOP - 1, a_)
-    d_q = r.class_row[...].astype(BF)
-    sources = (
-        r.top_b[:, FEATURE_],
-        r.top_b[:, LOGIT_],
-        r.top_b[:, Z_],
-        g_low,
-        r.top_b[:, M_],
-        r.top_du[...],
-        r.top_b[:, O_],
-        g1_low,
-        r.top_b[:, A_],
-        d_q,
-    )
-    r.rows_f[...] = jnp.zeros_like(r.rows_f)
-    first = 0
-    for source in sources:
-        value = source.astype(F32)
-        for j in range(value.shape[1] // 128):
-            for image in range(images):
-                at = image * PER_IMAGE + first + j
-                r.rows_f[at : at + 1] = value[image : image + 1, j * 128 : j * 128 + 128]
-        first += value.shape[1] // 128
-    r.rows_block[...] = r.rows_f[...].astype(BF)
-    if cube:
-        top_rows.stage0()
-    else:
-        save = load(r.rows_block, r.top_rows, r.loads.at[joined_ + 1])
-        save.wait()
-    r.g1[...] = dot(r.dt[:, D : 2 * D], weight(r.expand_w, D, D), NT)
-    r.g1[...] += dot(r.dt[:, 2 * D :], weight(r.expand_w, 2 * D, D), NT)
-    d_a = dot(d_q, weight(r.expand_w, 0, D), NT)
-    for image in range(images):
-        r.g1[image * PAD : image * PAD + 1] += d_a[image : image + 1]
-    start(TOP - 1, expand_)
-    d_h, d_gain, d_shift = normalize_back(r.vm_h[...], row(r.params, base), r.g1[...])
-    r.g[...] = d_h
-    for image in range(images):
-        r.g[image * PAD : image * PAD + 1] += g1[image : image + 1]
-    r.vectors[base : base + 1] = d_gain
-    r.vectors[base + 1 : base + 2] = d_shift
-    start(TOP - 1, h_)
 
     @pl.loop(1, LAYERS)
     def _(it):
@@ -1396,10 +1421,15 @@
     store_vectors(plan, r.unit, slot, r.vectors[...])
 
     drain()
-    r.tail_block[:BLOCK] = r.total[UNITS % 2, :, D // 2 : TAIL]
-    line = lax.broadcasted_iota(jnp.int32, (8, 128), 0)
-    squares, loss = jnp.sum(r.squares[...]), r.tail_in[0:1, 0:128]
-    r.tail_block[BLOCK:] = jnp.where(line == 0, squares, jnp.where(line == 1, loss, 0.0))
+    r.tail_block[:BLOCK] = r.total[UNITS % 2, :, D // 2 : TAIL].astype(BF)
+    line = lax.broadcasted_iota(jnp.int32, (16, 128), 0)
+    terms = jnp.zeros((16, 128), F32)
+    for k, rest in enumerate((jnp.full((16, 128), jnp.sum(r.squares[...]), F32), r.tail_in[0:1, 0:128])):
+        for j in range(3):
+            term = rest.astype(BF).astype(F32)
+            rest = rest - term
+            terms = jnp.where(line == 3 * k + j, term, terms)
+    r.tail_block[BLOCK:] = terms.astype(BF)
     gather = SmallGather(plan, r.tail_block, r.vector_rows, r.tail_send, r.tail_recv)
     gather.stage0()
     gather.stage1()
@@ -1418,14 +1448,14 @@
         images=images,
         params=params,
         tail_in=done.tail,
-        top_b=done.top_b,
-        top_f=done.top_f,
-        top_p=done.top_p,
+        rows_block=done.rows_block,
     )
     block = rows_block(images.shape[0])
     inputs.update(
         given_in(
             ANY_SPEC,
+            g_in=done.g,
+            keys_in=done.keys_out,
             joined_whole=done.joined_whole,
             expand_whole=done.expand_whole,
             shrink_whole=done.shrink_whole,
@@ -1437,14 +1467,13 @@
             owned=((UNITS - 1, 2, HALF, WIDTH), F32, ANY_SPEC),
             keys=((2, HALF, KEYS), F32, ANY_SPEC),
             patch=((2, HALF, D // 2), F32, ANY_SPEC),
-            vector_rows=(CHIPS + (2, BLOCK + 8, 128), F32, ANY_SPEC),
+            vector_rows=(CHIPS + (2, BLOCK + 16, 128), BF, ANY_SPEC),
             top_rows=(CHIPS + (2, block, 128), BF, ANY_SPEC),
         )
     else:
         outputs = dict(
             full=((UNITS + 1, 2, 4, 4, BLOCK, WIDTH), BF, ANY_SPEC),
             vector_rows=((VEC_ROWS, D), F32, ANY_SPEC),
-            top_rows=((block, 128), BF, ANY_SPEC),
         )
     scratch = {"vm_" + name: pltpu.VMEM(shape, kind) for name, (shape, kind) in shapes.items()}
     scratch.update(
@@ -1456,21 +1485,10 @@
             do=(rows, D),
             dt=(rows, 3 * D),
             unit=(SEND + 1, 4, 4, BLOCK, WIDTH),
-            top_du=(HEAD_ROWS, FF),
-            rows_block=(block, 128),
         )
     )
-    scratch.update(
-        vmem(
-            F32,
-            g=(rows, D),
-            g1=(rows, D),
-            vectors=(VEC_ROWS, D),
-            class_row=(HEAD_ROWS, D),
-            rows_f=(block, 128),
-        )
-    )
-    scratch.update(dma(loads=(15,)))
+    scratch.update(vmem(F32, g=(rows, D), g1=(rows, D), vectors=(VEC_ROWS, D)))
+    scratch.update(dma(loads=(16,)))
     extra = {}
     if plan.cube:
         other = other_part(WIDTH)
@@ -1479,6 +1497,7 @@
             vmem(
                 BF,
                 core=(4, 4, BLOCK, WIDTH),
+                tail_block=(BLOCK + 16, 128),
                 near=(3, 4, BLOCK, cut_of(most)),
                 far=(3, 4, BLOCK, most - cut_of(most)),
                 x=(3, 4, BLOCK, most),
@@ -1496,7 +1515,7 @@
             )
         )
         scratch.update(
-            vmem(F32, total=(2, BLOCK, WIDTH), squares=(8, WIDTH), tail_block=(BLOCK + 8, 128))
+            vmem(F32, total=(2, BLOCK, WIDTH), squares=(8, WIDTH))
         )
         scratch.update(
             dma(send=(4, 20), recv=(4, 18), rows_send=(7,), rows_recv=(7,), tail_send=(7,), tail_recv=(7,))
@@ -1566,7 +1585,9 @@
     for group in order:
         start_all(moves(group, False))
 
-    tile = jnp.sum(r.tails[:, BLOCK:, :], 0)
+    tile = jnp.sum(r.tails[:, BLOCK:, :].astype(F32), 0)
+    square_sum = tile[0:1, 0:1] + tile[1:2, 0:1] + tile[2:3, 0:1]
+    loss = tile[3:4] + tile[4:5] + tile[5:6]
     r.rows_f[...] = r.top_rows[...].astype(F32)
     stride = r.top_rows.shape[0] // plan.n
     found = class_matrices(r.rows_f, images, plan.n, stride)
@@ -1576,7 +1597,7 @@
     alike = (dot(features, features, NT) + 1.0) * dot(d_logits, d_logits, NT)
     for left, right in ((z, g), (m, du), (o, g1), (a, dq)):
         alike = alike + dot(left, left, NT) * dot(right, right, NT)
-    norm = jnp.sqrt(tile[0:1, 0:1] + jnp.sum(alike))
+    norm = jnp.sqrt(square_sum + jnp.sum(alike))
     me = plan.me()
 
     def top_grad(left, right, rows):
@@ -1584,7 +1605,7 @@
 
     clip = CLIP / jnp.maximum(norm, CLIP)
     line = lax.broadcasted_iota(jnp.int32, (8, 128), 0)
-    r.scalars[...] = jnp.where(line == 0, norm, tile[1:2])
+    r.scalars[...] = jnp.where(line == 0, norm, loss)
 
     def step(group, at, gradient, rate):
         bufs = [buf for _, buf, _ in groups[group]]
@@ -1654,8 +1675,9 @@
     finish(patch)
     count = groups[vector][0][0].shape[0]
     for d in range(-(-count // 8)):
+        block = r.tails[d].astype(F32)
         for j in range(6):
-            r.vector_grad[8 * d : 8 * d + 8, 128 * j : 128 * j + 128] = r.tails[d, 8 * j : 8 * j + 8, :]
+            r.vector_grad[8 * d : 8 * d + 8, 128 * j : 128 * j + 128] = block[8 * j : 8 * j + 8]
     wait_all(moves(vector, False))
     step(vector, (every, every), r.vector_grad[:count], RATE_VECTOR)
     finish(vector)
@@ -1675,7 +1697,7 @@
             VMEM_SPEC,
             owned=got.owned,
             patch_grad=got.patch,
-            tails=got.vector_rows.reshape(plan.n, BLOCK + 8, 128),
+            tails=got.vector_rows.reshape(plan.n, BLOCK + 16, 128),
             keys=got.keys,
             top_rows=got.top_rows.reshape(-1, 128),
         )
@@ -1706,7 +1728,7 @@
 
     shrink = layers[:, 0].reshape(TOP, 2, 16, BLOCK, 2, D).transpose(0, 2, 1, 4, 3, 5)
     joined = scattered(from_cols(layers[:, 2]))
-    rows_all = lax.all_gather(got.top_rows, AXES, axis=0)[:, : PER_IMAGE * images]
+    rows_all = lax.all_gather(done.rows_block, AXES, axis=0)[:, : PER_IMAGE * images]
     rows_all = rows_all.reshape(plan.n * images, PER_IMAGE * 128)
     ends = [sum(PIECES[: k + 1]) for k in range(len(PIECES))]
     features, d_logits, z, g, m, du, o, g1, a, dq = jnp.split(rows_all, ends[:-1], axis=1)
@@ -1748,18 +1770,12 @@
     states = [params[3 * k : 3 * k + 3] for k in range(7)]
     patch, triple, output, expand, shrink, vector, head = (state[0] for state in states)
     count = images.shape[0]
-    pad_rows = ((0, HEAD_ROWS - count), (0, 0))
     weights = slot_mask.astype(F32)
-    args = dict(
-        images=images,
-        vectors=vector,
-        head=head,
-        labels=jnp.pad(labels[:, None], pad_rows),
-        weights=jnp.pad(weights[:, None], pad_rows),
-    )
+    args = dict(images=images, vectors=vector, head=head)
+    scalars = dict(labels=labels, mask=slot_mask)
     if plan.cube:
         shards = dict(patch=patch, triple=triple, output=output, expand=expand, shrink=shrink)
-        done = forward(plan, shards, args, None, None)
+        done = forward(plan, shards, args, scalars, None, None)
     else:
 
         def whole(shard, shape):
@@ -1774,7 +1790,7 @@
             whole(shrink, ROWS_SHAPE),
         ]
         total = jnp.full((8, 128), lax.psum(jnp.sum(weights), AXES), F32)
-        done = forward(plan, None, args, gathered, total)
+        done = forward(plan, None, args, scalars, gathered, total)
     got = backward(plan, images, vector, done)
     if plan.cube:
         norm, loss, states, bias_grad = update(plan, count, states, got)

time: 422 us -> 406 us (0.962); the launches traced: 416 us -> 406 us
  Pallas kernels: 407 us -> 401 us
    pallas_call x3, Pallas kernels: 407 us -> 401 us  [pallas(): pl.pallas_call(functools.partial(kernel, names), out_shape=[jax.ShapeDtyp...]
where the time goes in v4:
time: 406 us
  Pallas kernels  401 us (99%)
  local copies, waits for them, and re-layouts  4.41 us (1%)
    pallas_call x3, Pallas kernels, pallas(): pl.pallas_call(functools.partial(kernel, names), out_shape=[jax.ShapeDtyp...  401 us

profile of v4, /device:TPU:0, one launch (start us, length us, event | category | flops | bytes accessed | tf_op | source)
XLA Modules:
  0.0 405.8 jit_solution(16535410019909767554)
XLA Ops:
  0.7 2.0 copy.50.refs_0_
  2.6 208.1 %forward.1 = (bf16[4,2,2,48,768]{4,3,2,1,0:T(8,128)(2,1)}, bf16[3,4,2,2,48,3072]{5,4,3,2,1,0:T(8,128)(2,1)}, bf16[3,4,2,2,48,3072]{5,4,3,2,1,0:T(8,128)(2,1)}, b...) custom-call(bf16[2,196,768]{2,1,0:T(8,128)(2,1)} %copy.50.refs_0_, ...), custom_call_target="tpu_custom_call" | custom-call | tf_op jit(solution)/shard_map/forward/pallas_call | solution.py:784
  210.7 1.2 slice.10
  211.9 175.1 %backward.1 = (f32[6,2,24,1536]{3,2,1,0:T(8,128)}, f32[2,24,768]{2,1,0:T(8,128)}, f32[2,24,384]{2,1,0:T(8,128)}, bf16[4,2,2,2,64,128]{5,4,3,2,1,0:T(8,128)(2,1)}, bf16[4,2,2,2,208,128]{5,4,3,2,1,0:T(8,128)(2,1)}) custom-call(bf16[2,196,768]{2,1,0:T(8,128)(2,1)} %copy.50.refs_0_, f32[213,768]{1,0:T(8,128)} %refs_15_.1, f32[8,768]{1,0:T(8,128)} %get-tuple-element.70.refs_2_, ...), custom_call_target="tpu_custom_call" | custom-call | tf_op jit(solution)/shard_map/backward/pallas_call | solution.py:784
  387.1 17.5 %update.1 = (f32[24,768]{1,0:T(8,128)}, f32[24,768]{1,0:T(8,128)}, f32[24,768]{1,0:T(8,128)}, f32[3,24,2304]{2,1,0:T(8,128)}, f32[3,24,2304]{2,1,0:T(8,128)}, /*...) custom-call(f32[24,768]{1,0:T(8,128)} %refs_0_.3, ...), custom_call_target="tpu_custom_call" | custom-call | tf_op jit(solution)/shard_map/update/pallas_call | solution.py:784
  404.5 1.3 fusion

commit v5 on v4

--- a/solution.py
+++ b/solution.py
@@ -267,12 +267,8 @@
 def cube_barrier(plan):
     z, x, y, c = plan.where()
     barrier = pltpu.get_barrier_semaphore()
-    partners = [(jnp.bitwise_xor(z, k) * 2 + x, y * 2 + c) for k in (1, 2, 3)]
-    partners += [
-        (z * 2 + 1 - x, y * 2 + c),
-        (z * 2 + x, (1 - y) * 2 + c),
-        (z * 2 + x, y * 2 + 1 - c),
-    ]
+    partners = [(jnp.bitwise_xor(z * 2 + x, k), y * 2 + c) for k in range(1, 8)]
+    partners += [(z * 2 + x, (1 - y) * 2 + c), (z * 2 + x, y * 2 + 1 - c)]
     for partner in partners:
         pl.semaphore_signal(barrier, inc=1, device_id=partner, device_id_type=pl.DeviceIdType.MESH)
     pl.semaphore_wait(barrier, len(partners))
@@ -302,58 +298,45 @@
 class SmallGather:
     def __init__(self, plan, block, whole, send, recv):
         self.z, self.x, self.y, self.c = plan.where()
+        self.to = over_links(plan)
         self.block, self.whole, self.send, self.recv = block, whole, send, recv
 
     def copy(self, at):
         z, x, y, c = self.z, self.x, self.y, self.c
         line = slice(None)
-        if at < 3:
+        if at < 7:
             src, dst = self.block, self.whole.at[z, x, y, c]
-            to = (jnp.bitwise_xor(z, at + 1) * 2 + x, y * 2 + c)
-        elif at == 3:
-            src = dst = self.whole.at[line, x, y, c]
-            to = (z * 2 + 1 - x, y * 2 + c)
-        elif at == 4:
+            device = (jnp.bitwise_xor(z * 2 + x, at + 1), y * 2 + c)
+        elif at == 7:
             src = dst = self.whole.at[line, line, y, c]
-            to = (z * 2 + x, (1 - y) * 2 + c)
+            device = self.to.y
         else:
             src = dst = self.whole.at[line, line, line, c]
-            to = (z * 2 + x, y * 2 + 1 - c)
-        return pltpu.make_async_remote_copy(
-            src_ref=src,
-            dst_ref=dst,
-            send_sem=self.send.at[at],
-            recv_sem=self.recv.at[at],
-            device_id=to,
-            device_id_type=pl.DeviceIdType.MESH,
-        )
+            device = self.to.core
+        return remote(src, dst, self.send.at[at], self.recv.at[at], device)
 
     def keep(self):
         here = self.whole.at[self.z, self.x, self.y, self.c]
-        return pltpu.make_async_copy(self.block, here, self.send.at[6])
+        return pltpu.make_async_copy(self.block, here, self.send.at[9])
 
     def stage0(self):
-        for at in range(3):
+        for at in range(7):
             self.copy(at).start()
         self.keep().start()
 
     def stage1(self):
-        for at in range(3):
+        for at in range(7):
             self.copy(at).wait_recv()
         self.keep().wait()
-        self.copy(3).start()
+        self.copy(7).start()
 
     def stage2(self):
-        self.copy(3).wait_recv()
-        self.copy(4).start()
-
-    def stage3(self):
-        self.copy(4).wait_recv()
-        self.copy(5).start()
+        self.copy(7).wait_recv()
+        self.copy(8).start()
 
     def finish(self):
-        self.copy(5).wait_recv()
-        for at in range(6):
+        self.copy(8).wait_recv()
+        for at in range(9):
             self.copy(at).wait_send()
 
 
@@ -440,15 +423,19 @@
     r.patch_f[mine] = r.patch[:, part(c, D // 2)]
     r.joined_b[:, mine] = r.joined_f[:, :, part(c, WIDTH)]
     r.expand_b[:, mine] = r.expand[:, :, part(c, WIDTH)]
-    for copy, src, dst in zip(
-        copies,
-        (r.patch_f, r.joined_b, r.expand_b),
-        (r.patch_block, r.joined_block, r.expand_block),
-    ):
-        copy.wait_recv()
+    targets = (
+        (r.patch_f, r.patch_block),
+        (r.joined_b, r.joined_block),
+        (r.expand_b, r.expand_block),
+    )
+
+    def arrive(which):
+        src, dst = targets[which]
+        copies[which].wait_recv()
         dst[...] = src[...].astype(BF)
-    for copy in copies:
-        copy.wait_send()
+        copies[which].wait_send()
+
+    return arrive
 
 
 def class_column(ref, kind):
@@ -482,6 +469,17 @@
     r.tail[0:1] = jnp.full((1, D), loss, F32)
     r.tail[1:2] = d_gain
     r.tail[2:3] = d_shift
+
+
+def pack_rows(r, kind, *sources):
+    first = sum(PIECES[:kind]) // 128
+    for source in sources:
+        value = source.astype(F32)
+        for j in range(value.shape[1] // 128):
+            for image in range(r.images.shape[0]):
+                at = image * PER_IMAGE + first + j
+                r.rows_f[at : at + 1] = value[image : image + 1, j * 128 : j * 128 + 128]
+        first += value.shape[1] // 128
 
 
 def top_backward(plan, r):
@@ -533,27 +531,11 @@
         r.g[image * PAD : image * PAD + 1] += g1[image : image + 1]
     r.tail[3:4] = d_gain
     r.tail[4:5] = d_shift
-    sources = (
-        r.top_b[:, FEATURE_],
-        r.top_b[:, LOGIT_],
-        r.top_b[:, Z_],
-        g_low,
-        r.top_b[:, M_],
-        r.top_du[...],
-        r.top_b[:, O_],
-        g1_low,
-        r.top_b[:, A_],
-        d_q,
-    )
-    r.rows_f[...] = jnp.zeros_like(r.rows_f)
-    first = 0
-    for source in sources:
-        value = source.astype(F32)
-        for j in range(value.shape[1] // 128):
-            for image in range(images):
-                at = image * PER_IMAGE + first + j
-                r.rows_f[at : at + 1] = value[image : image + 1, j * 128 : j * 128 + 128]
-        first += value.shape[1] // 128
+    pack_rows(r, 0, r.top_b[:, FEATURE_], r.top_b[:, LOGIT_])
+    pack_rows(r, 3, g_low)
+    pack_rows(r, 5, r.top_du[...])
+    pack_rows(r, 7, g1_low)
+    pack_rows(r, 9, d_q)
     r.rows_block[...] = r.rows_f[...].astype(BF)
     keys.wait()
 
@@ -563,13 +545,14 @@
     cube = plan.cube
     images = r.images.shape[0]
     patch, joined, expand, shrink = range(4)
+    pixels = load(r.images_in, r.images, r.loads.at[4])
     wholes = (r.patch_whole, r.joined_whole, r.expand_whole, r.shrink_whole)
     weights = (r.patch_w, r.joined_w, r.expand_w, r.shrink_w)
     if cube:
         blocks = (r.patch_block, r.joined_block, r.expand_block, r.shrink_block)
         cube_barrier(plan)
         r.shrink_block[...] = r.shrink[...].astype(BF)
-        share_shards(plan, r)
+        arrive = share_shards(plan, r)
         r.count[...] = jnp.full((8, 128), jnp.sum(class_column(r.mask, F32)), F32)
         counting = SmallGather(plan, r.count, r.counts, r.count_send, r.count_recv)
 
@@ -595,10 +578,13 @@
 
     if cube:
         first = [unit(patch, 0), unit(joined, 0), unit(expand, 0), unit(shrink, 0), unit(joined, 1)]
+        arrive(0)
         first[0].stage0()
         counting.stage0()
+        arrive(1)
         first[1].stage0()
         first[0].stage1()
+        arrive(2)
         first[2].stage0()
         first[1].stage1()
         first[0].stage2()
@@ -613,6 +599,7 @@
         first[0].stage4()
     r.table[...] = r.head[:D].astype(BF)
     ready(patch, 0).wait()
+    pixels.wait()
     for image in range(images):
         at = image * PAD
         r.h[at : at + 1] = r.vectors[0:1] + r.vectors[S : S + 1]
@@ -681,7 +668,7 @@
             unit(shrink, layer).stage3()
             unit(expand, layer).stage4()
             pl.when(layer == 0)(counting.stage1)
-            pl.when(layer == 1)(counting.stage3)
+            pl.when(layer == 1)(counting.finish)
         r.m[...] = normalize(r.h1[...], row(r.vectors, base + 2), row(r.vectors, base + 3)).astype(BF)
         start_all(saves(layer, m_))
         wait_all(saves(layer, h_))
@@ -710,7 +697,6 @@
             unit(joined, layer + 1).stage3()
             unit(shrink, layer).stage4()
             pl.when(layer == 0)(counting.stage2)
-            pl.when(layer == 1)(counting.finish)
         ready(shrink, layer).wait()
 
         @pl.loop(0, 4)
@@ -764,6 +750,11 @@
         r.top_f[:, cols] = slope
     if cube:
         unit(shrink, TOP).stage4()
+    r.rows_f[...] = jnp.zeros_like(r.rows_f)
+    pack_rows(r, 2, r.top_b[:, Z_])
+    pack_rows(r, 4, r.top_b[:, M_])
+    pack_rows(r, 6, r.top_b[:, O_])
+    pack_rows(r, 8, r.top_b[:, A_])
     ready(shrink, TOP).wait()
     last = h1
     for j in range(4):
@@ -805,8 +796,8 @@
     return {name: pltpu.SemaphoreType.DMA(count) for name, count in counts.items()}
 
 
-def forward(plan, shards, args, scalars, gathered, count):
-    rows = args["images"].shape[0] * PAD
+def forward(plan, images, shards, args, scalars, gathered, count):
+    rows = images.shape[0] * PAD
     shapes = saved_shapes(rows)
     whole = dict(
         patch_whole=cols_shape(D),
@@ -815,6 +806,7 @@
         shrink_whole=(LAYERS,) + ROWS_SHAPE,
     )
     inputs = given_in(VMEM_SPEC, **args)
+    inputs.update(given_in(ANY_SPEC, images_in=images))
     inputs.update(given_in(pl.BlockSpec(memory_space=pltpu.SMEM), **scalars))
     outputs = {}
     if plan.cube:
@@ -836,6 +828,7 @@
     scratch = vmem(
         BF,
         table=(D, CLASSES),
+        images=images.shape,
         top_b=(HEAD_ROWS, LOGIT_.stop),
         top_p=(rows // PAD, PAD, 16),
         top_du=(HEAD_ROWS, FF),
@@ -857,7 +850,7 @@
             rows_f=(rows_block(rows // PAD), 128),
         )
     )
-    scratch.update(dma(saves=(9,), loads=(4,)))
+    scratch.update(dma(saves=(9,), loads=(5,)))
     extra = {}
     if plan.cube:
         scratch.update(
@@ -881,7 +874,7 @@
             )
         )
         scratch.update(
-            dma(send=(10, 23), recv=(10, 22), share_send=(3,), share_recv=(3,), count_send=(7,), count_recv=(7,))
+            dma(send=(10, 23), recv=(10, 22), share_send=(3,), share_recv=(3,), count_send=(10,), count_recv=(9,))
         )
         extra = dict(collective_id=1, has_side_effects=True)
     got = pallas(functools.partial(forward_kernel, plan), "forward", inputs, outputs, scratch, **extra)
@@ -892,7 +885,9 @@
     return got
 
 
-UNITS = 3 * TOP + 1
+UNITS = 4 * TOP + 1
+WIDTHS = (WIDTH, WIDTH, D // 2, 3 * D // 2)
+SHRINK, EXPAND, OUTPUT, TRIPLE = range(4)
 KEYS = D
 TAIL = 512
 SEND = 4
@@ -939,9 +934,9 @@
         self.plan, self.bufs, self.unit, self.width = plan, bufs, unit, width
         self.z, self.x, self.y, self.c = plan.where()
         self.to = over_links(plan)
-        self.other = other_part(width) if width == WIDTH else 0
+        self.other = other_part(width) if width > KEYS else 0
         self.most = width - self.other
-        self.cut, self.cut_other = cut_of(self.most), cut_of(self.other)
+        self.cut, self.cut_other = cut_of(self.most), max(cut_of(self.other), 128)
         self.slot, self.three, self.two = unit % 4, unit % 3, unit % 2
 
     def copy(self, at):
@@ -950,7 +945,7 @@
         line = slice(None)
         full, main = pl.ds(0, self.width), pl.ds(0, most)
         left, right, low = pl.ds(0, cut), pl.ds(cut, most - cut), pl.ds(0, most - cut)
-        other = pl.ds(most, self.other)
+        other, all_other = pl.ds(most, self.other), pl.ds(0, self.other)
         own = b.unit.at[slot]
         if at == 17:
             rows = pl.ds(pl.multiple_of((1 - c) * HALF, 8), HALF)
@@ -967,31 +962,35 @@
                 6: lambda: (b.line.at[three, 2, :, main], b.main_two.at[three, 1, :, main], to.z3),
                 7: lambda: (b.line.at[three, 1, :, main], b.main_one.at[slot, 0, :, main], to.z1),
                 8: lambda: (b.line.at[three, 3, :, main], b.main_one.at[slot, 1, :, main], to.z3),
-                9: lambda: (own.at[2, :, :, other], b.other_two.at[three, 0], to.z1),
-                10: lambda: (own.at[2, :, :, other], b.other_two.at[three, 1], to.z3),
-                11: lambda: (own.at[1, :, :, other], b.other_one.at[slot, 0], to.z1),
-                12: lambda: (own.at[3, :, :, other], b.other_one.at[slot, 1], to.z3),
+                9: lambda: (own.at[2, :, :, other], b.other_two.at[three, 0, :, :, all_other], to.z1),
+                10: lambda: (own.at[2, :, :, other], b.other_two.at[three, 1, :, :, all_other], to.z3),
+                11: lambda: (own.at[1, :, :, other], b.other_one.at[slot, 0, :, :, all_other], to.z1),
+                12: lambda: (own.at[3, :, :, other], b.other_one.at[slot, 1, :, :, all_other], to.z3),
                 13: lambda: (b.plane.at[three, 3, :, pl.ds(0, cut_other)], b.other_near.at[three], to.x),
                 14: lambda: (b.plane.at[three, 3, :, pl.ds(cut_other, cut_other)], b.other_far.at[three], to.y),
-                15: lambda: (b.plane.at[three, 1], b.other_y.at[three], to.y),
-                16: lambda: (b.plane.at[three, 2], b.other_x.at[three], to.x),
+                15: lambda: (b.plane.at[three, 1, :, all_other], b.other_y.at[three, :, all_other], to.y),
+                16: lambda: (b.plane.at[three, 2, :, all_other], b.other_x.at[three, :, all_other], to.x),
             }[at]()
         return remote(src, dst, b.send.at[slot, at], b.recv.at[slot, at], device)
 
     def result(self, rows):
         b, c = self.bufs, self.c
-        total = b.total.at[self.two]
+        total, at = b.total.at[self.two], (self.unit - 1) // 4
         if self.width == WIDTH:
-            return total.at[rows], b.owned.at[self.unit - 1, c]
+            return total.at[rows], b.expand_grad.at[at, c]
+        if self.width == TAIL:
+            return total.at[rows, pl.ds(0, D // 2)], b.patch.at[c]
+        total = total.at[rows, pl.ds(0, self.width)]
         if self.width == KEYS:
-            return total.at[rows, pl.ds(0, KEYS)], b.keys.at[c]
-        return total.at[rows, pl.ds(0, D // 2)], b.patch.at[c]
+            return total, b.keys.at[c]
+        return total, (b.output_grad if self.width == WIDTHS[OUTPUT] else b.triple_grad).at[at, c]
 
     def own(self, by_rows):
         b, c = self.bufs, self.c
         total = b.total.at[self.two]
         if by_rows:
-            moves = [(total.at[pl.ds(k * HALF, HALF)], b.owned.at[self.unit - 1, k]) for k in range(2)]
+            at = (self.unit - 1) // 4
+            moves = [(total.at[pl.ds(k * HALF, HALF)], b.shrink_grad.at[at, k]) for k in range(2)]
         else:
             moves = [self.result(pl.ds(pl.multiple_of(c * HALF, 8), HALF))]
         return [
@@ -1011,6 +1010,9 @@
         for at in which:
             self.copy(at).wait_send()
 
+    def corner(self):
+        return (13, 14) if self.other > self.cut_other else (13,)
+
     def by_place(self, middle, end):
         inside = (self.z == 1) | (self.z == 2)
         if middle:
@@ -1069,7 +1071,7 @@
             self.arrived(9, 10)
             for z, k in ((3, 0), (1, 1)):
                 for chip in range(4):
-                    got = b.other_two[three, k, chip].astype(F32)
+                    got = b.other_two[three, k, chip, :, pl.ds(0, self.other)].astype(F32)
                     unit[slot, z, chip, :, other] = (
                         unit[slot, z, chip, :, other].astype(F32) + got
                     ).astype(BF)
@@ -1095,12 +1097,13 @@
             return
         self.arrived(11, 12)
         for chip in range(4):
-            b.plane[three, chip] = (
+            every = pl.ds(0, self.other)
+            b.plane[three, chip, :, every] = (
                 b.unit[slot, 0, chip, :, pl.ds(self.most, self.other)].astype(F32)
-                + b.other_one[slot, 0, chip].astype(F32)
-                + b.other_one[slot, 1, chip].astype(F32)
+                + b.other_one[slot, 0, chip, :, every].astype(F32)
+                + b.other_one[slot, 1, chip, :, every].astype(F32)
             ).astype(BF)
-        self.start(13, 14)
+        self.start(*self.corner())
         self.by_place(lambda: self.sent(10), lambda: self.sent(9))
         self.sent(11, 12)
 
@@ -1117,16 +1120,16 @@
         self.start(7, 8)
         if not self.other:
             return
-        self.arrived(13, 14)
+        self.arrived(*self.corner())
         half = self.cut_other
         for chip, cols, got in (
             (1, pl.ds(0, half), b.other_near),
             (2, pl.ds(half, half), b.other_far),
-        ):
+        )[: len(self.corner())]:
             both = b.plane[three, chip, :, cols].astype(F32) + got[three].astype(F32)
             b.plane[three, chip, :, cols] = both.astype(BF)
         self.start(15, 16)
-        self.sent(13, 14)
+        self.sent(*self.corner())
 
     def stage5(self, by_rows):
         b, slot, three, two = self.bufs, self.slot, self.three, self.two
@@ -1140,10 +1143,11 @@
         if self.other:
             self.arrived(15, 16)
             other = pl.ds(self.most, self.other)
+            every = pl.ds(0, self.other)
             total = (
-                b.plane[three, 0].astype(F32)
-                + b.other_y[three].astype(F32)
-                + b.other_x[three].astype(F32)
+                b.plane[three, 0, :, every].astype(F32)
+                + b.other_y[three, :, every].astype(F32)
+                + b.other_x[three, :, every].astype(F32)
             )
             b.total[two, :, other] = total
             b.squares[0:1, other] += jnp.sum(total * total, 0, keepdims=True)
@@ -1162,7 +1166,6 @@
 
 
 POINTS = 4
-ENTRY = (0, 1, 3)
 STAGE_ORDER = (1, 0, 2, 3, 4, 6, 5)
 
 
@@ -1204,6 +1207,7 @@
         load(r.keys_in.at[1], r.unit.at[SEND, :, :, :, pl.ds(0, KEYS)], r.loads.at[joined_ + 3]),
     ]
     start(TOP - 1, *range(joined_))
+    pixels = load(r.images_in, r.images, r.loads.at[joined_ + 4])
     if cube:
         cube_barrier(plan)
         r.squares[...] = jnp.zeros_like(r.squares)
@@ -1226,43 +1230,37 @@
 
     def point(it, at):
         if not cube:
-            for kind in range(3):
-                if ENTRY[kind] == at:
-                    unit = 3 * it - 2 + kind
-                    copies = [
-                        pltpu.make_async_copy(
-                            r.unit.at[(unit % 4, SEND)[i]],
-                            r.full.at[unit, i],
-                            r.loads.at[joined_ + 1 + i],
-                        )
-                        for i in range(2)
-                    ]
-                    start_all(copies)
-                    wait_all(copies)
+            unit = 4 * it - 3 + at
+            copies = [
+                pltpu.make_async_copy(
+                    r.unit.at[(unit % 4, SEND)[i]], r.full.at[unit, i], r.loads.at[joined_ + 1 + i]
+                )
+                for i in range(2)
+            ]
+            start_all(copies)
+            wait_all(copies)
             return
         for stage in STAGE_ORDER:
-            for kind in range(3):
-                past, phase = divmod(ENTRY[kind] + stage, POINTS)
-                if phase != at:
-                    continue
-                unit = 3 * (it - past) - 2 + kind
-                if past:
-                    pl.when(it > past)(functools.partial(run, unit, stage, kind == 0))
-                else:
-                    run(unit, stage, kind == 0)
-                if past and kind == 2:
-                    pl.when(it == past)(functools.partial(run, unit, stage, False, KEYS))
+            kind = (at - stage) % POINTS
+            past = (kind + stage) // POINTS
+            unit = 4 * (it - past) - 3 + kind
+            go = functools.partial(run, unit, stage, kind == SHRINK, WIDTHS[kind])
+            if past:
+                pl.when(it > past)(go)
+            else:
+                go()
+            if past and kind == TRIPLE:
+                pl.when(it == past)(functools.partial(run, unit, stage, False, KEYS))
 
     def drain():
-        at = 0
-        while at <= 5:
+        for at in range(6):
             for stage in STAGE_ORDER:
-                for past, kind in ((1, 0), (1, 1), (1, 2), (2, 0), (2, 1), (2, 2)):
-                    if POINTS * past + at - ENTRY[kind] == stage:
-                        run(jnp.int32(UNITS - 3 * past + kind), stage, kind == 0)
-                if at == stage:
+                unit = UNITS + at - stage
+                if UNITS - 2 * POINTS <= unit < UNITS:
+                    kind = (unit - 1) % POINTS
+                    run(jnp.int32(unit), stage, kind == SHRINK, WIDTHS[kind])
+                if unit == UNITS:
                     run(jnp.int32(UNITS), stage, False, TAIL)
-            at += 1
 
     def sent(unit, width=WIDTH):
         if cube:
@@ -1287,13 +1285,13 @@
     def _(it):
         layer = TOP - it
         below = it < TOP
-        unit_s = 3 * it - 2
+        unit_s = 4 * it - 3
         base = S + 2 + 4 * layer
         r.gr[...] = r.g[...].astype(BF)
         wait(layer, z_)
         slot = unit_s % 4
         pl.when(it == 1)(lambda: sent(unit_s, KEYS))
-        pl.when(it > 1)(lambda: sent(unit_s))
+        pl.when(it > 1)(lambda: sent(unit_s, WIDTHS[TRIPLE]))
 
         @pl.loop(0, 8)
         def _(j):
@@ -1336,10 +1334,13 @@
         pl.when(below)(lambda: start(layer - 1, h1_))
 
         r.gr[...] = r.g1[...].astype(BF)
-        slot_t = (unit_s + 2) % 4
+        slot_t = (unit_s + TRIPLE) % 4
         wait(layer, o_)
         sent(unit_s + 2)
-        store_cols(plan, r.unit, slot_t, 3, D, dot(r.vm_o[...], r.gr[...], TN))
+        for part in range(2):
+            half = D // 2
+            value = dot(r.vm_o[...], r.gr[:, part * half : part * half + half], TN)
+            store_cols(plan, r.unit, (unit_s + OUTPUT) % 4, part, half, value, half)
         wait(layer, joined_)
         r.do[...] = dot(r.gr[...], weight(r.expand_w, 3 * D, D), NT).astype(BF)
         wait(layer, t_, p_, a_, h_)
@@ -1369,19 +1370,20 @@
         pl.loop(0, half)(heads)
         point(it, 2)
         if cube:
-            pl.when(it == 1)(top_rows.stage3)
+            pl.when(it == 1)(top_rows.finish)
         pl.loop(half, 2 * half)(heads)
         pl.when(below)(lambda: start(layer - 1, o_, t_, p_))
         r.g[...] = jnp.zeros_like(r.g)
 
-        @pl.loop(0, 3)
+        sent(unit_s + TRIPLE, WIDTHS[OUTPUT])
+
+        @pl.loop(0, 6)
         def _(j):
-            cols = pl.ds(pl.multiple_of(j * D, 128), D)
-            store_cols(plan, r.unit, slot_t, j, D, dot(r.vm_a[...], r.dt[:, cols], TN))
+            cols = pl.ds(pl.multiple_of(j * (D // 2), 128), D // 2)
+            value = dot(r.vm_a[...], r.dt[:, cols], TN)
+            store_cols(plan, r.unit, slot_t, j, D // 2, value, WIDTHS[TRIPLE])
 
         point(it, 3)
-        if cube:
-            pl.when(it == 1)(top_rows.finish)
 
         @pl.loop(0, 3)
         def _(j):
@@ -1394,8 +1396,9 @@
         r.vectors[pl.ds(base + 1, 1)] = d_shift
         pl.when(below)(lambda: start(layer - 1, a_, h_, expand_))
 
+    pixels.wait()
     slot = UNITS % 4
-    sent(jnp.int32(UNITS))
+    sent(jnp.int32(UNITS), WIDTHS[TRIPLE])
     for part in range(2):
         half = D // 2
         value = jnp.zeros((D, half), F32)
@@ -1434,7 +1437,6 @@
     gather.stage0()
     gather.stage1()
     gather.stage2()
-    gather.stage3()
     run(jnp.int32(UNITS), 6, False, TAIL)
     Reduce(plan, r, jnp.int32(UNITS), TAIL).copy(0).wait_send()
     gather.finish()
@@ -1445,7 +1447,6 @@
     shapes = saved_shapes(rows)
     inputs = given_in(
         VMEM_SPEC,
-        images=images,
         params=params,
         tail_in=done.tail,
         rows_block=done.rows_block,
@@ -1454,6 +1455,7 @@
     inputs.update(
         given_in(
             ANY_SPEC,
+            images_in=images,
             g_in=done.g,
             keys_in=done.keys_out,
             joined_whole=done.joined_whole,
@@ -1464,7 +1466,10 @@
     inputs.update({"keep_" + name: (getattr(done, "keep_" + name), ANY_SPEC) for name in SAVED})
     if plan.cube:
         outputs = dict(
-            owned=((UNITS - 1, 2, HALF, WIDTH), F32, ANY_SPEC),
+            shrink_grad=((TOP, 2, HALF, WIDTH), F32, ANY_SPEC),
+            expand_grad=((TOP, 2, HALF, WIDTH), F32, ANY_SPEC),
+            output_grad=((TOP, 2, HALF, WIDTHS[OUTPUT]), F32, ANY_SPEC),
+            triple_grad=((TOP, 2, HALF, WIDTHS[TRIPLE]), F32, ANY_SPEC),
             keys=((2, HALF, KEYS), F32, ANY_SPEC),
             patch=((2, HALF, D // 2), F32, ANY_SPEC),
             vector_rows=(CHIPS + (2, BLOCK + 16, 128), BF, ANY_SPEC),
@@ -1485,10 +1490,11 @@
             do=(rows, D),
             dt=(rows, 3 * D),
             unit=(SEND + 1, 4, 4, BLOCK, WIDTH),
+            images=images.shape,
         )
     )
     scratch.update(vmem(F32, g=(rows, D), g1=(rows, D), vectors=(VEC_ROWS, D)))
-    scratch.update(dma(loads=(16,)))
+    scratch.update(dma(loads=(17,)))
     extra = {}
     if plan.cube:
         other = other_part(WIDTH)
@@ -1518,7 +1524,7 @@
             vmem(F32, total=(2, BLOCK, WIDTH), squares=(8, WIDTH))
         )
         scratch.update(
-            dma(send=(4, 20), recv=(4, 18), rows_send=(7,), rows_recv=(7,), tail_send=(7,), tail_recv=(7,))
+            dma(send=(4, 20), recv=(4, 18), rows_send=(10,), rows_recv=(9,), tail_send=(10,), tail_recv=(9,))
         )
         scratch.update(credit=pltpu.SemaphoreType.REGULAR)
         extra = dict(collective_id=2, has_side_effects=True)
@@ -1532,8 +1538,8 @@
 def adam_update(master, moment, square, gradient, step_rate):
     moment_new = BETA_ONE * moment + (1.0 - BETA_ONE) * gradient
     square_new = BETA_TWO * square + (1.0 - BETA_TWO) * gradient * gradient
-    moment_hat = moment_new / (1.0 - BETA_ONE**STEP_INDEX)
-    square_hat = square_new / (1.0 - BETA_TWO**STEP_INDEX)
+    moment_hat = moment_new * (1.0 / (1.0 - BETA_ONE**STEP_INDEX))
+    square_hat = square_new * (1.0 / (1.0 - BETA_TWO**STEP_INDEX))
     master_new = master - step_rate * (
         moment_hat / (jnp.sqrt(square_hat) + ADAM_EPS) + DECAY * master
     )
@@ -1605,7 +1611,7 @@
 
     clip = CLIP / jnp.maximum(norm, CLIP)
     line = lax.broadcasted_iota(jnp.int32, (8, 128), 0)
-    r.scalars[...] = jnp.where(line == 0, norm, loss)
+    r.scalars[...] = jnp.where(line == 0, norm, jnp.where(line == 1, loss, r.total[...]))
 
     def step(group, at, gradient, rate):
         bufs = [buf for _, buf, _ in groups[group]]
@@ -1635,9 +1641,9 @@
 
     @pl.loop(0, TOP)
     def _(layer):
-        unit = 3 * (TOP - 1 - layer)
+        at = TOP - 1 - layer
         for k in range(4):
-            gradient = r.owned[unit, k % 2, :, pl.ds(k // 2 * D, D)]
+            gradient = r.shrink_grad[at, k % 2, :, pl.ds(k // 2 * D, D)]
             step(shrink, (layer, pl.ds(k * HALF, HALF), every), gradient, RATE_MATRIX)
 
     finish(shrink)
@@ -1647,9 +1653,9 @@
 
     @pl.loop(0, TOP)
     def _(layer):
-        unit = 3 * (TOP - 1 - layer) + 1
+        at = TOP - 1 - layer
         for k in range(2):
-            step(expand, (layer, every, pl.ds(k * WIDTH, WIDTH)), r.owned[unit, k], RATE_MATRIX)
+            step(expand, (layer, every, pl.ds(k * WIDTH, WIDTH)), r.expand_grad[at, k], RATE_MATRIX)
 
     finish(expand)
     wait_all(moves(triple, False))
@@ -1662,10 +1668,12 @@
 
     @pl.loop(0, TOP)
     def _(layer):
-        unit = 3 * (TOP - 1 - layer) + 2
-        step(triple, (layer, every, pl.ds(0, WIDTH)), r.owned[unit, 0], RATE_MATRIX)
-        step(triple, (layer, every, pl.ds(WIDTH, D)), r.owned[unit, 1, :, pl.ds(0, D)], RATE_MATRIX)
-        step(output, (layer, every, every), r.owned[unit, 1, :, pl.ds(D, D)], RATE_OUTPUT)
+        at = TOP - 1 - layer
+        for k in range(2):
+            width = WIDTHS[TRIPLE]
+            step(triple, (layer, every, pl.ds(k * width, width)), r.triple_grad[at, k], RATE_MATRIX)
+            width = WIDTHS[OUTPUT]
+            step(output, (layer, every, pl.ds(k * width, width)), r.output_grad[at, k], RATE_OUTPUT)
 
     finish(triple)
     finish(output)
@@ -1685,7 +1693,7 @@
         wait_all(moves(group, True))
 
 
-def update(plan, images, states, got):
+def update(plan, images, states, got, done):
     inputs, outputs, scratch = {}, {}, {}
     for name, state in zip(PARAMS, states):
         for kind, value in zip(KINDS, state):
@@ -1695,11 +1703,15 @@
     inputs.update(
         given_in(
             VMEM_SPEC,
-            owned=got.owned,
+            total=done.total,
+            tails=got.vector_rows.reshape(plan.n, BLOCK + 16, 128),
+            top_rows=got.top_rows.reshape(-1, 128),
+            shrink_grad=got.shrink_grad,
+            expand_grad=got.expand_grad,
+            output_grad=got.output_grad,
+            triple_grad=got.triple_grad,
             patch_grad=got.patch,
-            tails=got.vector_rows.reshape(plan.n, BLOCK + 16, 128),
             keys=got.keys,
-            top_rows=got.top_rows.reshape(-1, 128),
         )
     )
     outputs.update(scalars=((8, 128), F32, VMEM_SPEC), bias_grad=((1, CLASSES), F32, VMEM_SPEC))
@@ -1708,7 +1720,7 @@
     scratch.update(dma(sems=(3 * len(PARAMS),)))
     new = pallas(functools.partial(update_kernel, plan, images), "update", inputs, outputs, scratch)
     states = [[getattr(new, "to_" + kind + name) for kind in KINDS] for name in PARAMS]
-    return new.scalars[0, 0], new.scalars[1, 0], states, new.bias_grad[0]
+    return new.scalars[0, 0], new.scalars[1, 0], new.scalars[2, 0], states, new.bias_grad[0]
 
 
 AXES = ("wide", "grp")
@@ -1716,7 +1728,7 @@
 
 def update_whole(plan, images, states, got, done):
     full = got.full.reshape(UNITS + 1, 2, 16, BLOCK, WIDTH)
-    layers = full[1:UNITS].reshape(TOP, 3, 2, 16, BLOCK, WIDTH)[::-1]
+    layers = full[1:UNITS].reshape(TOP, 4, 2, 16, BLOCK, WIDTH)[::-1]
 
     def scattered(whole):
         axis = whole.ndim - 2
@@ -1727,7 +1739,8 @@
         return joined.reshape(part.shape[:-4] + (D, -1))
 
     shrink = layers[:, 0].reshape(TOP, 2, 16, BLOCK, 2, D).transpose(0, 2, 1, 4, 3, 5)
-    joined = scattered(from_cols(layers[:, 2]))
+    output = scattered(from_cols(layers[:, OUTPUT, ..., : WIDTHS[OUTPUT]]))
+    triple = scattered(from_cols(layers[:, TRIPLE, ..., : WIDTHS[TRIPLE]]))
     rows_all = lax.all_gather(done.rows_block, AXES, axis=0)[:, : PER_IMAGE * images]
     rows_all = rows_all.reshape(plan.n * images, PER_IMAGE * 128)
     ends = [sum(PIECES[: k + 1]) for k in range(len(PIECES))]
@@ -1746,8 +1759,8 @@
     keys = scattered(from_cols(full[0, ..., :KEYS]))
     split = [
         scattered(from_cols(full[UNITS, ..., : D // 2])),
-        with_top(joined[:, :, : 3 * D], jnp.concatenate([top_grad(a, dq), keys], 1)),
-        with_top(joined[:, :, 3 * D :], top_grad(o, g1)),
+        with_top(triple, jnp.concatenate([top_grad(a, dq), keys], 1)),
+        with_top(output, top_grad(o, g1)),
         with_top(scattered(from_cols(layers[:, 1])), top_grad(m, du)),
         with_top(scattered(shrink.reshape(TOP, FF, D)), top_grad(z, g)),
     ]
@@ -1763,7 +1776,7 @@
         adam_update(*state, gradient * clip, rate)
         for state, gradient, rate in zip(states, split + same, rates)
     ]
-    return norm, lax.psum(done.tail[0, 0], AXES), states, bias[0] * clip
+    return norm, lax.psum(done.tail[0, 0], AXES), done.total[0, 0], states, bias[0] * clip
 
 
 def per_device(plan, images, slot_mask, labels, *params):
@@ -1771,11 +1784,11 @@
     patch, triple, output, expand, shrink, vector, head = (state[0] for state in states)
     count = images.shape[0]
     weights = slot_mask.astype(F32)
-    args = dict(images=images, vectors=vector, head=head)
+    args = dict(vectors=vector, head=head)
     scalars = dict(labels=labels, mask=slot_mask)
     if plan.cube:
         shards = dict(patch=patch, triple=triple, output=output, expand=expand, shrink=shrink)
-        done = forward(plan, shards, args, scalars, None, None)
+        done = forward(plan, images, shards, args, scalars, None, None)
     else:
 
         def whole(shard, shape):
@@ -1790,15 +1803,15 @@
             whole(shrink, ROWS_SHAPE),
         ]
         total = jnp.full((8, 128), lax.psum(jnp.sum(weights), AXES), F32)
-        done = forward(plan, None, args, scalars, gathered, total)
+        done = forward(plan, images, None, args, scalars, gathered, total)
     got = backward(plan, images, vector, done)
     if plan.cube:
-        norm, loss, states, bias_grad = update(plan, count, states, got)
+        norm, loss, total, states, bias_grad = update(plan, count, states, got, done)
     else:
-        norm, loss, states, bias_grad = update_whole(plan, count, states, got, done)
+        norm, loss, total, states, bias_grad = update_whole(plan, count, states, got, done)
     return (
         loss,
-        done.total[0, 0],
+        total,
         norm,
         *(value for state in states for value in state),
         bias_grad,

time: 406 us -> 401 us (0.988); the launches traced: 406 us -> 395 us
  Pallas kernels: 401 us -> 391 us
    pallas_call x3, Pallas kernels: 401 us -> 391 us  [pallas(): pl.pallas_call(functools.partial(kernel, names), out_shape=[jax.ShapeDtyp...]
where the time goes in v5:
time: 401 us; the launch traced here: 395 us
  Pallas kernels  391 us (98%)
    pallas_call x3, Pallas kernels, pallas(): pl.pallas_call(functools.partial(kernel, names), out_shape=[jax.ShapeDtyp...  391 us

profile of v5, /device:TPU:0, one launch (start us, length us, event | category | flops | bytes accessed | tf_op | source)
XLA Modules:
  0.0 395.2 jit_solution(3723230547698566440)
XLA Ops:
  0.7 2.0 copy.49.refs_2_.refs_3_
  2.6 207.2 %forward.1 = (bf16[4,2,2,48,768]{4,3,2,1,0:T(8,128)(2,1)}, bf16[3,4,2,2,48,3072]{5,4,3,2,1,0:T(8,128)(2,1)}, bf16[3,4,2,2,48,3072]{5,4,3,2,1,0:T(8,128)(2,1)}, b...) custom-call(f32[213,768]{1,0:T(8,128)} %refs_15_.1, ...), custom_call_target="tpu_custom_call" | custom-call | tf_op jit(solution)/shard_map/forward/pallas_call | solution.py:775
  209.9 166.2 %backward.1 = (f32[2,2,24,1536]{3,2,1,0:T(8,128)}, f32[2,2,24,1536]{3,2,1,0:T(8,128)}, f32[2,2,24,384]{3,2,1,0:T(8,128)}, f32[2,2,24,1152]{3,2,1,0:T(8,128)}, f3...) custom-call(f32[213,768]{1,0:T(8,128)} %refs_15_.1, ...), custom_call_target="tpu_custom_call" | custom-call | tf_op jit(solution)/shard_map/backward/pallas_call | solution.py:775
  376.1 17.3 %update.1 = (f32[24,768]{1,0:T(8,128)}, f32[24,768]{1,0:T(8,128)}, f32[24,768]{1,0:T(8,128)}, f32[3,24,2304]{2,1,0:T(8,128)}, f32[3,24,2304]{2,1,0:T(8,128)}, /*...) custom-call(f32[24,768]{1,0:T(8,128)} %refs_0_.5, ...), custom_call_target="tpu_custom_call" | custom-call | tf_op jit(solution)/shard_map/update/pallas_call | solution.py:775
  393.4 1.3 fusion

commit v6 on v5

--- a/solution.py
+++ b/solution.py
@@ -109,7 +109,7 @@
 
 
 def other_part(width):
-    return width // 6 // 128 * 128
+    return width * 2 // 9 // 128 * 128
 
 
 def cut_of(columns):
@@ -597,9 +597,9 @@
         first[2].stage2()
         first[1].stage3()
         first[0].stage4()
-    r.table[...] = r.head[:D].astype(BF)
     ready(patch, 0).wait()
     pixels.wait()
+    classifier = load(r.head_in, r.head, r.loads.at[5])
     for image in range(images):
         at = image * PAD
         r.h[at : at + 1] = r.vectors[0:1] + r.vectors[S : S + 1]
@@ -654,13 +654,13 @@
             r.o[rows, lanes[0]] = jnp.where(low_lane, outs[0], outs[1]).astype(BF)
 
         half = images * (HEADS // 2) // 2
-        pl.loop(0, half)(heads)
+        pl.loop(0, half, unroll=2)(heads)
         if cube:
             unit(shrink, layer + 1).stage0()
             unit(expand, layer + 1).stage1()
             unit(joined, layer + 1).stage2()
 
-        pl.loop(half, 2 * half)(heads)
+        pl.loop(half, 2 * half, unroll=2)(heads)
         start_all(saves(layer, o_, p_))
         r.h1[...] = r.h[...] + dot(r.o[...], weight(r.joined_w, 3 * D, D))
         start_all(saves(layer, h1_))
@@ -750,6 +750,8 @@
         r.top_f[:, cols] = slope
     if cube:
         unit(shrink, TOP).stage4()
+    classifier.wait()
+    r.table[...] = r.head[:D].astype(BF)
     r.rows_f[...] = jnp.zeros_like(r.rows_f)
     pack_rows(r, 2, r.top_b[:, Z_])
     pack_rows(r, 4, r.top_b[:, M_])
@@ -796,7 +798,7 @@
     return {name: pltpu.SemaphoreType.DMA(count) for name, count in counts.items()}
 
 
-def forward(plan, images, shards, args, scalars, gathered, count):
+def forward(plan, images, head, shards, args, scalars, gathered, count):
     rows = images.shape[0] * PAD
     shapes = saved_shapes(rows)
     whole = dict(
@@ -806,7 +808,7 @@
         shrink_whole=(LAYERS,) + ROWS_SHAPE,
     )
     inputs = given_in(VMEM_SPEC, **args)
-    inputs.update(given_in(ANY_SPEC, images_in=images))
+    inputs.update(given_in(ANY_SPEC, images_in=images, head_in=head))
     inputs.update(given_in(pl.BlockSpec(memory_space=pltpu.SMEM), **scalars))
     outputs = {}
     if plan.cube:
@@ -846,11 +848,12 @@
             first=(HEAD_ROWS, D),
             class_row=(HEAD_ROWS, D),
             d_logits=(HEAD_ROWS, CLASS_PAD),
+            head=head.shape,
             top_f=(HEAD_ROWS, G_.stop),
             rows_f=(rows_block(rows // PAD), 128),
         )
     )
-    scratch.update(dma(saves=(9,), loads=(5,)))
+    scratch.update(dma(saves=(9,), loads=(6,)))
     extra = {}
     if plan.cube:
         scratch.update(
@@ -934,7 +937,7 @@
         self.plan, self.bufs, self.unit, self.width = plan, bufs, unit, width
         self.z, self.x, self.y, self.c = plan.where()
         self.to = over_links(plan)
-        self.other = other_part(width) if width > KEYS else 0
+        self.other = other_part(width)
         self.most = width - self.other
         self.cut, self.cut_other = cut_of(self.most), max(cut_of(self.other), 128)
         self.slot, self.three, self.two = unit % 4, unit % 3, unit % 2
@@ -1206,8 +1209,7 @@
         load(r.keys_in.at[0], r.unit.at[0, :, :, :, pl.ds(0, KEYS)], r.loads.at[joined_ + 2]),
         load(r.keys_in.at[1], r.unit.at[SEND, :, :, :, pl.ds(0, KEYS)], r.loads.at[joined_ + 3]),
     ]
-    start(TOP - 1, *range(joined_))
-    pixels = load(r.images_in, r.images, r.loads.at[joined_ + 4])
+    start(TOP - 1, z_)
     if cube:
         cube_barrier(plan)
         r.squares[...] = jnp.zeros_like(r.squares)
@@ -1270,6 +1272,8 @@
     scale = HEAD_DIM**-0.5
 
     wait_all(loaded)
+    start(TOP - 1, shrink_, slope_, expand_, m_, h1_, o_, t_, p_, a_, h_)
+    pixels = load(r.images_in, r.images, r.loads.at[joined_ + 4])
     if cube:
         run(jnp.int32(0), 0, False, KEYS)
         top_rows.stage0()
@@ -1367,11 +1371,11 @@
             r.dt[rows, lanes[2]] = jnp.where(low_lane, dvs[0], dvs[1]).astype(BF)
 
         half = images * (HEADS // 2) // 2
-        pl.loop(0, half)(heads)
+        pl.loop(0, half, unroll=2)(heads)
         point(it, 2)
         if cube:
             pl.when(it == 1)(top_rows.finish)
-        pl.loop(half, 2 * half)(heads)
+        pl.loop(half, 2 * half, unroll=2)(heads)
         pl.when(below)(lambda: start(layer - 1, o_, t_, p_))
         r.g[...] = jnp.zeros_like(r.g)
 
@@ -1588,8 +1592,7 @@
         ]
 
     order = (head, shrink, expand, triple, output, patch, vector)
-    for group in order:
-        start_all(moves(group, False))
+    start_all(moves(head, False))
 
     tile = jnp.sum(r.tails[:, BLOCK:, :].astype(F32), 0)
     square_sum = tile[0:1, 0:1] + tile[1:2, 0:1] + tile[2:3, 0:1]
@@ -1610,6 +1613,8 @@
         return dot(own_columns(left, me * rows, rows), right, TN)[:rows]
 
     clip = CLIP / jnp.maximum(norm, CLIP)
+    for group in order[1:]:
+        start_all(moves(group, False))
     line = lax.broadcasted_iota(jnp.int32, (8, 128), 0)
     r.scalars[...] = jnp.where(line == 0, norm, jnp.where(line == 1, loss, r.total[...]))
 
@@ -1784,11 +1789,11 @@
     patch, triple, output, expand, shrink, vector, head = (state[0] for state in states)
     count = images.shape[0]
     weights = slot_mask.astype(F32)
-    args = dict(vectors=vector, head=head)
+    args = dict(vectors=vector)
     scalars = dict(labels=labels, mask=slot_mask)
     if plan.cube:
         shards = dict(patch=patch, triple=triple, output=output, expand=expand, shrink=shrink)
-        done = forward(plan, images, shards, args, scalars, None, None)
+        done = forward(plan, images, head, shards, args, scalars, None, None)
     else:
 
         def whole(shard, shape):
@@ -1803,7 +1808,7 @@
             whole(shrink, ROWS_SHAPE),
         ]
         total = jnp.full((8, 128), lax.psum(jnp.sum(weights), AXES), F32)
-        done = forward(plan, images, None, args, scalars, gathered, total)
+        done = forward(plan, images, head, None, args, scalars, gathered, total)
     got = backward(plan, images, vector, done)
     if plan.cube:
         norm, loss, total, states, bias_grad = update(plan, count, states, got, done)

time: 401 us -> 396 us (0.988)
  Pallas kernels: 391 us -> 386 us
    pallas_call x3, Pallas kernels: 391 us -> 386 us  [pallas(): pl.pallas_call(functools.partial(kernel, names), out_shape=[jax.ShapeDtyp...]
where the time goes in v6:
time: 396 us; the launch traced here: 390 us
  Pallas kernels  386 us (97%)
    pallas_call x3, Pallas kernels, pallas(): pl.pallas_call(functools.partial(kernel, names), out_shape=[jax.ShapeDtyp...  386 us

profile of v6, /device:TPU:0, one launch (start us, length us, event | category | flops | bytes accessed | tf_op | source)
XLA Modules:
  0.0 390.2 jit_solution(86298427500620661)
XLA Ops:
  0.7 2.0 copy.49.refs_1_.refs_3_
  2.6 203.0 %forward.1 = (bf16[4,2,2,48,768]{4,3,2,1,0:T(8,128)(2,1)}, bf16[3,4,2,2,48,3072]{5,4,3,2,1,0:T(8,128)(2,1)}, bf16[3,4,2,2,48,3072]{5,4,3,2,1,0:T(8,128)(2,1)}, b...) custom-call(f32[213,768]{1,0:T(8,128)} %refs_15_.1, ...), custom_call_target="tpu_custom_call" | custom-call | tf_op jit(solution)/shard_map/forward/pallas_call | solution.py:777
  205.6 165.5 %backward.1 = (f32[2,2,24,1536]{3,2,1,0:T(8,128)}, f32[2,2,24,1536]{3,2,1,0:T(8,128)}, f32[2,2,24,384]{3,2,1,0:T(8,128)}, f32[2,2,24,1152]{3,2,1,0:T(8,128)}, f3...) custom-call(f32[213,768]{1,0:T(8,128)} %refs_15_.1, ...), custom_call_target="tpu_custom_call" | custom-call | tf_op jit(solution)/shard_map/backward/pallas_call | solution.py:777
  371.1 17.3 %update.1 = (f32[24,768]{1,0:T(8,128)}, f32[24,768]{1,0:T(8,128)}, f32[24,768]{1,0:T(8,128)}, f32[3,24,2304]{2,1,0:T(8,128)}, f32[3,24,2304]{2,1,0:T(8,128)}, /*...) custom-call(f32[24,768]{1,0:T(8,128)} %refs_0_.5, ...), custom_call_target="tpu_custom_call" | custom-call | tf_op jit(solution)/shard_map/update/pallas_call | solution.py:777
  388.5 1.3 fusion

commit v7 on v6

--- a/solution.py
+++ b/solution.py
@@ -1297,7 +1297,7 @@
         pl.when(it == 1)(lambda: sent(unit_s, KEYS))
         pl.when(it > 1)(lambda: sent(unit_s, WIDTHS[TRIPLE]))
 
-        @pl.loop(0, 8)
+        @pl.loop(0, 8, unroll=2)
         def _(j):
             cols = pl.ds(pl.multiple_of(j * (D // 2), 128), D // 2)
             store_rows(plan, r.unit, slot, j, dot(r.vm_z[:, cols], r.gr[...], TN))
@@ -1324,7 +1324,7 @@
         if cube:
             pl.when(it == 1)(top_rows.stage2)
 
-        @pl.loop(0, 4)
+        @pl.loop(0, 4, unroll=2)
         def _(j):
             cols = pl.ds(pl.multiple_of(j * D, 128), D)
             r.g1[...] += dot(r.vm_slope[:, cols], weight(r.expand_w, j * D, D), NT)
@@ -1381,7 +1381,7 @@
 
         sent(unit_s + TRIPLE, WIDTHS[OUTPUT])
 
-        @pl.loop(0, 6)
+        @pl.loop(0, 6, unroll=2)
         def _(j):
             cols = pl.ds(pl.multiple_of(j * (D // 2), 128), D // 2)
             value = dot(r.vm_a[...], r.dt[:, cols], TN)

time: 396 us -> 395 us (level)
  no operation moved by 1% of the time
where the time goes in v7:
time: 395 us; the launch traced here: 389 us
  Pallas kernels  384 us (97%)
    pallas_call x3, Pallas kernels, pallas(): pl.pallas_call(functools.partial(kernel, names), out_shape=[jax.ShapeDtyp...  384 us

profile of v7, /device:TPU:0, one launch (start us, length us, event | category | flops | bytes accessed | tf_op | source)
XLA Modules:
  0.0 388.9 jit_solution(3312583150770298428)
XLA Ops:
  0.7 2.0 copy.49.refs_1_.refs_3_
  2.6 203.0 %forward.1 = (bf16[4,2,2,48,768]{4,3,2,1,0:T(8,128)(2,1)}, bf16[3,4,2,2,48,3072]{5,4,3,2,1,0:T(8,128)(2,1)}, bf16[3,4,2,2,48,3072]{5,4,3,2,1,0:T(8,128)(2,1)}, b...) custom-call(f32[213,768]{1,0:T(8,128)} %refs_15_.1, ...), custom_call_target="tpu_custom_call" | custom-call | tf_op jit(solution)/shard_map/forward/pallas_call | solution.py:777
  205.6 164.1 %backward.1 = (f32[2,2,24,1536]{3,2,1,0:T(8,128)}, f32[2,2,24,1536]{3,2,1,0:T(8,128)}, f32[2,2,24,384]{3,2,1,0:T(8,128)}, f32[2,2,24,1152]{3,2,1,0:T(8,128)}, f3...) custom-call(f32[213,768]{1,0:T(8,128)} %refs_15_.1, ...), custom_call_target="tpu_custom_call" | custom-call | tf_op jit(solution)/shard_map/backward/pallas_call | solution.py:777
  369.8 17.3 %update.1 = (f32[24,768]{1,0:T(8,128)}, f32[24,768]{1,0:T(8,128)}, f32[24,768]{1,0:T(8,128)}, f32[3,24,2304]{2,1,0:T(8,128)}, f32[3,24,2304]{2,1,0:T(8,128)}, /*...) custom-call(f32[24,768]{1,0:T(8,128)} %refs_0_.5, ...), custom_call_target="tpu_custom_call" | custom-call | tf_op jit(solution)/shard_map/update/pallas_call | solution.py:777
  387.1 1.3 fusion
